TPU v7x, 512 devices: a whole 4x4x16 slice. The times are simulated.
512 devices in a mesh: space: 32 (over z_lo, y, core), chan: 4 (over z_hi), batch: 4 (over x).
Axes of the slice: x: 4, y: 4, z: 16 (z_hi: 4, z_lo: 4; z = z_hi * 4 + z_lo), core: 2. Of those that a mesh axis runs over, the one named last changes fastest.
Arguments:
- crops: bfloat16 [4, 32, 64, 48, 128], P('batch', 'chan', 'space'), may hold values from -6 to 6
- cotangent: bfloat16 [4, 32, 64, 48, 128], P('batch', 'chan', 'space'), may hold values from -6 to 6
- weights: bfloat16 [32, 27, 32], replicated, may hold values from -0.21875 to 0.21875
Outputs:
- activated: bfloat16 [4, 32, 64, 48, 128], P('batch', 'chan', 'space')
- input_grad: bfloat16 [4, 32, 64, 48, 128], P('batch', 'chan', 'space')
- weight_grad: float32 [32, 27, 32], replicated
All inputs are finite; a program needn't handle non-finite values.
Results may differ from a plain program's by a relative error of at most 0.013.
Values may be sent and summed in bfloat16 or wider, within the bound.
No kernel may reach another device: no remote copies, remote signals or barrier semaphores. Data moves between devices by JAX's collectives and lax.ppermute only.
A program may use at most 64 MiB of HBM per device.

v0:
```python
import jax
import jax.numpy as jnp
from jax import lax
from jax.sharding import PartitionSpec as P


def extended(array, sides, width):
    for axis, dim in sides:
        count, length = (lax.axis_size(axis), array.shape[dim])
        up = [(i, (i + 1) % count) for i in range(count - 1)]
        down = [(j, i) for i, j in up]
        last = lax.slice_in_dim(array, length - width, length, axis=dim)
        initial = lax.slice_in_dim(array, 0, width, axis=dim)
        before = lax.ppermute(last, axis, up)
        after = lax.ppermute(initial, axis, down)
        array = jnp.concatenate([before, array, after], axis=dim)
    return array


def pad_sides(field):
    return jnp.pad(field, ((0, 0), (0, 0), (1, 1), (1, 1)))


def rounded(value):
    return lax.optimization_barrier(value.astype(jnp.bfloat16)).astype(jnp.float32)


def columns_of(padded, plane):
    rows = padded.shape[2] - 2
    depth = padded.shape[3] - 2
    slab = lax.dynamic_slice_in_dim(padded, plane, 3, 1)
    taps = [
        slab[:, tap_a, tap_b : tap_b + rows, tap_c : tap_c + depth]
        for tap_a in range(3)
        for tap_b in range(3)
        for tap_c in range(3)
    ]
    return jnp.stack(taps, 0).reshape(27 * padded.shape[0], rows * depth)


def conv_planes(padded, kernel):
    planes = padded.shape[1] - 2
    rows = padded.shape[2] - 2
    depth = padded.shape[3] - 2
    outs = kernel.shape[0]
    flat_kernel = kernel.reshape(outs, 27 * kernel.shape[2])

    def conv_one_plane(plane, total):
        result = jnp.dot(flat_kernel, columns_of(padded, plane), preferred_element_type=jnp.float32)
        return lax.dynamic_update_slice_in_dim(
            total, result.reshape(outs, 1, rows, depth), plane, 1
        )

    return lax.fori_loop(
        0, planes, conv_one_plane, jnp.zeros((outs, planes, rows, depth), jnp.float32)
    )


def grad_planes(padded, upstream):
    outs = upstream.shape[0]
    planes = upstream.shape[1]
    ins = padded.shape[0]

    def grad_one_plane(plane, total):
        above = lax.dynamic_index_in_dim(upstream, plane, 1, keepdims=False).reshape(outs, -1)
        return total + lax.dot_general(
            above,
            columns_of(padded, plane),
            (((1,), (1,)), ((), ())),
            preferred_element_type=jnp.float32,
        )

    total = lax.fori_loop(0, planes, grad_one_plane, jnp.zeros((outs, 27 * ins), jnp.float32))
    return total.reshape(outs, 27, ins)


def grouped_sum(padded_all, kernel, groups, share, shape):
    total = jnp.zeros(shape, jnp.float32)
    for group in range(groups):
        low = group * share
        total = total + rounded(
            conv_planes(padded_all[low : low + share], kernel[:, :, low : low + share])
        )
    return total


def body(crops, cotangent, weights):
    groups = lax.axis_size("chan")
    member = lax.axis_index("chan")
    share = weights.shape[0] // groups
    width = weights.shape[0]
    local = crops[0]
    own_shape = (share,) + local.shape[1:]
    rimmed = extended(local, (("space", 1),), 1)
    flipped = jnp.transpose(weights[:, ::-1, :], (2, 1, 0))
    own_padded = pad_sides(rimmed)
    own_inputs = lax.dynamic_slice_in_dim(weights, member * share, share, 2)
    pre = lax.psum_scatter(
        conv_planes(own_padded, own_inputs).astype(jnp.bfloat16),
        "chan",
        scatter_dimension=0,
        tiled=True,
    ).astype(jnp.float32)
    below = jnp.minimum(pre, 0.0)
    activated = jnp.where(pre > 0, pre, jnp.expm1(below)).astype(jnp.bfloat16)
    wide_upper = cotangent[0].astype(jnp.float32)
    upstream = jnp.where(pre > 0, wide_upper, wide_upper * jnp.exp(below)).astype(jnp.bfloat16)
    upstream_rim = extended(upstream, (("space", 1),), 1)
    full = jnp.zeros((width, 27, width), jnp.float32)
    own_kernel = lax.dynamic_slice_in_dim(flipped, member * share, share, 0)
    every_output = lax.all_gather(upstream_rim, "chan", axis=0, tiled=True)
    back = grouped_sum(pad_sides(every_output), own_kernel, groups, share, own_shape)
    part = grad_planes(own_padded, every_output[:, 1:-1])
    full = lax.dynamic_update_slice_in_dim(full, part, member * share, 2)
    total = lax.psum(full, ("space", "chan", "batch"))
    cells = (
        lax.axis_size("batch")
        * crops.shape[0]
        * lax.axis_size("space")
        * local.shape[1]
        * local.shape[2]
        * local.shape[3]
    )
    weight_grad = total / jnp.sqrt(jnp.float32(cells))
    return (activated[None], back.astype(jnp.bfloat16)[None], weight_grad)


def solution(mesh):
    return jax.shard_map(
        body,
        mesh=mesh,
        in_specs=(
            P("batch", "chan", "space", None, None),
            P("batch", "chan", "space", None, None),
            P(),
        ),
        out_specs=(
            P("batch", "chan", "space", None, None),
            P("batch", "chan", "space", None, None),
            P(),
        ),
        check_vma=False,
    )
```

profile of v0, /device:TPU:1, one launch (start us, length us, event | category | flops | bytes accessed | tf_op | source)
XLA Modules:
  0.0 651.1 jit_solution(17660408661148631133)
XLA Ops:
  8.2 4.6 collective-permute-start
  12.8 5.5 collective-permute-start.1
  18.3 1.1 constant_dynamic-slice_fusion.1
  19.6 1.6 select_maximum_fusion
  21.2 7.8 %while.79 = (s32[]{:T(128)}, bf16[32,2,48,128]{3,2,1,0:T(8,128)(2,1)S(1)}, bf16[8,4,50,130]{3,2,1,0:T(8,128)(2,1)S(1)}, bf16[32,216]{1,0:T(8,128)(2,1)S(1)}, s32[]{:T(128)}, /*index=5*/s32[]{:T(128)}, s32[]{}, s32[]{}) while((s32[]{:T(128)}, bf16[32,2,48,128]{3,2,1,0:T(8,128)(2,1)S(1)}, bf16[8,4,50,130]{3,2,1,0:T(8,128)(2,1)S(1)}, ...), condition=%wide.region_1.2_spmd, body=%wide.region_0.1_spmd.sunk | while | flops 84934664 | bytes 9942901 | solution.py:54
  30.0 56.2 %reduce-scatter.2.cloned.1.call-done = bf16[8,2,48,128]{3,2,1,0:T(8,128)(2,1)} async-done(((bf16[32,2,48,128]{3,2,1,0:T(8,128)(2,1)}), bf16[8,2,48,128]{3,2,1,0:T(8,128)(2,1)}) %reduce-scatter.2.cloned.1.call-update) | async-done | bytes 196624 | tf_op jit(solution)/shard_map/reduce_scatter | solution.py:98
  86.2 1.8 fusion.209
  88.0 3.8 collective-permute-start.2
  91.8 1.9 collective-permute-start.3
  93.7 4.0 collective-permute-done.3
  99.3 70.7 %all-gather.2.cloned.1.call-done = bf16[32,4,48,128]{3,2,1,0:T(8,128)(2,1)} async-done(((bf16[8,4,48,128]{3,2,1,0:T(8,128)(2,1)}), bf16[32,4,48,128]{3,2,1,0:T(8,128)(2,1)}) %all-gather.2.cloned.1.call-update) | async-done | bytes 1572880 | tf_op jit(solution)/shard_map/all_gather | solution.py:111
  170.0 1.2 slice.1221
  171.2 8.3 %while.84 = (s32[]{:T(128)}, f32[32,216]{1,0:T(8,128)S(1)}, bf16[32,2,48,128]{3,2,1,0:T(8,128)(2,1)S(1)}, bf16[8,4,50,130]{3,2,1,0:T(8,128)(2,1)S(1)}, s32[]{:T(128)}, /*index=5*/s32[]{:T(128)}, s32[]{}, s32[]{}) while((s32[]{:T(128)}, f32[32,216]{1,0:T(8,128)S(1)}, bf16[32,2,48,128]{3,2,1,0:T(8,128)(2,1)S(1)}, ...), condition=%wide.region_12.13_spmd.clone, body=%wide.region_11.12_spmd.clone.sunk | while | flops 84948488 | bytes 9197951 | solution.py:73
  179.9 4.4 dynamic_update_slice.38
  185.0 4.7 pad_slice_fusion.3
  189.8 33.3 %while.80 = (s32[]{:T(128)}, bf16[8,2,48,128]{3,2,1,0:T(8,128)(2,1)S(1)}, bf16[8,4,50,130]{3,2,1,0:T(8,128)(2,1)}, bf16[8,216]{1,0:T(8,128)(2,1)S(1)}, s32[]{:T(128)}, /*index=5*/s32[]{:T(128)}, s32[]{}, s32[]{}) while((s32[]{:T(128)}, bf16[8,2,48,128]{3,2,1,0:T(8,128)(2,1)S(1)}, bf16[8,4,50,130]{3,2,1,0:T(8,128)(2,1)}, ...), condition=%wide.region_4.5_spmd, body=%wide.region_3.4_spmd.sunk | while | flops 21233668 | bytes 9925393 | solution.py:54
  193.8 1.1 fusion.435
  194.9 1.1 fusion.436
  197.0 1.1 fusion.438
  198.1 1.1 fusion.439
  201.2 1.1 fusion.442
  203.2 1.1 fusion.444
  210.5 1.1 fusion.435
  211.6 1.1 fusion.436
  213.7 1.1 fusion.438
  214.8 1.1 fusion.439
  219.9 1.1 fusion.444
  223.1 7.6 %while.81 = (s32[]{:T(128)}, bf16[8,2,48,128]{3,2,1,0:T(8,128)(2,1)S(1)}, bf16[8,4,50,130]{3,2,1,0:T(8,128)(2,1)S(1)}, bf16[8,216]{1,0:T(8,128)(2,1)S(1)}, s32[]{:T(128)}, /*index=5*/s32[]{:T(128)}, s32[]{}, s32[]{}) while((s32[]{:T(128)}, bf16[8,2,48,128]{3,2,1,0:T(8,128)(2,1)S(1)}, bf16[8,4,50,130]{3,2,1,0:T(8,128)(2,1)S(1)}, ...), condition=%wide.region_6.7_spmd, body=%wide.region_5.6_spmd.sunk | while | flops 21233668 | bytes 8261365 | solution.py:54
  230.8 7.4 %while.82 = (s32[]{:T(128)}, bf16[8,2,48,128]{3,2,1,0:T(8,128)(2,1)S(1)}, bf16[8,4,50,130]{3,2,1,0:T(8,128)(2,1)S(1)}, bf16[8,216]{1,0:T(8,128)(2,1)S(1)}, s32[]{:T(128)}, /*index=5*/s32[]{:T(128)}, s32[]{}, s32[]{}) while((s32[]{:T(128)}, bf16[8,2,48,128]{3,2,1,0:T(8,128)(2,1)S(1)}, bf16[8,4,50,130]{3,2,1,0:T(8,128)(2,1)S(1)}, ...), condition=%wide.region_8.9_spmd, body=%wide.region_7.8_spmd.sunk | while | flops 21233668 | bytes 8261365 | solution.py:54
  238.2 7.4 %while.83 = (s32[]{:T(128)}, bf16[8,2,48,128]{3,2,1,0:T(8,128)(2,1)S(1)}, bf16[8,4,50,130]{3,2,1,0:T(8,128)(2,1)S(1)}, bf16[8,216]{1,0:T(8,128)(2,1)S(1)}, s32[]{:T(128)}, /*index=5*/s32[]{:T(128)}, s32[]{}, s32[]{}) while((s32[]{:T(128)}, bf16[8,2,48,128]{3,2,1,0:T(8,128)(2,1)S(1)}, bf16[8,4,50,130]{3,2,1,0:T(8,128)(2,1)S(1)}, ...), condition=%wide.region_10.11_spmd, body=%wide.region_9.10_spmd.sunk | while | flops 21233668 | bytes 8261365 | solution.py:54
  246.4 396.3 %all-reduce.4.cloned.1.call-done = f32[32,27,32]{2,0,1:T(8,128)} async-done(((f32[32,27,32]{2,0,1:T(8,128)}), f32[32,27,32]{2,0,1:T(8,128)}) %all-reduce.4.cloned.1.call-update) | async-done | bytes 110608 | tf_op jit(solution)/shard_map/psum | solution.py:115
  642.7 1.8 broadcast_multiply_fusion
  (382 shorter events, 64.2 us)
Async XLA Ops:
  7.2 79.0 %reduce-scatter.2.cloned.1.call-start = ((), (), s32[]{:S(2)}) async-start(), calls=%async_computation.1 | async-start | bytes 983040 | tf_op jit(solution)/shard_map/reduce_scatter | solution.py:98
  8.2 11.4 %collective-permute-start = (bf16[8,1,48,128]{3,2,1,0:T(8,128)(2,1)S(1)}, bf16[8,1,48,128]{3,2,1,0:T(8,128)(2,1)S(1)}, u32[]{:S(2)}, u32[]{:S(2)}) collective-permute-start(bf16[8,1,48,128]{3,2,1,0:T(8,128)(2,1)S(1)} %get-tuple-element.614), channel_id=1, source_target_pairs={{0,16},{16,32},{32,48},{48,64},{64,80},{80,96},{96,112},{112,128},... | collective-permute-start | bytes 294920 | tf_op jit(solution)/shard_map/ppermute | solution.py:14
  12.8 6.8 %collective-permute-start.1 = (bf16[8,1,48,128]{3,2,1,0:T(8,128)(2,1)S(1)}, bf16[8,1,48,128]{3,2,1,0:T(8,128)(2,1)S(1)}, u32[]{:S(2)}, u32[]{:S(2)}) collective-permute-start(bf16[8,1,48,128]{3,2,1,0:T(8,128)(2,1)S(1)} %get-tuple-element.615), channel_id=1, source_target_pairs={{16,0},{32,16},{48,32},{64,48},{80,64},{96,80},{112,96},{128,112},... | collective-permute-start | bytes 294920 | tf_op jit(solution)/shard_map/ppermute | solution.py:15
  21.2 65.0 %copy-start.4 = (bf16[1,8,2,48,128]{4,3,2,1,0:T(8,128)(2,1)S(1)}, bf16[1,8,2,48,128]{4,3,2,1,0:T(8,128)(2,1)}, u32[]{:S(2)}) copy-start(bf16[1,8,2,48,128]{4,3,2,1,0:T(8,128)(2,1)} %param.16) | copy-start | bytes 589828
  29.0 0.9 copy-start.3
  29.0 69.8 %copy-start.2 = (bf16[32,27,32]{2,0,1:T(8,128)(2,1)S(1)}, bf16[32,27,32]{2,0,1:T(8,128)(2,1)}, u32[]{:S(2)}) copy-start(bf16[32,27,32]{2,0,1:T(8,128)(2,1)} %param.17) | copy-start | bytes 165892
  29.9 140.1 %all-gather.2.cloned.1.call-start = ((), (), s32[]{:S(2)}) async-start(), calls=%async_computation.2 | async-start | bytes 1966080 | tf_op jit(solution)/shard_map/all_gather | solution.py:111
  88.0 5.7 collective-permute-start.2
  91.8 5.9 collective-permute-start.3
  98.6 544.2 %all-reduce.4.cloned.1.call-start = ((), (), s32[]{:S(2)}) async-start(), calls=%async_computation.3 | async-start | bytes 884736 | tf_op jit(solution)/shard_map/psum | solution.py:115
  184.3 0.8 copy-start.1
  189.8 14.5 %copy-start = (bf16[8,4,50,130]{3,2,1,0:T(8,128)(2,1)S(1)}, bf16[8,4,50,130]{3,2,1,0:T(8,128)(2,1)}, u32[]{:S(2)}) copy-start(bf16[8,4,50,130]{3,2,1,0:T(8,128)(2,1)} %get-tuple-element.880) | copy-start | bytes 1248004 | tf_op jit(solution)/shard_map/while
  206.4 14.5 %copy-start = (bf16[8,4,50,130]{3,2,1,0:T(8,128)(2,1)S(1)}, bf16[8,4,50,130]{3,2,1,0:T(8,128)(2,1)}, u32[]{:S(2)}) copy-start(bf16[8,4,50,130]{3,2,1,0:T(8,128)(2,1)} %get-tuple-element.880) | copy-start | bytes 1248004 | tf_op jit(solution)/shard_map/while
Sparse Core Ops, SparseCore 0:
  30.1 56.0 reduce-scatter.1
  98.7 71.2 all-gather.1
  185.2 457.5 all-reduce.3
where the time goes:
time: 653 us; the launch traced here: 651 us
  waiting for transfers between devices  527 us (81%)
  local copies, waits for them, and re-layouts  79 us (12%)
  starting transfers between devices  16.1 us (2%)
  between operations  14 us (2%)
  other arithmetic  6.82 us (1%)
  matrix products  6.72 us (1%)
    psum x1, waiting for transfers between devices, body(): total = lax.psum(full, ('space', 'chan', 'batch'))  396 us
    all_gather x1, waiting for transfers between devices, body(): every_output = lax.all_gather(upstream_rim, 'chan', axis=0, tiled=True)  70.7 us
    while x318, local copies, waits for them, and re-layouts  61.6 us
    reduce_scatter x1, waiting for transfers between devices, body(): lax.psum_scatter(conv_planes(own_padded, own_inputs).astype(jnp.bfloat16)...  56.2 us
  transfers between devices with their start and end apart: 7, of which 4 were waited for; matrix products, arithmetic and copies ran while one was open for 10% of the time, Pallas kernels for 0%

commit v1 on v0

v1 whole, which is shorter than its diff:
```python
import functools

import jax
import jax.numpy as jnp
from jax import lax
from jax.experimental import pallas as pl
from jax.experimental.pallas import tpu as pltpu
from jax.sharding import PartitionSpec as P

LANES = 128
F32 = jnp.float32
BF16 = jnp.bfloat16


def iota(shape, dim):
    return lax.broadcasted_iota(jnp.int32, shape, dim)


def one_hot(hit):
    return jnp.where(hit, 1.0, 0.0)


def dot(left, right, **options):
    return jnp.dot(left, right, preferred_element_type=F32, **options)


def shifted(block, step):
    moved = pltpu.roll(block, step % LANES, 1)
    lane = iota(block.shape, 1)
    edge = 0 if step == 1 else LANES - 1
    return jnp.where(lane == edge, 0.0, moved)


def pack_kernel(crops, cotangent, out):
    both = jnp.concatenate([crops[...].reshape(768, LANES), cotangent[...].reshape(768, LANES)], axis=1)
    for part in range(4):
        row = iota((256, 768), 0)
        y = row // 16 + (12 * part - 2)
        source = (row % 8) * 96 + (row // 8 % 2) * 48 + y
        source = jnp.where((y >= 0) & (y < 48), source, -1)
        move = one_hot(source == iota((256, 768), 1)).astype(BF16)
        moved = dot(move, both).astype(BF16).reshape(16, 16, 2 * LANES)
        out[part, 0:16] = moved[:, :, :LANES]
        out[part, 16:30] = moved[1:15, :, LANES:]


def unpack_kernel(back, activated, input_grad):
    rows = [back[:, which].reshape(768, LANES) for which in range(2)]
    both = jnp.concatenate(rows, axis=1)
    row = iota((768, 768), 0)
    source = (row % 48) * 16 + (row // 48 % 2) * 8 + row // 96
    move = one_hot(source == iota((768, 768), 1)).astype(BF16)
    moved = dot(move, both).astype(BF16)
    activated[...] = moved[:, :LANES].reshape(8, 2, 48, LANES)
    input_grad[...] = moved[:, LANES:].reshape(8, 2, 48, LANES)


def main_kernel(before, own, after, by_out, by_in, back, grads, field, forward, backward, upper, sides):
    slabs = (before, own, after)
    for row in range(16):
        for slab in range(3):
            field[slab * 64 : slab * 64 + 64, row * LANES : (row + 1) * LANES] = slabs[slab][:, row].reshape(64, LANES)

    column = iota((32, 192), 1)
    spread = one_hot(column // 16 % 4 * 8 + column % 8 == iota((32, 192), 0)).astype(BF16)
    wide = dot(by_out[...], spread)
    column = iota((8, 192), 1)
    plane = column // 64 * 2 + column // 8 % 2
    for c in range(3):
        for b in range(3):

            def band(group, target):
                total = jnp.zeros((8, 192), F32)
                for a in range(3):
                    low = (9 * a + 3 * b + c) * 32 + group * 8
                    total = jnp.where(plane == target + a - 1, wide[low : low + 8], total)
                return total

            pieces = [band(group, 2 + x) for group in range(4) for x in range(2)]
            pieces += [band(group, 1) for group in range(4)]
            pieces += [band(group, 4) for group in range(4)]
            forward[b, c * 128 : c * 128 + 128] = jnp.concatenate(pieces, axis=0).astype(BF16)

    column = iota((32, 128), 1)
    channel = jnp.where(column < 64, column // 16 * 8 + column % 8, column % 32)
    wide_in = dot(by_in[...], one_hot(channel == iota((32, 128), 0)).astype(BF16))
    column = iota((8, 128), 1)
    plane_in = jnp.where(column < 64, 2 + column // 8 % 2, jnp.where(column < 96, 1, 4))
    for c in range(3):
        for b in range(3):
            pieces = []
            for group in range(4):
                for x in range(2):
                    total = jnp.zeros((8, 128), F32)
                    for a in range(3):
                        low = (26 - (9 * a + 3 * b + c)) * 32 + group * 8
                        total = jnp.where(plane_in == 1 + x + a, wide_in[low : low + 8], total)
                    pieces.append(total)
            backward[b, c * 64 : c * 64 + 64] = jnp.concatenate(pieces, axis=0).astype(BF16)

    for pair in range(7):
        low = pair * 2
        total = sum(dot(forward[b], field[:, (low + b) * LANES : (low + b + 2) * LANES]) for b in range(3))
        for side in range(2):
            row = low + side
            cut = total[:, side * LANES : (side + 1) * LANES]
            pre = cut[128:256] + shifted(cut[0:128], 1) + shifted(cut[256:384], -1)
            power = jnp.exp(jnp.minimum(pre, 0.0))
            if 1 <= row <= 12:
                activated = jnp.where(pre[:64] > 0, pre[:64], power[:64] - 1.0).astype(BF16)
                back[:, 0, row - 1] = activated.reshape(4, 16, LANES)
            cot_own = own[:, 16 + row].astype(F32).reshape(64, LANES)
            cot_before = before[:, 16 + row].astype(F32)[:, 8:16].reshape(32, LANES)
            cot_after = after[:, 16 + row].astype(F32)[:, 0:8].reshape(32, LANES)
            cot = jnp.concatenate([cot_own, cot_before, cot_after], axis=0)
            up = jnp.where(pre > 0, cot, cot * power).astype(BF16)
            upper[:, row * LANES : (row + 1) * LANES] = up
            if 1 <= row <= 12:
                here = slice((row - 1) * LANES, row * LANES)
                wide_up = up[:64].astype(F32)
                sides[0:64, here] = shifted(wide_up, -1).astype(BF16)
                sides[64:128, here] = up[:64]
                sides[128:192, here] = shifted(wide_up, 1).astype(BF16)

    for pair in range(6):
        low = pair * 2
        total = sum(dot(backward[b], upper[:, (low + b) * LANES : (low + b + 2) * LANES]) for b in range(3))
        for side in range(2):
            cut = total[:, side * LANES : (side + 1) * LANES]
            grad = cut[64:128] + shifted(cut[0:64], 1) + shifted(cut[128:192], -1)
            back[:, 1, low + side] = grad.astype(BF16).reshape(4, 16, LANES)

    row = iota((192, 256), 0)
    col = iota((192, 256), 1)
    row_plane = row // 64 * 2 + row // 8 % 2
    same = row // 16 % 4 * 8 + row % 8 == col % 32
    row9 = iota((192, 128), 0)
    col9 = iota((192, 128), 1)
    plane9 = row9 // 64 * 2 + row9 // 8 % 2
    same9 = row9 // 16 % 4 * 8 + row9 % 8 == col9 % 32
    eight = jnp.zeros((96, 256), F32)
    ninth = jnp.zeros((32, 128), F32)
    for b in range(3):
        product = lax.dot_general(
            sides[...],
            field[:, (1 + b) * LANES : (13 + b) * LANES],
            (((1,), (1,)), ((), ())),
            preferred_element_type=F32,
        ).reshape(12, 2, 8, 192)
        for x in range(2):
            part = product[:, x].reshape(96, 192)
            pick = same & (col // 32 % 3 == b) & (row_plane == 1 + x + col // 96)
            eight = eight + dot(part, one_hot(pick), precision=lax.Precision.HIGHEST)
            if b == 2:
                for c in range(3):
                    pick = same9 & (col9 // 32 == c) & (plane9 == 3 + x)
                    ninth = ninth + dot(part[c * 32 : c * 32 + 32], one_hot(pick), precision=lax.Precision.HIGHEST)
    for c in range(3):
        for half in range(2):
            cut = eight[c * 32 : c * 32 + 32, half * LANES : (half + 1) * LANES]
            grads[(c * 2 + half) * 4 : (c * 2 + half) * 4 + 4] = cut.reshape(4, 8, LANES)
    grads[24:28] = ninth.reshape(4, 8, LANES)
    grads[28:32] = jnp.zeros((4, 8, LANES), F32)


def call(kernel, outs, scratch=(), flops=0, moved=0):
    vmem = pl.BlockSpec(memory_space=pltpu.VMEM)
    return pl.pallas_call(
        kernel,
        out_shape=outs,
        out_specs=jax.tree.map(lambda _: vmem, outs),
        scratch_shapes=scratch,
        compiler_params=pltpu.CompilerParams(vmem_limit_bytes=48 * 1024 * 1024),
        cost_estimate=pl.CostEstimate(flops=flops, bytes_accessed=moved, transcendentals=0),
    )


def body(crops, cotangent, weights):
    space = lax.axis_size("space")
    outer = lax.axis_size("chan") * lax.axis_size("batch")
    up = [(i, i + 1) for i in range(space - 1)]
    down = [(i + 1, i) for i in range(space - 1)]
    packed = call(pack_kernel, jax.ShapeDtypeStruct((4, 30, 16, LANES), BF16))(crops[0], cotangent[0])
    own = lax.all_to_all(packed, "chan", 0, 0)
    before = lax.ppermute(own, "space", up)
    after = lax.ppermute(own, "space", down)
    by_out = jnp.transpose(weights, (1, 0, 2)).reshape(864, 32)
    by_in = jnp.transpose(weights, (1, 2, 0)).reshape(864, 32)
    back, grads = call(
        main_kernel,
        (
            jax.ShapeDtypeStruct((4, 2, 12, 16, LANES), BF16),
            jax.ShapeDtypeStruct((32, 8, LANES), F32),
        ),
        [
            pltpu.VMEM((192, 16 * LANES), BF16),
            pltpu.VMEM((3, 384, 192), BF16),
            pltpu.VMEM((3, 192, 128), BF16),
            pltpu.VMEM((128, 14 * LANES), BF16),
            pltpu.VMEM((192, 12 * LANES), BF16),
        ],
    )(before, own, after, by_out, by_in)
    slab = jax.ShapeDtypeStruct((8, 2, 48, LANES), BF16)
    activated, input_grad = call(unpack_kernel, (slab, slab))(lax.all_to_all(back, "chan", 0, 0))

    tiles = 32 // space
    terms = lax.all_to_all(grads.reshape(space, tiles, 8, LANES), "space", 0, 0)
    share = jnp.sum(terms, axis=0)
    terms = lax.all_to_all(jnp.broadcast_to(share, (outer,) + share.shape), ("chan", "batch"), 0, 0)
    cells = lax.axis_size("batch") * space * crops.shape[2] * crops.shape[3] * crops.shape[4]
    share = jnp.sum(terms, axis=0) / jnp.sqrt(jnp.float32(cells))
    whole = lax.all_to_all(jnp.broadcast_to(share, (space,) + share.shape), "space", 0, 0).reshape(32, 8, LANES)
    eight = whole[:24].reshape(3, 2, 4, 8, 4, 32).transpose(2, 3, 1, 4, 0, 5).reshape(32, 8, 3, 32)
    ninth = whole[24:28].reshape(32, 1, 4, 32)[:, :, :3]
    weight_grad = jnp.concatenate([eight, ninth], axis=1).reshape(32, 27, 32)
    return activated[None], input_grad[None], weight_grad


def solution(mesh):
    return jax.shard_map(
        body,
        mesh=mesh,
        in_specs=(
            P("batch", "chan", "space", None, None),
            P("batch", "chan", "space", None, None),
            P(),
        ),
        out_specs=(
            P("batch", "chan", "space", None, None),
            P("batch", "chan", "space", None, None),
            P(),
        ),
        check_vma=False,
    )
```

time: 653 us -> 148 us (0.23)
  waiting for transfers between devices: 527 us -> 33.9 us
  blocking collectives: 0 us -> 82 us
  local copies, waits for them, and re-layouts: 79 us -> 3.04 us
  between operations: 14 us -> 0.75 us
  Pallas kernels: 0 us -> 6.81 us
  matrix products: 6.72 us -> 0 us
    psum x1 -> x0, waiting for transfers between devices: 396 us -> none  [body(): total = lax.psum(full, ('space', 'chan', 'batch'))]
    all_to_all x0 -> x3, blocking collectives: none -> 82 us  [the longest x1 40.5 us: body(): own = lax.all_to_all(packed, 'chan', 0, 0)]
    all_gather x1 -> x0, waiting for transfers between devices: 70.7 us -> none  [body(): every_output = lax.all_gather(upstream_rim, 'chan', axis=0, tiled=True)]
    while x320 -> x0, local copies, waits for them, and re-layouts: 61.8 us -> none
    reduce_scatter x1 -> x0, waiting for transfers between devices: 56.2 us -> none  [body(): lax.psum_scatter(conv_planes(own_padded, own_inputs).astype(jnp.bfloat16)...]
    all_to_all x0 -> x2, waiting for transfers between devices: none -> 28.3 us  [the longest x1 21.2 us: body(): lax.all_to_all(back, 'chan', 0, 0)]
    all_to_all x0 -> x2, starting transfers between devices: none -> 13.4 us  [the longest x1 9.94 us: body(): lax.all_to_all(jnp.broadcast_to(share, (space,) + share.shape), 'space',...]
    ppermute x4 -> x2, starting transfers between devices: 15.8 us -> 6.59 us  [the longest x1 3.48 us: body(): after = lax.ppermute(own, 'space', down)]
  transfers between devices with their start and end apart: 7 -> 4, of which waited for: 4 -> 4; matrix products, arithmetic and copies ran while one was open for 10% -> 0% of each run, Pallas kernels for 0% -> 1%
where the time goes in v1:
time: 148 us; the launch traced here: 147 us
  blocking collectives  82 us (55%)
  waiting for transfers between devices  33.9 us (23%)
  starting transfers between devices  20 us (14%)
  Pallas kernels  6.81 us (5%)
  local copies, waits for them, and re-layouts  3.04 us (2%)
    all_to_all x1, blocking collectives, body(): own = lax.all_to_all(packed, 'chan', 0, 0)  40.5 us
    all_to_all x1, blocking collectives, body(): terms = lax.all_to_all(grads.reshape(space, tiles, 8, LANES), 'space', 0, 0)  22.8 us
    all_to_all x1, waiting for transfers between devices, body(): lax.all_to_all(back, 'chan', 0, 0)  21.2 us
    all_to_all x1, blocking collectives, body(): lax.all_to_all(jnp.broadcast_to(share, (outer,) + share.shape), ('chan',...  18.6 us
    all_to_all x1, starting transfers between devices, body(): lax.all_to_all(jnp.broadcast_to(share, (space,) + share.shape), 'space',...  9.94 us
    all_to_all x1, waiting for transfers between devices, body(): lax.all_to_all(jnp.broadcast_to(share, (space,) + share.shape), 'space',...  7.12 us
    pallas_call x1, Pallas kernels, body(): call(main_kernel, (jax.ShapeDtypeStruct((4, 2, 12, 16, LANES), BF16), jax...  4.8 us
    ppermute x1, waiting for transfers between devices, body(): after = lax.ppermute(own, 'space', down)  4.4 us
  transfers between devices with their start and end apart: 4, of which 4 were waited for; matrix products, arithmetic and copies ran while one was open for 0% of the time, Pallas kernels for 1%

profile of v1, /device:TPU:1, one launch (start us, length us, event | category | flops | bytes accessed | tf_op | source)
XLA Modules:
  0.0 147.3 jit_solution(5567175746481576870)
XLA Ops:
  0.6 0.0 copy-start.1
  0.6 0.9 copy-done.1
  1.6 0.0 copy-start.2
  1.6 0.9 copy-done.2
  2.5 0.6 shard_map.58
  3.1 0.0 copy-start
  3.1 40.5 %all_to_all.25.own = bf16[4,30,16,128]{3,2,1,0:T(8,128)(2,1)S(1)} all-to-all(bf16[4,30,16,128]{3,2,1,0:T(8,128)(2,1)S(1)} %shard_map.58), channel_id=1, replica_groups=mesh['space'=32,'chan'=4,'batch'=4] {'chan'}, dimensions={0} | all-to-all | bytes 983040 | tf_op jit(solution)/shard_map/all_to_all | solution.py:184
  43.6 3.5 %collective-permute-start.1 = (bf16[4,30,16,128]{3,2,1,0:T(8,128)(2,1)S(1)}, bf16[4,30,16,128]{3,2,1,0:T(8,128)(2,1)S(1)}, u32[]{:S(2)}, u32[]{:S(2)}) collective-permute-start(bf16[4,30,16,128]{3,2,1,0:T(8,128)(2,1)S(1)} %all_to_all.25.own), channel_id=1, source_target_pairs={{16,0},{32,16},{48,32},{64,48},{80,64},{96,80},{112,96},{128,112},... | collective-permute-start | bytes 1474568 | tf_op jit(solution)/shard_map/ppermute | solution.py:186
  47.1 3.1 %collective-permute-start = (bf16[4,30,16,128]{3,2,1,0:T(8,128)(2,1)S(1)}, bf16[4,30,16,128]{3,2,1,0:T(8,128)(2,1)S(1)}, u32[]{:S(2)}, u32[]{:S(2)}) collective-permute-start(bf16[4,30,16,128]{3,2,1,0:T(8,128)(2,1)S(1)} %all_to_all.25.own), channel_id=1, source_target_pairs={{0,16},{16,32},{32,48},{48,64},{64,80},{80,96},{96,112},{112,128},... | collective-permute-start | bytes 1474568 | tf_op jit(solution)/shard_map/ppermute | solution.py:185
  50.2 0.0 copy-done
  50.2 0.2 copy.16
  50.4 4.4 %collective-permute-done.1.after = bf16[4,30,16,128]{3,2,1,0:T(8,128)(2,1)S(1)} collective-permute-done((bf16[4,30,16,128]{3,2,1,0:T(8,128)(2,1)S(1)}, bf16[4,30,16,128]{3,2,1,0:T(8,128)(2,1)S(1)}, u32[]{:S(2)}, u32[]{:S(2)}) %collective-permute-start.1) | collective-permute-done | bytes 491552 | tf_op jit(solution)/shard_map/ppermute | solution.py:186
  54.8 1.2 collective-permute-done.before
  56.0 4.8 %shard_map.59 = (bf16[4,2,12,16,128]{4,3,2,1,0:T(8,128)(2,1)}, f32[32,8,128]{2,1,0:T(8,128)S(1)}) custom-call(bf16[4,30,16,128]{3,2,1,0:T(8,128)(2,1)S(1)} %collective-permute-done.before, bf16[4,30,16,128]{3,2,1,0:T(8,128)(2,1)S(1)} %all_to_all.25.own, bf16[4,30,16,128]{3,2,1,0:T(8,128)(2,1)S(1)} %collective-permute-done.1.after, ...), custom_call_target="tpu_custom_call" | custom-call | tf_op jit(solution)/shard_map/pallas_call | solution.py:189
  60.8 22.8 %all_to_all.26 = f32[32,1,8,128]{3,2,1,0:T(8,128)S(1)} all-to-all(f32[32,1,8,128]{3,2,1,0:T(8,128)S(1)} %bitcast.25), channel_id=1, replica_groups=mesh['space'=32,'chan'=4,'batch'=4] {'space'}, dimensions={0} | all-to-all | bytes 262144 | tf_op jit(solution)/shard_map/all_to_all | solution.py:207
  83.6 18.6 %all_to_all.27 = f32[16,1,8,128]{3,2,1,0:T(8,128)S(1)} all-to-all(f32[16,1,8,128]{3,2,1,0:T(8,128)S(1)} %broadcast_in_dim.14), channel_id=1, replica_groups=mesh['space'=32,'chan'=4,'batch'=4] {'chan','batch'}, dimensions={0} | all-to-all | bytes 131072 | tf_op jit(solution)/shard_map/all_to_all | solution.py:209
  102.3 3.5 %all-to-all-start.1 = ((bf16[4,2,12,16,128]{4,3,2,1,0:T(8,128)(2,1)}), bf16[4,2,12,16,128]{4,3,2,1,0:T(8,128)(2,1)S(1)}, u32[]{:S(2)}, u32[]{:S(2)}) async-start(bf16[4,2,12,16,128]{4,3,2,1,0:T(8,128)(2,1)} %get-tuple-element.7), calls=%async_computation.1 | async-start | bytes 786432 | tf_op jit(solution)/shard_map/all_to_all | solution.py:204
  105.8 21.2 %all-to-all-done.1.back = bf16[4,2,12,16,128]{4,3,2,1,0:T(8,128)(2,1)S(1)} async-done(((bf16[4,2,12,16,128]{4,3,2,1,0:T(8,128)(2,1)}), bf16[4,2,12,16,128]{4,3,2,1,0:T(8,128)(2,1)S(1)}, u32[]{:S(2)}, u32[]{:S(2)}) %all-to-all-start.1) | async-done | bytes 393248 | tf_op jit(solution)/shard_map/all_to_all | solution.py:204
  127.0 0.7 broadcast_in_dim.15
  127.6 9.9 %all-to-all-start.4 = ((f32[32,1,8,128]{3,2,1,0:T(8,128)}), f32[32,1,8,128]{3,2,1,0:T(8,128)S(1)}, u32[]{:S(2)}, u32[]{:S(2)}) async-start(f32[32,1,8,128]{3,2,1,0:T(8,128)} %broadcast_in_dim.15), calls=%async_computation.4 | async-start | bytes 262144 | tf_op jit(solution)/shard_map/all_to_all | solution.py:212
  137.6 1.4 shard_map.60
  139.0 7.1 %all-to-all-done.4 = f32[32,1,8,128]{3,2,1,0:T(8,128)S(1)} async-done(((f32[32,1,8,128]{3,2,1,0:T(8,128)}), f32[32,1,8,128]{3,2,1,0:T(8,128)S(1)}, u32[]{:S(2)}, u32[]{:S(2)}) %all-to-all-start.4) | async-done | bytes 131104 | tf_op jit(solution)/shard_map/all_to_all | solution.py:212
  146.1 0.1 reshape.46
  146.2 0.2 reshape.44
  146.5 0.8 pad_maximum_fusion
  (8 shorter events, 0.1 us)
Async XLA Ops:
  0.6 0.9 copy-start.1
  1.6 0.9 copy-start.2
  3.1 47.1 %copy-start = (bf16[32,27,32]{2,0,1:T(8,128)(2,1)S(1)}, bf16[32,27,32]{2,0,1:T(8,128)(2,1)}, u32[]{:S(2)}) copy-start(bf16[32,27,32]{2,0,1:T(8,128)(2,1)} %param.5) | copy-start | bytes 165892
  43.6 11.2 %collective-permute-start.1 = (bf16[4,30,16,128]{3,2,1,0:T(8,128)(2,1)S(1)}, bf16[4,30,16,128]{3,2,1,0:T(8,128)(2,1)S(1)}, u32[]{:S(2)}, u32[]{:S(2)}) collective-permute-start(bf16[4,30,16,128]{3,2,1,0:T(8,128)(2,1)S(1)} %all_to_all.25.own), channel_id=1, source_target_pairs={{16,0},{32,16},{48,32},{64,48},{80,64},{96,80},{112,96},{128,112},... | collective-permute-start | bytes 1474568 | tf_op jit(solution)/shard_map/ppermute | solution.py:186
  47.1 8.9 %collective-permute-start = (bf16[4,30,16,128]{3,2,1,0:T(8,128)(2,1)S(1)}, bf16[4,30,16,128]{3,2,1,0:T(8,128)(2,1)S(1)}, u32[]{:S(2)}, u32[]{:S(2)}) collective-permute-start(bf16[4,30,16,128]{3,2,1,0:T(8,128)(2,1)S(1)} %all_to_all.25.own), channel_id=1, source_target_pairs={{0,16},{16,32},{32,48},{48,64},{64,80},{80,96},{96,112},{112,128},... | collective-permute-start | bytes 1474568 | tf_op jit(solution)/shard_map/ppermute | solution.py:185
  102.3 24.7 %all-to-all-start.1 = ((bf16[4,2,12,16,128]{4,3,2,1,0:T(8,128)(2,1)}), bf16[4,2,12,16,128]{4,3,2,1,0:T(8,128)(2,1)S(1)}, u32[]{:S(2)}, u32[]{:S(2)}) async-start(bf16[4,2,12,16,128]{4,3,2,1,0:T(8,128)(2,1)} %get-tuple-element.7), calls=%async_computation.1 | async-start | bytes 786432 | tf_op jit(solution)/shard_map/all_to_all | solution.py:204
  127.6 18.5 %all-to-all-start.4 = ((f32[32,1,8,128]{3,2,1,0:T(8,128)}), f32[32,1,8,128]{3,2,1,0:T(8,128)S(1)}, u32[]{:S(2)}, u32[]{:S(2)}) async-start(f32[32,1,8,128]{3,2,1,0:T(8,128)} %broadcast_in_dim.15), calls=%async_computation.4 | async-start | bytes 262144 | tf_op jit(solution)/shard_map/all_to_all | solution.py:212

commit v2 on v1

v2 whole, which is shorter than its diff:
```python
import functools

import jax
import jax.numpy as jnp
from jax import lax
from jax.experimental import pallas as pl
from jax.experimental.pallas import tpu as pltpu
from jax.sharding import Mesh, PartitionSpec as P

LANES = 128
F32 = jnp.float32
BF16 = jnp.bfloat16


def iota(shape, dim):
    return lax.broadcasted_iota(jnp.int32, shape, dim)


def one_hot(hit):
    return jnp.where(hit, 1.0, 0.0)


def dot(left, right, **options):
    return jnp.dot(left, right, preferred_element_type=F32, **options)


def split(block):
    high = block.astype(BF16)
    rest = block - high.astype(F32)
    middle = rest.astype(BF16)
    low = (rest - middle.astype(F32)).astype(BF16)
    return jnp.concatenate([high, middle, low], axis=0)


def shifted(block, step):
    moved = pltpu.roll(block, step % LANES, 1)
    lane = iota(block.shape, 1)
    edge = 0 if step == 1 else LANES - 1
    return jnp.where(lane == edge, 0.0, moved)


def pack_kernel(place, crops, cotangent, *outs):
    row = iota((256, LANES), 0)
    lane = iota((256, LANES), 1)
    base = (row & 7) * 96 + (row >> 3 & 1) * 48
    moves = []
    for step in range(4):
        part = (place[0] + step) & 3
        y = (row >> 4) + (12 * part - 2)
        source = jnp.where((y >= 0) & (y < 48), base + y, -1)
        tiles = [one_hot(source == lane + k * LANES).astype(BF16) for k in range(6)]
        moves.append(jnp.concatenate(tiles, axis=1))
    both = jnp.concatenate([crops[...].reshape(768, LANES), cotangent[...].reshape(768, LANES)], axis=1)
    for move, out in zip(moves, outs):
        moved = dot(move, both).astype(BF16).reshape(16, 16, 2 * LANES)
        out[0:16] = moved[:, :, :LANES]
        out[16:30] = moved[1:15, :, LANES:]


def unpack_kernel(place, *refs):
    parts, (activated, input_grad) = refs[:4], refs[4:]
    rows = [
        jnp.concatenate([part[which * 12 : which * 12 + 12].reshape(192, LANES) for part in parts], axis=0)
        for which in range(2)
    ]
    both = jnp.concatenate(rows, axis=1)
    outer = iota((16, 48, LANES), 0)
    y = iota((16, 48, LANES), 1)
    part = (y >= 12).astype(jnp.int32) + (y >= 24).astype(jnp.int32) + (y >= 36).astype(jnp.int32)
    step = (part + 4 - place[0]) & 3
    source = (step * 192 + (y - 12 * part) * 16 + (outer & 1) * 8 + (outer >> 1)).reshape(768, LANES)
    lane = iota((768, LANES), 1)
    move = jnp.concatenate([one_hot(source == lane + k * LANES).astype(BF16) for k in range(6)], axis=1)
    moved = dot(move, both).astype(BF16)
    activated[...] = moved[:, :LANES].reshape(8, 2, 48, LANES)
    input_grad[...] = moved[:, LANES:].reshape(8, 2, 48, LANES)


def band_kernel(by_out, by_in, forward, backward):
    column = iota((32, 192), 1)
    spread = one_hot(column // 16 % 4 * 8 + column % 8 == iota((32, 192), 0)).astype(BF16)
    wide = dot(by_out[...], spread)
    column = iota((8, 192), 1)
    plane = column // 64 * 2 + column // 8 % 2
    for c in range(3):
        for b in range(3):

            def band(group, target):
                total = jnp.zeros((8, 192), F32)
                for a in range(3):
                    low = (9 * a + 3 * b + c) * 32 + group * 8
                    total = jnp.where(plane == target + a - 1, wide[low : low + 8], total)
                return total

            pieces = [band(group, 2 + x) for group in range(4) for x in range(2)]
            pieces += [band(group, 1) for group in range(4)]
            pieces += [band(group, 4) for group in range(4)]
            forward[b, c * 128 : c * 128 + 128] = jnp.concatenate(pieces, axis=0).astype(BF16)

    column = iota((32, 128), 1)
    channel = jnp.where(column < 64, column // 16 * 8 + column % 8, column % 32)
    wide_in = dot(by_in[...], one_hot(channel == iota((32, 128), 0)).astype(BF16))
    column = iota((8, 128), 1)
    plane_in = jnp.where(column < 64, 2 + column // 8 % 2, jnp.where(column < 96, 1, 4))
    for c in range(3):
        for b in range(3):
            pieces = []
            for group in range(4):
                for x in range(2):
                    total = jnp.zeros((8, 128), F32)
                    for a in range(3):
                        low = (26 - (9 * a + 3 * b + c)) * 32 + group * 8
                        total = jnp.where(plane_in == 1 + x + a, wide_in[low : low + 8], total)
                    pieces.append(total)
            backward[b, c * 64 : c * 64 + 64] = jnp.concatenate(pieces, axis=0).astype(BF16)


def forward_kernel(place, *refs):
    parts, refs = refs[:9], refs[9:]
    forward, activated, upper, grads, field, cots, sides = refs
    member, core = place[0], place[1]

    for s in range(4):
        group = (member + s) & 3
        mine, near, far = parts[(0, 6, 3, 3)[s] :][:3]
        base = 30 if s == 3 else 0
        near_row = pl.multiple_of((1 - core) * 128 + group * 16, 16)
        far_row = pl.multiple_of(core * 128 + group * 16, 16)
        own_row = pl.multiple_of(64 + group * 16, 16)
        for row in range(16):
            here = slice(row * LANES, (row + 1) * LANES)
            field[pl.ds(near_row, 16), here] = near[base + row]
            field[pl.ds(own_row, 16), here] = mine[base + row]
            field[pl.ds(far_row, 16), here] = far[base + row]
        cot_row = pl.multiple_of(group * 16, 16)
        near_cot = pl.multiple_of(64 + (1 - core) * 32 + group * 8, 8)
        far_cot = pl.multiple_of(64 + core * 32 + group * 8, 8)
        for row in range(14):
            here = slice(row * LANES, (row + 1) * LANES)
            cots[pl.ds(cot_row, 16), here] = mine[base + 16 + row].astype(F32)
            wide_near = near[base + 16 + row].astype(F32)
            wide_far = far[base + 16 + row].astype(F32)
            cots[pl.ds(near_cot, 8), here] = jnp.where(core == 0, wide_near[0:8], wide_near[8:16])
            cots[pl.ds(far_cot, 8), here] = jnp.where(core == 0, wide_far[8:16], wide_far[0:8])

    for pair in range(7):
        low = pair * 2
        total = sum(dot(forward[b], field[:, (low + b) * LANES : (low + b + 2) * LANES]) for b in range(3))
        for side in range(2):
            row = low + side
            cut = total[:, side * LANES : (side + 1) * LANES]
            pre = cut[128:256] + shifted(cut[0:128], 1) + shifted(cut[256:384], -1)
            power = jnp.exp(jnp.minimum(pre, 0.0))
            if 1 <= row <= 12:
                result = jnp.where(pre[:64] > 0, pre[:64], power[:64] - 1.0).astype(BF16)
                activated[:, (row - 1) * LANES : row * LANES] = result
            cot = cots[:, row * LANES : (row + 1) * LANES]
            up = jnp.where(pre > 0, cot, cot * power).astype(BF16)
            upper[:, row * LANES : (row + 1) * LANES] = up
            if 1 <= row <= 12:
                here = slice((row - 1) * LANES, row * LANES)
                wide_up = up[:64].astype(F32)
                sides[0:64, here] = shifted(wide_up, -1).astype(BF16)
                sides[64:128, here] = up[:64]
                sides[128:192, here] = shifted(wide_up, 1).astype(BF16)

    row = iota((192, 256), 0)
    col = iota((192, 256), 1)
    row_plane = row // 64 * 2 + row // 8 % 2
    same = row // 16 % 4 * 8 + row % 8 == col % 32
    row9 = iota((192, 128), 0)
    col9 = iota((192, 128), 1)
    plane9 = row9 // 64 * 2 + row9 // 8 % 2
    same9 = row9 // 16 % 4 * 8 + row9 % 8 == col9 % 32
    eight = jnp.zeros((96, 256), F32)
    ninth = jnp.zeros((32, 128), F32)
    for b in range(3):
        product = lax.dot_general(
            sides[...],
            field[:, (1 + b) * LANES : (13 + b) * LANES],
            (((1,), (1,)), ((), ())),
            preferred_element_type=F32,
        ).reshape(12, 2, 8, 192)
        for x in range(2):
            part = split(product[:, x].reshape(96, 192))
            pick = same & (col // 32 % 3 == b) & (row_plane == 1 + x + col // 96)
            picked = dot(part, one_hot(pick).astype(BF16))
            eight = eight + (picked[0:96] + picked[96:192] + picked[192:288])
            if b == 2:
                for c in range(3):
                    pick = same9 & (col9 // 32 == c) & (plane9 == 3 + x)
                    rows = [part[k * 96 + c * 32 : k * 96 + c * 32 + 32] for k in range(3)]
                    picked = dot(jnp.concatenate(rows, axis=0), one_hot(pick).astype(BF16))
                    ninth = ninth + (picked[0:32] + picked[32:64] + picked[64:96])
    for c in range(3):
        for half in range(2):
            cut = eight[c * 32 : c * 32 + 32, half * LANES : (half + 1) * LANES]
            grads[(c * 2 + half) * 4 : (c * 2 + half) * 4 + 4] = cut.reshape(4, 8, LANES)
    grads[24:28] = ninth.reshape(4, 8, LANES)
    grads[28:32] = jnp.zeros((4, 8, LANES), F32)


def backward_kernel(place, activated, upper, backward, *refs):
    backs, results = refs[:4], refs[4]
    member = place[0]
    for pair in range(6):
        low = pair * 2
        total = sum(dot(backward[b], upper[:, (low + b) * LANES : (low + b + 2) * LANES]) for b in range(3))
        for side in range(2):
            cut = total[:, side * LANES : (side + 1) * LANES]
            grad = cut[64:128] + shifted(cut[0:64], 1) + shifted(cut[128:192], -1)
            results[:, (low + side) * LANES : (low + side + 1) * LANES] = grad.astype(BF16)

    for step, back in enumerate(backs):
        for which, source in enumerate((activated, results)):
            low = pl.multiple_of(((member + step) & 3) * 16, 16)
            for row in range(12):
                back[which * 12 + row] = source[pl.ds(low, 16), row * LANES : (row + 1) * LANES]


def call(kernel, outs, scratch=(), place=False, flops=0, moved=0):
    vmem = pl.BlockSpec(memory_space=pltpu.VMEM)
    smem = pl.BlockSpec(memory_space=pltpu.SMEM)

    def run(*args):
        specs = [vmem] * len(args)
        if place:
            specs[0] = smem
        return pl.pallas_call(
            kernel,
            out_shape=outs,
            in_specs=specs,
            out_specs=jax.tree.map(lambda _: vmem, outs),
            scratch_shapes=scratch,
            compiler_params=pltpu.CompilerParams(vmem_limit_bytes=48 * 1024 * 1024),
            cost_estimate=pl.CostEstimate(flops=flops, bytes_accessed=moved, transcendentals=0),
        )(*args)

    return run


def reshard(parts):
    got = [parts[0], None, None, None]
    for step in (2, 1, 3):
        got[4 - step] = lax.ppermute(parts[step], "chan", [(i, (i + step) % 4) for i in range(4)])
    return got


def body(crops, cotangent, weights):
    place = jnp.stack([lax.axis_index("chan"), lax.axis_index("core")]).astype(jnp.int32)
    piece = jax.ShapeDtypeStruct((30, 16, LANES), BF16)
    packed = call(pack_kernel, (piece,) * 4, place=True, flops=10**9)(place, crops[0], cotangent[0])
    got = reshard(packed)
    chips = lax.axis_size("zlo") * lax.axis_size("y")
    remote = [(2 * i + 1, 2 * i + 2) for i in range(chips - 1)]
    remote += [(j, i) for i, j in remote]
    parts = []
    for mine in (got[0], jnp.concatenate([got[2], got[3]], axis=0), got[1]):
        near = lax.ppermute(mine, "core", [(0, 1), (1, 0)])
        far = lax.ppermute(mine, ("zlo", "y", "core"), remote)
        parts += [mine, near, far]
    by_out = jnp.transpose(weights, (1, 0, 2)).reshape(864, 32)
    by_in = jnp.transpose(weights, (1, 2, 0)).reshape(864, 32)
    forward, backward = call(
        band_kernel,
        (jax.ShapeDtypeStruct((3, 384, 192), BF16), jax.ShapeDtypeStruct((3, 192, 128), BF16)),
        flops=10**9,
    )(by_out, by_in)
    rows = jax.ShapeDtypeStruct((64, 12 * LANES), BF16)
    activated, upper, grads = call(
        forward_kernel,
        (rows, jax.ShapeDtypeStruct((128, 14 * LANES), BF16), jax.ShapeDtypeStruct((32, 8, LANES), F32)),
        [
            pltpu.VMEM((192, 16 * LANES), BF16),
            pltpu.VMEM((128, 14 * LANES), F32),
            pltpu.VMEM((192, 12 * LANES), BF16),
        ],
        place=True,
        flops=3 * 10**9,
    )(place, *parts, forward)
    piece = jax.ShapeDtypeStruct((24, 16, LANES), BF16)
    backs = call(
        backward_kernel,
        (piece,) * 4,
        [pltpu.VMEM((64, 12 * LANES), BF16)],
        place=True,
        flops=2 * 10**9,
    )(place, activated, upper, backward)
    slab = jax.ShapeDtypeStruct((8, 2, 48, LANES), BF16)
    activated, input_grad = call(unpack_kernel, (slab, slab), place=True, flops=10**9)(place, *reshard(backs))

    plane = ("y", "core", "batch")
    column = ("zlo", "chan")
    pieces, rest = lax.axis_size(plane), lax.axis_size(column)
    terms = lax.all_to_all(grads.reshape((pieces, -1) + grads.shape[1:]), plane, 0, 0)
    share = jnp.sum(terms, axis=0)
    terms = lax.all_to_all(jnp.broadcast_to(share, (rest,) + share.shape), column, 0, 0)
    cells = pieces * rest // lax.axis_size("chan") * crops.shape[2] * crops.shape[3] * crops.shape[4]
    share = jnp.sum(terms, axis=0) / jnp.sqrt(jnp.float32(cells))
    whole = lax.all_to_all(jnp.broadcast_to(share, (pieces,) + share.shape), plane, 0, 0).reshape(32, 8, LANES)
    eight = whole[:24].reshape(3, 2, 4, 8, 4, 32).transpose(2, 3, 1, 4, 0, 5).reshape(32, 8, 3, 32)
    ninth = whole[24:28].reshape(32, 1, 4, 32)[:, :, :3]
    weight_grad = jnp.concatenate([eight, ninth], axis=1).reshape(32, 27, 32)
    return activated[None], input_grad[None], weight_grad


def solution(mesh):
    space, chan, batch = (mesh.shape[name] for name in ("space", "chan", "batch"))
    cut = mesh.devices.reshape(space // 8, 4, 2, chan, batch)
    fine = Mesh(cut, ("zlo", "y", "core", "chan", "batch"))
    spec = P("batch", "chan", ("zlo", "y", "core"), None, None)
    return jax.shard_map(
        body,
        mesh=fine,
        in_specs=(spec, spec, P()),
        out_specs=(spec, spec, P()),
        check_vma=False,
    )
```

time: 148 us -> 122 us (0.82)
  blocking collectives: 82 us -> 17.1 us
  starting transfers between devices: 20 us -> 83.2 us
  waiting for transfers between devices: 33.9 us -> 7.83 us
    all_to_all x3 -> x1, blocking collectives: 82 us -> 17.1 us  [body(): lax.all_to_all(grads.reshape((pieces, -1) + grads.shape[1:]), plane, 0, 0)]
    ppermute x2 -> x12, starting transfers between devices: 6.59 us -> 64.5 us  [the longest x6 46.6 us: reshard(): lax.ppermute(parts[step], 'chan', [(i, (i + step) % 4) for i in range(4)])]
    all_to_all x2, waiting for transfers between devices: 28.3 us -> 5.83 us  [the longest x1 5.82 us: body(): lax.all_to_all(jnp.broadcast_to(share, (pieces,) + share.shape), plane, 0...]
    all_to_all x2, starting transfers between devices: 13.4 us -> 18.7 us  [the longest x1 13.3 us: body(): lax.all_to_all(jnp.broadcast_to(share, (rest,) + share.shape), column, 0, 0)]
    ppermute x2 -> x12, waiting for transfers between devices: 5.58 us -> 2.01 us  [the longest x6 1.3 us: reshard(): lax.ppermute(parts[step], 'chan', [(i, (i + step) % 4) for i in range(4)])]
    pallas_call x3 -> x5, Pallas kernels: 6.81 us -> 8.15 us  [run(): pl.pallas_call(kernel, out_shape=outs, in_specs=specs, out_specs=jax.tree...]
  transfers between devices with their start and end apart: 4 -> 14, of which waited for: 4 -> 3; matrix products, arithmetic and copies ran while one was open for 0% -> 1% of each run, Pallas kernels for 1% -> 3%
where the time goes in v2:
time: 122 us
  starting transfers between devices  83.2 us (68%)
  blocking collectives  17.1 us (14%)
  Pallas kernels  8.15 us (7%)
  waiting for transfers between devices  7.83 us (6%)
  local copies, waits for them, and re-layouts  3.7 us (3%)
    ppermute x6, starting transfers between devices, reshard(): lax.ppermute(parts[step], 'chan', [(i, (i + step) % 4) for i in range(4)])  46.6 us
    all_to_all x1, blocking collectives, body(): lax.all_to_all(grads.reshape((pieces, -1) + grads.shape[1:]), plane, 0, 0)  17.1 us
    all_to_all x1, starting transfers between devices, body(): lax.all_to_all(jnp.broadcast_to(share, (rest,) + share.shape), column, 0, 0)  13.3 us
    ppermute x3, starting transfers between devices, body(): far = lax.ppermute(mine, ('zlo', 'y', 'core'), remote)  11.6 us
    pallas_call x5, Pallas kernels, run(): pl.pallas_call(kernel, out_shape=outs, in_specs=specs, out_specs=jax.tree...  8.15 us
    ppermute x3, starting transfers between devices, body(): near = lax.ppermute(mine, 'core', [(0, 1), (1, 0)])  6.25 us
    all_to_all x1, waiting for transfers between devices, body(): lax.all_to_all(jnp.broadcast_to(share, (pieces,) + share.shape), plane, 0...  5.82 us
    all_to_all x1, starting transfers between devices, body(): lax.all_to_all(jnp.broadcast_to(share, (pieces,) + share.shape), plane, 0...  5.43 us
  transfers between devices with their start and end apart: 14, of which 3 were waited for; matrix products, arithmetic and copies ran while one was open for 1% of the time, Pallas kernels for 3%

profile of v2, /device:TPU:1, one launch (start us, length us, event | category | flops | bytes accessed | tf_op | source)
XLA Modules:
  0.0 121.8 jit_solution(9804642578910904754)
XLA Ops:
  0.6 0.1 pad_add_fusion.place
  0.7 0.9 copy-done.1
  1.6 0.9 copy-done.2
  2.6 1.1 shard_map.58
  3.7 16.3 %collective-permute-start.2 = (bf16[30,16,128]{2,1,0:T(8,128)(2,1)S(1)}, bf16[30,16,128]{2,1,0:T(8,128)(2,1)S(1)}, u32[]{:S(2)}, u32[]{:S(2)}) collective-permute-start(bf16[30,16,128]{2,1,0:T(8,128)(2,1)S(1)} %get-tuple-element.19), channel_id=1, source_target_pairs={{0,8},{4,12},{8,0},{12,4},{1,9},{5,13},{9,1},{13,5},{2,10},{6,14},... | collective-permute-start | bytes 368648 | tf_op jit(solution)/shard_map/ppermute | solution.py:245
  20.0 4.0 %collective-permute-start.3 = (bf16[30,16,128]{2,1,0:T(8,128)(2,1)S(1)}, bf16[30,16,128]{2,1,0:T(8,128)(2,1)S(1)}, u32[]{:S(2)}, u32[]{:S(2)}) collective-permute-start(bf16[30,16,128]{2,1,0:T(8,128)(2,1)S(1)} %get-tuple-element.20), channel_id=1, source_target_pairs={{0,4},{4,8},{8,12},{12,0},{1,5},{5,9},{9,13},{13,1},{2,6},{6,10},{... | collective-permute-start | bytes 368648 | tf_op jit(solution)/shard_map/ppermute | solution.py:245
  24.0 5.2 %collective-permute-start.6 = (bf16[30,16,128]{2,1,0:T(8,128)(2,1)S(1)}, bf16[30,16,128]{2,1,0:T(8,128)(2,1)S(1)}, u32[]{:S(2)}, u32[]{:S(2)}) collective-permute-start(bf16[30,16,128]{2,1,0:T(8,128)(2,1)S(1)} %get-tuple-element.21), channel_id=1, source_target_pairs={{0,12},{4,0},{8,4},{12,8},{1,13},{5,1},{9,5},{13,9},{2,14},{6,2},{... | collective-permute-start | bytes 368648 | tf_op jit(solution)/shard_map/ppermute | solution.py:245
  29.2 4.7 %collective-permute-start.1 = (bf16[30,16,128]{2,1,0:T(8,128)(2,1)S(1)}, bf16[30,16,128]{2,1,0:T(8,128)(2,1)S(1)}, u32[]{:S(2)}, u32[]{:S(2)}) collective-permute-start(bf16[30,16,128]{2,1,0:T(8,128)(2,1)S(1)} %get-tuple-element.18.refs_0_), channel_id=1, source_target_pairs={{16,32},{48,64},{80,96},{112,128},{144,160},{176,192},{208,224},{2... | collective-permute-start | bytes 368648 | tf_op jit(solution)/shard_map/ppermute | solution.py:260
  34.0 2.2 %collective-permute-start.5 = (bf16[60,16,128]{2,1,0:T(8,128)(2,1)S(1)}, bf16[60,16,128]{2,1,0:T(8,128)(2,1)S(1)}, u32[]{:S(2)}, u32[]{:S(2)}) collective-permute-start(bf16[60,16,128]{2,1,0:T(8,128)(2,1)S(1)} %constant_dynamic-update-slice_fusion.refs_3_), channel_id=1, source_target_pairs={{16,32},{48,64},{80,96},{112,128},{144,160},{176,192},{208,224},{2... | collective-permute-start | bytes 737288 | tf_op jit(solution)/shard_map/ppermute | solution.py:260
  36.2 1.9 %collective-permute-start.4 = (bf16[60,16,128]{2,1,0:T(8,128)(2,1)S(1)}, bf16[60,16,128]{2,1,0:T(8,128)(2,1)S(1)}, u32[]{:S(2)}, u32[]{:S(2)}) collective-permute-start(bf16[60,16,128]{2,1,0:T(8,128)(2,1)S(1)} %constant_dynamic-update-slice_fusion.refs_3_), channel_id=1, source_target_pairs={{0,16},{16,0},{1,17},{17,1},{2,18},{18,2},{3,19},{19,3},{4,20},{20... | collective-permute-start | bytes 737288 | tf_op jit(solution)/shard_map/ppermute | solution.py:259
  38.1 2.4 %collective-permute-start = (bf16[30,16,128]{2,1,0:T(8,128)(2,1)S(1)}, bf16[30,16,128]{2,1,0:T(8,128)(2,1)S(1)}, u32[]{:S(2)}, u32[]{:S(2)}) collective-permute-start(bf16[30,16,128]{2,1,0:T(8,128)(2,1)S(1)} %get-tuple-element.18.refs_0_), channel_id=1, source_target_pairs={{0,16},{16,0},{1,17},{17,1},{2,18},{18,2},{3,19},{19,3},{4,20},{20... | collective-permute-start | bytes 368648 | tf_op jit(solution)/shard_map/ppermute | solution.py:259
  40.5 1.3 %collective-permute-done.6.refs_6_ = bf16[30,16,128]{2,1,0:T(8,128)(2,1)S(1)} collective-permute-done((bf16[30,16,128]{2,1,0:T(8,128)(2,1)S(1)}, bf16[30,16,128]{2,1,0:T(8,128)(2,1)S(1)}, u32[]{:S(2)}, u32[]{:S(2)}) %collective-permute-start.6) | collective-permute-done | bytes 122912 | tf_op jit(solution)/shard_map/ppermute | solution.py:245
  41.8 4.7 %collective-permute-start.8 = (bf16[30,16,128]{2,1,0:T(8,128)(2,1)S(1)}, bf16[30,16,128]{2,1,0:T(8,128)(2,1)S(1)}, u32[]{:S(2)}, u32[]{:S(2)}) collective-permute-start(bf16[30,16,128]{2,1,0:T(8,128)(2,1)S(1)} %collective-permute-done.6.refs_6_), channel_id=1, source_target_pairs={{16,32},{48,64},{80,96},{112,128},{144,160},{176,192},{208,224},{2... | collective-permute-start | bytes 368648 | tf_op jit(solution)/shard_map/ppermute | solution.py:260
  46.6 1.9 %collective-permute-start.7 = (bf16[30,16,128]{2,1,0:T(8,128)(2,1)S(1)}, bf16[30,16,128]{2,1,0:T(8,128)(2,1)S(1)}, u32[]{:S(2)}, u32[]{:S(2)}) collective-permute-start(bf16[30,16,128]{2,1,0:T(8,128)(2,1)S(1)} %collective-permute-done.6.refs_6_), channel_id=1, source_target_pairs={{0,16},{16,0},{1,17},{17,1},{2,18},{18,2},{3,19},{19,3},{4,20},{20... | collective-permute-start | bytes 368648 | tf_op jit(solution)/shard_map/ppermute | solution.py:259
  48.5 0.2 copy.16
  48.7 0.4 shard_map.59
  49.1 0.7 collective-permute-done.7.refs_7_
  49.8 3.6 %shard_map.60 = (bf16[64,1536]{1,0:T(8,128)(2,1)S(1)}, bf16[128,1792]{1,0:T(8,128)(2,1)S(1)}, f32[32,8,128]{2,1,0:T(8,128)S(1)}) custom-call(s32[2]{0:T(128)S(1)} %pad_add_fusion.place, bf16[30,16,128]{2,1,0:T(8,128)(2,1)S(1)} %get-tuple-element.18.refs_0_, bf16[30,16,128]{2,1,0:T(8,128)(2,1)S(1)} %collective-permute-done.refs_1_, ...), custom_call_target="tpu_custom_call" | custom-call | flops 3000000000 | tf_op jit(solution)/shard_map/pallas_call | solution.py:229
  53.4 17.1 %all_to_all.15 = f32[32,1,8,128]{3,2,1,0:T(8,128)S(1)} all-to-all(f32[32,1,8,128]{3,2,1,0:T(8,128)S(1)} %bitcast.25), channel_id=1, replica_groups=mesh['zlo'=4,'y'=4,'core'=2,'chan'=4,'batch'=4] {'y','core','batch'}, dimensions={0} | all-to-all | bytes 262144 | tf_op jit(solution)/shard_map/all_to_all | solution.py:295
  70.5 0.6 broadcast_in_dim.14
  71.1 13.3 %all-to-all-start.1 = ((f32[16,1,8,128]{3,2,1,0:T(8,128)}), f32[16,1,8,128]{3,2,1,0:T(8,128)S(1)}, u32[]{:S(2)}, u32[]{:S(2)}) async-start(f32[16,1,8,128]{3,2,1,0:T(8,128)} %broadcast_in_dim.14), calls=%async_computation.1 | async-start | bytes 131072 | tf_op jit(solution)/shard_map/all_to_all | solution.py:297
  84.4 1.2 %shard_map.61 = (bf16[24,16,128]{2,1,0:T(8,128)(2,1)S(1)}, bf16[24,16,128]{2,1,0:T(8,128)(2,1)S(1)}, bf16[24,16,128]{2,1,0:T(8,128)(2,1)S(1)}, bf16[24,16,128]{2,1,0:T(8,128)(2,1)S(1)}) custom-call(s32[2]{0:T(128)S(1)} %pad_add_fusion.place, bf16[64,1536]{1,0:T(8,128)(2,1)S(1)} %get-tuple-element.23.activated, ...), custom_call_target="tpu_custom_call" | custom-call | flops 2000000000 | tf_op jit(solution)/shard_map/pallas_call | solution.py:229
  85.7 7.2 %collective-permute-start.9 = (bf16[24,16,128]{2,1,0:T(8,128)(2,1)S(1)}, bf16[24,16,128]{2,1,0:T(8,128)(2,1)S(1)}, u32[]{:S(2)}, u32[]{:S(2)}) collective-permute-start(bf16[24,16,128]{2,1,0:T(8,128)(2,1)S(1)} %get-tuple-element.27), channel_id=1, source_target_pairs={{0,12},{4,0},{8,4},{12,8},{1,13},{5,1},{9,5},{13,9},{2,14},{6,2},{... | collective-permute-start | bytes 294920 | tf_op jit(solution)/shard_map/ppermute | solution.py:245
  92.9 7.0 %collective-permute-start.10 = (bf16[24,16,128]{2,1,0:T(8,128)(2,1)S(1)}, bf16[24,16,128]{2,1,0:T(8,128)(2,1)S(1)}, u32[]{:S(2)}, u32[]{:S(2)}) collective-permute-start(bf16[24,16,128]{2,1,0:T(8,128)(2,1)S(1)} %get-tuple-element.28), channel_id=1, source_target_pairs={{0,8},{4,12},{8,0},{12,4},{1,9},{5,13},{9,1},{13,5},{2,10},{6,14},... | collective-permute-start | bytes 294920 | tf_op jit(solution)/shard_map/ppermute | solution.py:245
  99.9 7.0 %collective-permute-start.11 = (bf16[24,16,128]{2,1,0:T(8,128)(2,1)S(1)}, bf16[24,16,128]{2,1,0:T(8,128)(2,1)S(1)}, u32[]{:S(2)}, u32[]{:S(2)}) collective-permute-start(bf16[24,16,128]{2,1,0:T(8,128)(2,1)S(1)} %get-tuple-element.29), channel_id=1, source_target_pairs={{0,4},{4,8},{8,12},{12,0},{1,5},{5,9},{9,13},{13,1},{2,6},{6,10},{... | collective-permute-start | bytes 294920 | tf_op jit(solution)/shard_map/ppermute | solution.py:245
  106.9 0.7 broadcast_in_dim.15
  107.6 5.4 %all-to-all-start.2 = ((f32[32,1,8,128]{3,2,1,0:T(8,128)}), f32[32,1,8,128]{3,2,1,0:T(8,128)S(1)}, u32[]{:S(2)}, u32[]{:S(2)}) async-start(f32[32,1,8,128]{3,2,1,0:T(8,128)} %broadcast_in_dim.15), calls=%async_computation.2 | async-start | bytes 262144 | tf_op jit(solution)/shard_map/all_to_all | solution.py:300
  113.0 1.8 %shard_map.62 = (bf16[8,2,48,128]{3,2,1,0:T(8,128)(2,1)}, bf16[8,2,48,128]{3,2,1,0:T(8,128)(2,1)}) custom-call(s32[2]{0:T(128)S(1)} %pad_add_fusion.place, bf16[24,16,128]{2,1,0:T(8,128)(2,1)S(1)} %get-tuple-element.26.refs_0_, bf16[24,16,128]{2,1,0:T(8,128)(2,1)S(1)} %collective-permute-done.9.refs_1_, ...), custom_call_target="tpu_custom_call" | custom-call | flops 1000000000 | tf_op jit(solution)/shard_map/pallas_call | solution.py:229
  114.8 5.8 %all-to-all-done.2 = f32[32,1,8,128]{3,2,1,0:T(8,128)S(1)} async-done(((f32[32,1,8,128]{3,2,1,0:T(8,128)}), f32[32,1,8,128]{3,2,1,0:T(8,128)S(1)}, u32[]{:S(2)}, u32[]{:S(2)}) %all-to-all-start.2) | async-done | bytes 131104 | tf_op jit(solution)/shard_map/all_to_all | solution.py:300
  120.6 0.1 reshape.46
  120.8 0.2 reshape.44
  121.0 0.8 pad_maximum_fusion
  (24 shorter events, 0.2 us)
Async XLA Ops:
  0.7 0.9 copy-start.1
  1.6 0.9 copy-start.2
  3.7 30.2 %collective-permute-start.2 = (bf16[30,16,128]{2,1,0:T(8,128)(2,1)S(1)}, bf16[30,16,128]{2,1,0:T(8,128)(2,1)S(1)}, u32[]{:S(2)}, u32[]{:S(2)}) collective-permute-start(bf16[30,16,128]{2,1,0:T(8,128)(2,1)S(1)} %get-tuple-element.19), channel_id=1, source_target_pairs={{0,8},{4,12},{8,0},{12,4},{1,9},{5,13},{9,1},{13,5},{2,10},{6,14},... | collective-permute-start | bytes 368648 | tf_op jit(solution)/shard_map/ppermute | solution.py:245
  20.0 14.0 %collective-permute-start.3 = (bf16[30,16,128]{2,1,0:T(8,128)(2,1)S(1)}, bf16[30,16,128]{2,1,0:T(8,128)(2,1)S(1)}, u32[]{:S(2)}, u32[]{:S(2)}) collective-permute-start(bf16[30,16,128]{2,1,0:T(8,128)(2,1)S(1)} %get-tuple-element.20), channel_id=1, source_target_pairs={{0,4},{4,8},{8,12},{12,0},{1,5},{5,9},{9,13},{13,1},{2,6},{6,10},{... | collective-permute-start | bytes 368648 | tf_op jit(solution)/shard_map/ppermute | solution.py:245
  24.0 17.8 %collective-permute-start.6 = (bf16[30,16,128]{2,1,0:T(8,128)(2,1)S(1)}, bf16[30,16,128]{2,1,0:T(8,128)(2,1)S(1)}, u32[]{:S(2)}, u32[]{:S(2)}) collective-permute-start(bf16[30,16,128]{2,1,0:T(8,128)(2,1)S(1)} %get-tuple-element.21), channel_id=1, source_target_pairs={{0,12},{4,0},{8,4},{12,8},{1,13},{5,1},{9,5},{13,9},{2,14},{6,2},{... | collective-permute-start | bytes 368648 | tf_op jit(solution)/shard_map/ppermute | solution.py:245
  29.2 19.3 %copy-start = (bf16[32,27,32]{2,0,1:T(8,128)(2,1)S(1)}, bf16[32,27,32]{2,0,1:T(8,128)(2,1)}, u32[]{:S(2)}) copy-start(bf16[32,27,32]{2,0,1:T(8,128)(2,1)} %param.5) | copy-start | bytes 165892
  29.2 17.3 %collective-permute-start.1 = (bf16[30,16,128]{2,1,0:T(8,128)(2,1)S(1)}, bf16[30,16,128]{2,1,0:T(8,128)(2,1)S(1)}, u32[]{:S(2)}, u32[]{:S(2)}) collective-permute-start(bf16[30,16,128]{2,1,0:T(8,128)(2,1)S(1)} %get-tuple-element.18.refs_0_), channel_id=1, source_target_pairs={{16,32},{48,64},{80,96},{112,128},{144,160},{176,192},{208,224},{2... | collective-permute-start | bytes 368648 | tf_op jit(solution)/shard_map/ppermute | solution.py:260
  34.0 15.8 %collective-permute-start.5 = (bf16[60,16,128]{2,1,0:T(8,128)(2,1)S(1)}, bf16[60,16,128]{2,1,0:T(8,128)(2,1)S(1)}, u32[]{:S(2)}, u32[]{:S(2)}) collective-permute-start(bf16[60,16,128]{2,1,0:T(8,128)(2,1)S(1)} %constant_dynamic-update-slice_fusion.refs_3_), channel_id=1, source_target_pairs={{16,32},{48,64},{80,96},{112,128},{144,160},{176,192},{208,224},{2... | collective-permute-start | bytes 737288 | tf_op jit(solution)/shard_map/ppermute | solution.py:260
  36.2 13.6 %collective-permute-start.4 = (bf16[60,16,128]{2,1,0:T(8,128)(2,1)S(1)}, bf16[60,16,128]{2,1,0:T(8,128)(2,1)S(1)}, u32[]{:S(2)}, u32[]{:S(2)}) collective-permute-start(bf16[60,16,128]{2,1,0:T(8,128)(2,1)S(1)} %constant_dynamic-update-slice_fusion.refs_3_), channel_id=1, source_target_pairs={{0,16},{16,0},{1,17},{17,1},{2,18},{18,2},{3,19},{19,3},{4,20},{20... | collective-permute-start | bytes 737288 | tf_op jit(solution)/shard_map/ppermute | solution.py:259
  38.1 11.0 %collective-permute-start = (bf16[30,16,128]{2,1,0:T(8,128)(2,1)S(1)}, bf16[30,16,128]{2,1,0:T(8,128)(2,1)S(1)}, u32[]{:S(2)}, u32[]{:S(2)}) collective-permute-start(bf16[30,16,128]{2,1,0:T(8,128)(2,1)S(1)} %get-tuple-element.18.refs_0_), channel_id=1, source_target_pairs={{0,16},{16,0},{1,17},{17,1},{2,18},{18,2},{3,19},{19,3},{4,20},{20... | collective-permute-start | bytes 368648 | tf_op jit(solution)/shard_map/ppermute | solution.py:259
  41.8 7.3 %collective-permute-start.8 = (bf16[30,16,128]{2,1,0:T(8,128)(2,1)S(1)}, bf16[30,16,128]{2,1,0:T(8,128)(2,1)S(1)}, u32[]{:S(2)}, u32[]{:S(2)}) collective-permute-start(bf16[30,16,128]{2,1,0:T(8,128)(2,1)S(1)} %collective-permute-done.6.refs_6_), channel_id=1, source_target_pairs={{16,32},{48,64},{80,96},{112,128},{144,160},{176,192},{208,224},{2... | collective-permute-start | bytes 368648 | tf_op jit(solution)/shard_map/ppermute | solution.py:260
  46.6 3.2 %collective-permute-start.7 = (bf16[30,16,128]{2,1,0:T(8,128)(2,1)S(1)}, bf16[30,16,128]{2,1,0:T(8,128)(2,1)S(1)}, u32[]{:S(2)}, u32[]{:S(2)}) collective-permute-start(bf16[30,16,128]{2,1,0:T(8,128)(2,1)S(1)} %collective-permute-done.6.refs_6_), channel_id=1, source_target_pairs={{0,16},{16,0},{1,17},{17,1},{2,18},{18,2},{3,19},{19,3},{4,20},{20... | collective-permute-start | bytes 368648 | tf_op jit(solution)/shard_map/ppermute | solution.py:259
  71.1 35.8 %all-to-all-start.1 = ((f32[16,1,8,128]{3,2,1,0:T(8,128)}), f32[16,1,8,128]{3,2,1,0:T(8,128)S(1)}, u32[]{:S(2)}, u32[]{:S(2)}) async-start(f32[16,1,8,128]{3,2,1,0:T(8,128)} %broadcast_in_dim.14), calls=%async_computation.1 | async-start | bytes 131072 | tf_op jit(solution)/shard_map/all_to_all | solution.py:297
  85.7 27.4 %collective-permute-start.9 = (bf16[24,16,128]{2,1,0:T(8,128)(2,1)S(1)}, bf16[24,16,128]{2,1,0:T(8,128)(2,1)S(1)}, u32[]{:S(2)}, u32[]{:S(2)}) collective-permute-start(bf16[24,16,128]{2,1,0:T(8,128)(2,1)S(1)} %get-tuple-element.27), channel_id=1, source_target_pairs={{0,12},{4,0},{8,4},{12,8},{1,13},{5,1},{9,5},{13,9},{2,14},{6,2},{... | collective-permute-start | bytes 294920 | tf_op jit(solution)/shard_map/ppermute | solution.py:245
  92.9 20.2 %collective-permute-start.10 = (bf16[24,16,128]{2,1,0:T(8,128)(2,1)S(1)}, bf16[24,16,128]{2,1,0:T(8,128)(2,1)S(1)}, u32[]{:S(2)}, u32[]{:S(2)}) collective-permute-start(bf16[24,16,128]{2,1,0:T(8,128)(2,1)S(1)} %get-tuple-element.28), channel_id=1, source_target_pairs={{0,8},{4,12},{8,0},{12,4},{1,9},{5,13},{9,1},{13,5},{2,10},{6,14},... | collective-permute-start | bytes 294920 | tf_op jit(solution)/shard_map/ppermute | solution.py:245
  99.9 13.2 %collective-permute-start.11 = (bf16[24,16,128]{2,1,0:T(8,128)(2,1)S(1)}, bf16[24,16,128]{2,1,0:T(8,128)(2,1)S(1)}, u32[]{:S(2)}, u32[]{:S(2)}) collective-permute-start(bf16[24,16,128]{2,1,0:T(8,128)(2,1)S(1)} %get-tuple-element.29), channel_id=1, source_target_pairs={{0,4},{4,8},{8,12},{12,0},{1,5},{5,9},{9,13},{13,1},{2,6},{6,10},{... | collective-permute-start | bytes 294920 | tf_op jit(solution)/shard_map/ppermute | solution.py:245
  107.6 13.1 %all-to-all-start.2 = ((f32[32,1,8,128]{3,2,1,0:T(8,128)}), f32[32,1,8,128]{3,2,1,0:T(8,128)S(1)}, u32[]{:S(2)}, u32[]{:S(2)}) async-start(f32[32,1,8,128]{3,2,1,0:T(8,128)} %broadcast_in_dim.15), calls=%async_computation.2 | async-start | bytes 262144 | tf_op jit(solution)/shard_map/all_to_all | solution.py:300

commit v3 on v2

--- a/solution.py
+++ b/solution.py
@@ -53,27 +53,34 @@
     both = jnp.concatenate([crops[...].reshape(768, LANES), cotangent[...].reshape(768, LANES)], axis=1)
     for move, out in zip(moves, outs):
         moved = dot(move, both).astype(BF16).reshape(16, 16, 2 * LANES)
-        out[0:16] = moved[:, :, :LANES]
-        out[16:30] = moved[1:15, :, LANES:]
+        out[0:14] = moved[1:15, :, :LANES]
+        out[14:26] = moved[2:14, :, LANES:]
 
 
 def unpack_kernel(place, *refs):
     parts, (activated, input_grad) = refs[:4], refs[4:]
-    rows = [
-        jnp.concatenate([part[which * 12 : which * 12 + 12].reshape(192, LANES) for part in parts], axis=0)
-        for which in range(2)
-    ]
-    both = jnp.concatenate(rows, axis=1)
     outer = iota((16, 48, LANES), 0)
     y = iota((16, 48, LANES), 1)
     part = (y >= 12).astype(jnp.int32) + (y >= 24).astype(jnp.int32) + (y >= 36).astype(jnp.int32)
+    row = y - 12 * part
+    inner = (outer & 1) * 8 + (outer >> 1)
     step = (part + 4 - place[0]) & 3
-    source = (step * 192 + (y - 12 * part) * 16 + (outer & 1) * 8 + (outer >> 1)).reshape(768, LANES)
     lane = iota((768, LANES), 1)
-    move = jnp.concatenate([one_hot(source == lane + k * LANES).astype(BF16) for k in range(6)], axis=1)
-    moved = dot(move, both).astype(BF16)
-    activated[...] = moved[:, :LANES].reshape(8, 2, 48, LANES)
-    input_grad[...] = moved[:, LANES:].reshape(8, 2, 48, LANES)
+
+    def gather(source, tiles):
+        move = [one_hot(functools.reduce(jnp.logical_or, [at == lane + k * LANES for at in source])) for k in range(tiles)]
+        return jnp.concatenate(move, axis=1).astype(BF16)
+
+    rows = jnp.concatenate([part[0:12].reshape(192, LANES) for part in parts], axis=0)
+    source = (step * 192 + row * 16 + inner).reshape(768, LANES)
+    activated[...] = dot(gather([source], 6), rows).astype(BF16).reshape(8, 2, 48, LANES)
+
+    rows = jnp.concatenate([part[12:26].reshape(224, LANES) for part in parts], axis=0)
+    source = (step * 224 + (row + 1) * 16 + inner).reshape(768, LANES)
+    other = jnp.where(row == 0, ((step + 3) & 3) * 224 + 13 * 16, ((step + 1) & 3) * 224) + inner
+    border = ((row == 0) & (part > 0)) | ((row == 11) & (part < 3))
+    other = jnp.where(border, other, -1).reshape(768, LANES)
+    input_grad[...] = dot(gather([source, other], 7), rows).astype(BF16).reshape(8, 2, 48, LANES)
 
 
 def band_kernel(by_out, by_in, forward, backward):
@@ -123,11 +130,11 @@
     for s in range(4):
         group = (member + s) & 3
         mine, near, far = parts[(0, 6, 3, 3)[s] :][:3]
-        base = 30 if s == 3 else 0
+        base = 26 if s == 3 else 0
         near_row = pl.multiple_of((1 - core) * 128 + group * 16, 16)
         far_row = pl.multiple_of(core * 128 + group * 16, 16)
         own_row = pl.multiple_of(64 + group * 16, 16)
-        for row in range(16):
+        for row in range(14):
             here = slice(row * LANES, (row + 1) * LANES)
             field[pl.ds(near_row, 16), here] = near[base + row]
             field[pl.ds(own_row, 16), here] = mine[base + row]
@@ -135,34 +142,33 @@
         cot_row = pl.multiple_of(group * 16, 16)
         near_cot = pl.multiple_of(64 + (1 - core) * 32 + group * 8, 8)
         far_cot = pl.multiple_of(64 + core * 32 + group * 8, 8)
-        for row in range(14):
+        for row in range(12):
             here = slice(row * LANES, (row + 1) * LANES)
-            cots[pl.ds(cot_row, 16), here] = mine[base + 16 + row].astype(F32)
-            wide_near = near[base + 16 + row].astype(F32)
-            wide_far = far[base + 16 + row].astype(F32)
+            cots[pl.ds(cot_row, 16), here] = mine[base + 14 + row].astype(F32)
+            wide_near = near[base + 14 + row].astype(F32)
+            wide_far = far[base + 14 + row].astype(F32)
             cots[pl.ds(near_cot, 8), here] = jnp.where(core == 0, wide_near[0:8], wide_near[8:16])
             cots[pl.ds(far_cot, 8), here] = jnp.where(core == 0, wide_far[8:16], wide_far[0:8])
 
-    for pair in range(7):
+    upper[:, 0 : 2 * LANES] = jnp.zeros((128, 2 * LANES), BF16)
+    upper[:, 14 * LANES : 16 * LANES] = jnp.zeros((128, 2 * LANES), BF16)
+    for pair in range(6):
         low = pair * 2
         total = sum(dot(forward[b], field[:, (low + b) * LANES : (low + b + 2) * LANES]) for b in range(3))
         for side in range(2):
             row = low + side
+            here = slice(row * LANES, (row + 1) * LANES)
             cut = total[:, side * LANES : (side + 1) * LANES]
             pre = cut[128:256] + shifted(cut[0:128], 1) + shifted(cut[256:384], -1)
             power = jnp.exp(jnp.minimum(pre, 0.0))
-            if 1 <= row <= 12:
-                result = jnp.where(pre[:64] > 0, pre[:64], power[:64] - 1.0).astype(BF16)
-                activated[:, (row - 1) * LANES : row * LANES] = result
-            cot = cots[:, row * LANES : (row + 1) * LANES]
+            activated[:, here] = jnp.where(pre[:64] > 0, pre[:64], power[:64] - 1.0).astype(BF16)
+            cot = cots[:, here]
             up = jnp.where(pre > 0, cot, cot * power).astype(BF16)
-            upper[:, row * LANES : (row + 1) * LANES] = up
-            if 1 <= row <= 12:
-                here = slice((row - 1) * LANES, row * LANES)
-                wide_up = up[:64].astype(F32)
-                sides[0:64, here] = shifted(wide_up, -1).astype(BF16)
-                sides[64:128, here] = up[:64]
-                sides[128:192, here] = shifted(wide_up, 1).astype(BF16)
+            upper[:, (row + 2) * LANES : (row + 3) * LANES] = up
+            wide_up = up[:64].astype(F32)
+            sides[0:64, here] = shifted(wide_up, -1).astype(BF16)
+            sides[64:128, here] = up[:64]
+            sides[128:192, here] = shifted(wide_up, 1).astype(BF16)
 
     row = iota((192, 256), 0)
     col = iota((192, 256), 1)
@@ -177,7 +183,7 @@
     for b in range(3):
         product = lax.dot_general(
             sides[...],
-            field[:, (1 + b) * LANES : (13 + b) * LANES],
+            field[:, b * LANES : (12 + b) * LANES],
             (((1,), (1,)), ((), ())),
             preferred_element_type=F32,
         ).reshape(12, 2, 8, 192)
@@ -203,7 +209,7 @@
 def backward_kernel(place, activated, upper, backward, *refs):
     backs, results = refs[:4], refs[4]
     member = place[0]
-    for pair in range(6):
+    for pair in range(7):
         low = pair * 2
         total = sum(dot(backward[b], upper[:, (low + b) * LANES : (low + b + 2) * LANES]) for b in range(3))
         for side in range(2):
@@ -212,10 +218,11 @@
             results[:, (low + side) * LANES : (low + side + 1) * LANES] = grad.astype(BF16)
 
     for step, back in enumerate(backs):
-        for which, source in enumerate((activated, results)):
-            low = pl.multiple_of(((member + step) & 3) * 16, 16)
-            for row in range(12):
-                back[which * 12 + row] = source[pl.ds(low, 16), row * LANES : (row + 1) * LANES]
+        low = pl.multiple_of(((member + step) & 3) * 16, 16)
+        for row in range(12):
+            back[row] = activated[pl.ds(low, 16), row * LANES : (row + 1) * LANES]
+        for row in range(14):
+            back[12 + row] = results[pl.ds(low, 16), row * LANES : (row + 1) * LANES]
 
 
 def call(kernel, outs, scratch=(), place=False, flops=0, moved=0):
@@ -248,7 +255,7 @@
 
 def body(crops, cotangent, weights):
     place = jnp.stack([lax.axis_index("chan"), lax.axis_index("core")]).astype(jnp.int32)
-    piece = jax.ShapeDtypeStruct((30, 16, LANES), BF16)
+    piece = jax.ShapeDtypeStruct((26, 16, LANES), BF16)
     packed = call(pack_kernel, (piece,) * 4, place=True, flops=10**9)(place, crops[0], cotangent[0])
     got = reshard(packed)
     chips = lax.axis_size("zlo") * lax.axis_size("y")
@@ -269,35 +276,35 @@
     rows = jax.ShapeDtypeStruct((64, 12 * LANES), BF16)
     activated, upper, grads = call(
         forward_kernel,
-        (rows, jax.ShapeDtypeStruct((128, 14 * LANES), BF16), jax.ShapeDtypeStruct((32, 8, LANES), F32)),
+        (rows, jax.ShapeDtypeStruct((128, 16 * LANES), BF16), jax.ShapeDtypeStruct((32, 8, LANES), F32)),
         [
-            pltpu.VMEM((192, 16 * LANES), BF16),
-            pltpu.VMEM((128, 14 * LANES), F32),
+            pltpu.VMEM((192, 14 * LANES), BF16),
+            pltpu.VMEM((128, 12 * LANES), F32),
             pltpu.VMEM((192, 12 * LANES), BF16),
         ],
         place=True,
         flops=3 * 10**9,
     )(place, *parts, forward)
-    piece = jax.ShapeDtypeStruct((24, 16, LANES), BF16)
+    piece = jax.ShapeDtypeStruct((26, 16, LANES), BF16)
     backs = call(
         backward_kernel,
         (piece,) * 4,
-        [pltpu.VMEM((64, 12 * LANES), BF16)],
+        [pltpu.VMEM((64, 14 * LANES), BF16)],
         place=True,
         flops=2 * 10**9,
     )(place, activated, upper, backward)
-    slab = jax.ShapeDtypeStruct((8, 2, 48, LANES), BF16)
-    activated, input_grad = call(unpack_kernel, (slab, slab), place=True, flops=10**9)(place, *reshard(backs))
-
     plane = ("y", "core", "batch")
     column = ("zlo", "chan")
     pieces, rest = lax.axis_size(plane), lax.axis_size(column)
     terms = lax.all_to_all(grads.reshape((pieces, -1) + grads.shape[1:]), plane, 0, 0)
+    terms, backs = lax.optimization_barrier((terms, backs))
     share = jnp.sum(terms, axis=0)
     terms = lax.all_to_all(jnp.broadcast_to(share, (rest,) + share.shape), column, 0, 0)
     cells = pieces * rest // lax.axis_size("chan") * crops.shape[2] * crops.shape[3] * crops.shape[4]
     share = jnp.sum(terms, axis=0) / jnp.sqrt(jnp.float32(cells))
     whole = lax.all_to_all(jnp.broadcast_to(share, (pieces,) + share.shape), plane, 0, 0).reshape(32, 8, LANES)
+    slab = jax.ShapeDtypeStruct((8, 2, 48, LANES), BF16)
+    activated, input_grad = call(unpack_kernel, (slab, slab), place=True, flops=10**9)(place, *reshard(backs))
     eight = whole[:24].reshape(3, 2, 4, 8, 4, 32).transpose(2, 3, 1, 4, 0, 5).reshape(32, 8, 3, 32)
     ninth = whole[24:28].reshape(32, 1, 4, 32)[:, :, :3]
     weight_grad = jnp.concatenate([eight, ninth], axis=1).reshape(32, 27, 32)

time: 122 us -> 119 us (0.975)
  blocking collectives: 17.1 us -> 0 us
  starting transfers between devices: 83.2 us -> 91.3 us
  waiting for transfers between devices: 7.83 us -> 12.4 us
    all_to_all x1 -> x0, blocking collectives: 17.1 us -> none  [body(): lax.all_to_all(grads.reshape((pieces, -1) + grads.shape[1:]), plane, 0, 0)]
    all_to_all x0 -> x1, starting transfers between devices: none -> 11.1 us  [body(): lax.all_to_all(grads.reshape((pieces, -1) + grads.shape[1:]), plane, 0, 0)]
    all_to_all x0 -> x1, waiting for transfers between devices: none -> 6.27 us  [body(): lax.all_to_all(grads.reshape((pieces, -1) + grads.shape[1:]), plane, 0, 0)]
    all_to_all x1, starting transfers between devices: 13.3 us -> 11.6 us  [body(): lax.all_to_all(jnp.broadcast_to(share, (rest,) + share.shape), column, 0, 0)]
    ppermute x3, starting transfers between devices: 11.6 us -> 10.2 us  [body(): far = lax.ppermute(mine, ('zlo', 'y', 'core'), remote)]
    ppermute x6, waiting for transfers between devices: 1.3 us -> 0.02 us  [reshard(): lax.ppermute(parts[step], 'chan', [(i, (i + step) % 4) for i in range(4)])]
  transfers between devices with their start and end apart: 14 -> 15, of which waited for: 3 -> 3; matrix products, arithmetic and copies ran while one was open for 1% -> 1% of each run, Pallas kernels for 3% -> 3%
where the time goes in v3:
time: 119 us; the launch traced here: 118 us
  starting transfers between devices  91.3 us (77%)
  waiting for transfers between devices  12.4 us (10%)
  Pallas kernels  8.88 us (7%)
  local copies, waits for them, and re-layouts  3.7 us (3%)
    ppermute x6, starting transfers between devices, reshard(): lax.ppermute(parts[step], 'chan', [(i, (i + step) % 4) for i in range(4)])  46.8 us
    all_to_all x1, starting transfers between devices, body(): lax.all_to_all(jnp.broadcast_to(share, (rest,) + share.shape), column, 0, 0)  11.6 us
    all_to_all x1, starting transfers between devices, body(): lax.all_to_all(grads.reshape((pieces, -1) + grads.shape[1:]), plane, 0, 0)  11.1 us
    ppermute x3, starting transfers between devices, body(): far = lax.ppermute(mine, ('zlo', 'y', 'core'), remote)  10.2 us
    pallas_call x5, Pallas kernels, run(): pl.pallas_call(kernel, out_shape=outs, in_specs=specs, out_specs=jax.tree...  8.88 us
    all_to_all x1, waiting for transfers between devices, body(): lax.all_to_all(grads.reshape((pieces, -1) + grads.shape[1:]), plane, 0, 0)  6.27 us
    ppermute x3, starting transfers between devices, body(): near = lax.ppermute(mine, 'core', [(0, 1), (1, 0)])  6.25 us
    all_to_all x1, waiting for transfers between devices, body(): lax.all_to_all(jnp.broadcast_to(share, (pieces,) + share.shape), plane, 0...  5.48 us
  transfers between devices with their start and end apart: 15, of which 3 were waited for; matrix products, arithmetic and copies ran while one was open for 1% of the time, Pallas kernels for 3%

profile of v3, /device:TPU:1, one launch (start us, length us, event | category | flops | bytes accessed | tf_op | source)
XLA Modules:
  0.0 118.2 jit_solution(3579877486238029957)
XLA Ops:
  0.6 0.1 pad_add_fusion.place
  0.7 0.9 copy-done.1
  1.6 0.9 copy-done.2
  2.6 1.1 shard_map.58
  3.7 16.4 %collective-permute-start.2 = (bf16[26,16,128]{2,1,0:T(8,128)(2,1)S(1)}, bf16[26,16,128]{2,1,0:T(8,128)(2,1)S(1)}, u32[]{:S(2)}, u32[]{:S(2)}) collective-permute-start(bf16[26,16,128]{2,1,0:T(8,128)(2,1)S(1)} %get-tuple-element.24), channel_id=1, source_target_pairs={{0,8},{4,12},{8,0},{12,4},{1,9},{5,13},{9,1},{13,5},{2,10},{6,14},... | collective-permute-start | bytes 319496 | tf_op jit(solution)/shard_map/ppermute | solution.py:252
  20.1 4.0 %collective-permute-start.3 = (bf16[26,16,128]{2,1,0:T(8,128)(2,1)S(1)}, bf16[26,16,128]{2,1,0:T(8,128)(2,1)S(1)}, u32[]{:S(2)}, u32[]{:S(2)}) collective-permute-start(bf16[26,16,128]{2,1,0:T(8,128)(2,1)S(1)} %get-tuple-element.25), channel_id=1, source_target_pairs={{0,4},{4,8},{8,12},{12,0},{1,5},{5,9},{9,13},{13,1},{2,6},{6,10},{... | collective-permute-start | bytes 319496 | tf_op jit(solution)/shard_map/ppermute | solution.py:252
  24.2 5.2 %collective-permute-start.6 = (bf16[26,16,128]{2,1,0:T(8,128)(2,1)S(1)}, bf16[26,16,128]{2,1,0:T(8,128)(2,1)S(1)}, u32[]{:S(2)}, u32[]{:S(2)}) collective-permute-start(bf16[26,16,128]{2,1,0:T(8,128)(2,1)S(1)} %get-tuple-element.26), channel_id=1, source_target_pairs={{0,12},{4,0},{8,4},{12,8},{1,13},{5,1},{9,5},{13,9},{2,14},{6,2},{... | collective-permute-start | bytes 319496 | tf_op jit(solution)/shard_map/ppermute | solution.py:252
  29.4 4.6 %collective-permute-start.1 = (bf16[26,16,128]{2,1,0:T(8,128)(2,1)S(1)}, bf16[26,16,128]{2,1,0:T(8,128)(2,1)S(1)}, u32[]{:S(2)}, u32[]{:S(2)}) collective-permute-start(bf16[26,16,128]{2,1,0:T(8,128)(2,1)S(1)} %get-tuple-element.23.refs_0_), channel_id=1, source_target_pairs={{16,32},{48,64},{80,96},{112,128},{144,160},{176,192},{208,224},{2... | collective-permute-start | bytes 319496 | tf_op jit(solution)/shard_map/ppermute | solution.py:267
  34.0 1.9 %collective-permute-start.5 = (bf16[52,16,128]{2,1,0:T(8,128)(2,1)S(1)}, bf16[52,16,128]{2,1,0:T(8,128)(2,1)S(1)}, u32[]{:S(2)}, u32[]{:S(2)}) collective-permute-start(bf16[52,16,128]{2,1,0:T(8,128)(2,1)S(1)} %constant_dynamic-update-slice_fusion.refs_3_), channel_id=1, source_target_pairs={{16,32},{48,64},{80,96},{112,128},{144,160},{176,192},{208,224},{2... | collective-permute-start | bytes 638984 | tf_op jit(solution)/shard_map/ppermute | solution.py:267
  36.0 1.9 %collective-permute-start.4 = (bf16[52,16,128]{2,1,0:T(8,128)(2,1)S(1)}, bf16[52,16,128]{2,1,0:T(8,128)(2,1)S(1)}, u32[]{:S(2)}, u32[]{:S(2)}) collective-permute-start(bf16[52,16,128]{2,1,0:T(8,128)(2,1)S(1)} %constant_dynamic-update-slice_fusion.refs_3_), channel_id=1, source_target_pairs={{0,16},{16,0},{1,17},{17,1},{2,18},{18,2},{3,19},{19,3},{4,20},{20... | collective-permute-start | bytes 638984 | tf_op jit(solution)/shard_map/ppermute | solution.py:266
  37.9 2.4 %collective-permute-start = (bf16[26,16,128]{2,1,0:T(8,128)(2,1)S(1)}, bf16[26,16,128]{2,1,0:T(8,128)(2,1)S(1)}, u32[]{:S(2)}, u32[]{:S(2)}) collective-permute-start(bf16[26,16,128]{2,1,0:T(8,128)(2,1)S(1)} %get-tuple-element.23.refs_0_), channel_id=1, source_target_pairs={{0,16},{16,0},{1,17},{17,1},{2,18},{18,2},{3,19},{19,3},{4,20},{20... | collective-permute-start | bytes 319496 | tf_op jit(solution)/shard_map/ppermute | solution.py:266
  40.3 3.6 %collective-permute-start.8 = (bf16[26,16,128]{2,1,0:T(8,128)(2,1)S(1)}, bf16[26,16,128]{2,1,0:T(8,128)(2,1)S(1)}, u32[]{:S(2)}, u32[]{:S(2)}) collective-permute-start(bf16[26,16,128]{2,1,0:T(8,128)(2,1)S(1)} %collective-permute-done.6.refs_6_), channel_id=1, source_target_pairs={{16,32},{48,64},{80,96},{112,128},{144,160},{176,192},{208,224},{2... | collective-permute-start | bytes 319496 | tf_op jit(solution)/shard_map/ppermute | solution.py:267
  44.0 1.9 %collective-permute-start.7 = (bf16[26,16,128]{2,1,0:T(8,128)(2,1)S(1)}, bf16[26,16,128]{2,1,0:T(8,128)(2,1)S(1)}, u32[]{:S(2)}, u32[]{:S(2)}) collective-permute-start(bf16[26,16,128]{2,1,0:T(8,128)(2,1)S(1)} %collective-permute-done.6.refs_6_), channel_id=1, source_target_pairs={{0,16},{16,0},{1,17},{17,1},{2,18},{18,2},{3,19},{19,3},{4,20},{20... | collective-permute-start | bytes 319496 | tf_op jit(solution)/shard_map/ppermute | solution.py:266
  45.9 0.2 copy.16
  46.1 0.4 shard_map.59
  46.5 0.7 collective-permute-done.7.refs_7_
  47.2 3.9 %shard_map.60 = (bf16[64,1536]{1,0:T(8,128)(2,1)S(1)}, bf16[128,2048]{1,0:T(8,128)(2,1)S(1)}, f32[32,8,128]{2,1,0:T(8,128)}) custom-call(s32[2]{0:T(128)S(1)} %pad_add_fusion.place, bf16[26,16,128]{2,1,0:T(8,128)(2,1)S(1)} %get-tuple-element.23.refs_0_, bf16[26,16,128]{2,1,0:T(8,128)(2,1)S(1)} %collective-permute-done.refs_1_, ...), custom_call_target="tpu_custom_call" | custom-call | flops 3000000000 | tf_op jit(solution)/shard_map/pallas_call | solution.py:236
  51.1 11.1 %all-to-all-start = ((f32[32,1,8,128]{3,2,1,0:T(8,128)}), f32[32,1,8,128]{3,2,1,0:T(8,128)S(1)}, u32[]{:S(2)}, u32[]{:S(2)}) async-start(f32[32,1,8,128]{3,2,1,0:T(8,128)} %bitcast.9), calls=%async_computation | async-start | bytes 262144 | tf_op jit(solution)/shard_map/all_to_all | solution.py:299
  62.1 1.3 %shard_map.61 = (bf16[26,16,128]{2,1,0:T(8,128)(2,1)S(1)}, bf16[26,16,128]{2,1,0:T(8,128)(2,1)S(1)}, bf16[26,16,128]{2,1,0:T(8,128)(2,1)S(1)}, bf16[26,16,128]{2,1,0:T(8,128)(2,1)S(1)}) custom-call(s32[2]{0:T(128)S(1)} %pad_add_fusion.place, bf16[64,1536]{1,0:T(8,128)(2,1)S(1)} %get-tuple-element.29.activated, ...), custom_call_target="tpu_custom_call" | custom-call | flops 2000000000 | tf_op jit(solution)/shard_map/pallas_call | solution.py:236
  63.5 6.3 %all-to-all-done = f32[32,1,8,128]{3,2,1,0:T(8,128)S(1)} async-done(((f32[32,1,8,128]{3,2,1,0:T(8,128)}), f32[32,1,8,128]{3,2,1,0:T(8,128)S(1)}, u32[]{:S(2)}, u32[]{:S(2)}) %all-to-all-start) | async-done | bytes 131104 | tf_op jit(solution)/shard_map/all_to_all | solution.py:299
  69.8 0.6 broadcast_in_dim.14
  70.4 11.6 %all-to-all-start.1 = ((f32[16,1,8,128]{3,2,1,0:T(8,128)}), f32[16,1,8,128]{3,2,1,0:T(8,128)S(1)}, u32[]{:S(2)}, u32[]{:S(2)}) async-start(f32[16,1,8,128]{3,2,1,0:T(8,128)} %broadcast_in_dim.14), calls=%async_computation.1 | async-start | bytes 131072 | tf_op jit(solution)/shard_map/all_to_all | solution.py:302
  82.1 7.2 %collective-permute-start.9 = (bf16[26,16,128]{2,1,0:T(8,128)(2,1)S(1)}, bf16[26,16,128]{2,1,0:T(8,128)(2,1)S(1)}, u32[]{:S(2)}, u32[]{:S(2)}) collective-permute-start(bf16[26,16,128]{2,1,0:T(8,128)(2,1)S(1)} %get-tuple-element.37), channel_id=1, source_target_pairs={{0,12},{4,0},{8,4},{12,8},{1,13},{5,1},{9,5},{13,9},{2,14},{6,2},{... | collective-permute-start | bytes 319496 | tf_op jit(solution)/shard_map/ppermute | solution.py:252
  89.3 7.0 %collective-permute-start.10 = (bf16[26,16,128]{2,1,0:T(8,128)(2,1)S(1)}, bf16[26,16,128]{2,1,0:T(8,128)(2,1)S(1)}, u32[]{:S(2)}, u32[]{:S(2)}) collective-permute-start(bf16[26,16,128]{2,1,0:T(8,128)(2,1)S(1)} %get-tuple-element.38), channel_id=1, source_target_pairs={{0,8},{4,12},{8,0},{12,4},{1,9},{5,13},{9,1},{13,5},{2,10},{6,14},... | collective-permute-start | bytes 319496 | tf_op jit(solution)/shard_map/ppermute | solution.py:252
  96.3 7.0 %collective-permute-start.11 = (bf16[26,16,128]{2,1,0:T(8,128)(2,1)S(1)}, bf16[26,16,128]{2,1,0:T(8,128)(2,1)S(1)}, u32[]{:S(2)}, u32[]{:S(2)}) collective-permute-start(bf16[26,16,128]{2,1,0:T(8,128)(2,1)S(1)} %get-tuple-element.39), channel_id=1, source_target_pairs={{0,4},{4,8},{8,12},{12,0},{1,5},{5,9},{9,13},{13,1},{2,6},{6,10},{... | collective-permute-start | bytes 319496 | tf_op jit(solution)/shard_map/ppermute | solution.py:252
  103.3 0.7 broadcast_in_dim.15
  104.0 5.4 %all-to-all-start.2 = ((f32[32,1,8,128]{3,2,1,0:T(8,128)}), f32[32,1,8,128]{3,2,1,0:T(8,128)S(1)}, u32[]{:S(2)}, u32[]{:S(2)}) async-start(f32[32,1,8,128]{3,2,1,0:T(8,128)} %broadcast_in_dim.15), calls=%async_computation.2 | async-start | bytes 262144 | tf_op jit(solution)/shard_map/all_to_all | solution.py:305
  109.4 2.1 %shard_map.62 = (bf16[8,2,48,128]{3,2,1,0:T(8,128)(2,1)}, bf16[8,2,48,128]{3,2,1,0:T(8,128)(2,1)}) custom-call(s32[2]{0:T(128)S(1)} %pad_add_fusion.place, bf16[26,16,128]{2,1,0:T(8,128)(2,1)S(1)} %get-tuple-element.36.refs_0_, bf16[26,16,128]{2,1,0:T(8,128)(2,1)S(1)} %collective-permute-done.9.refs_1_, ...), custom_call_target="tpu_custom_call" | custom-call | flops 1000000000 | tf_op jit(solution)/shard_map/pallas_call | solution.py:236
  111.6 5.5 %all-to-all-done.2 = f32[32,1,8,128]{3,2,1,0:T(8,128)S(1)} async-done(((f32[32,1,8,128]{3,2,1,0:T(8,128)}), f32[32,1,8,128]{3,2,1,0:T(8,128)S(1)}, u32[]{:S(2)}, u32[]{:S(2)}) %all-to-all-start.2) | async-done | bytes 131104 | tf_op jit(solution)/shard_map/all_to_all | solution.py:305
  117.0 0.1 reshape.46
  117.2 0.2 reshape.44
  117.4 0.8 pad_maximum_fusion
  (25 shorter events, 0.2 us)
Async XLA Ops:
  0.7 0.9 copy-start.1
  1.6 0.9 copy-start.2
  3.7 42.2 %copy-start = (bf16[32,27,32]{2,0,1:T(8,128)(2,1)S(1)}, bf16[32,27,32]{2,0,1:T(8,128)(2,1)}, u32[]{:S(2)}) copy-start(bf16[32,27,32]{2,0,1:T(8,128)(2,1)} %param.5) | copy-start | bytes 165892
  3.7 30.2 %collective-permute-start.2 = (bf16[26,16,128]{2,1,0:T(8,128)(2,1)S(1)}, bf16[26,16,128]{2,1,0:T(8,128)(2,1)S(1)}, u32[]{:S(2)}, u32[]{:S(2)}) collective-permute-start(bf16[26,16,128]{2,1,0:T(8,128)(2,1)S(1)} %get-tuple-element.24), channel_id=1, source_target_pairs={{0,8},{4,12},{8,0},{12,4},{1,9},{5,13},{9,1},{13,5},{2,10},{6,14},... | collective-permute-start | bytes 319496 | tf_op jit(solution)/shard_map/ppermute | solution.py:252
  20.1 13.8 %collective-permute-start.3 = (bf16[26,16,128]{2,1,0:T(8,128)(2,1)S(1)}, bf16[26,16,128]{2,1,0:T(8,128)(2,1)S(1)}, u32[]{:S(2)}, u32[]{:S(2)}) collective-permute-start(bf16[26,16,128]{2,1,0:T(8,128)(2,1)S(1)} %get-tuple-element.25), channel_id=1, source_target_pairs={{0,4},{4,8},{8,12},{12,0},{1,5},{5,9},{9,13},{13,1},{2,6},{6,10},{... | collective-permute-start | bytes 319496 | tf_op jit(solution)/shard_map/ppermute | solution.py:252
  24.2 16.1 %collective-permute-start.6 = (bf16[26,16,128]{2,1,0:T(8,128)(2,1)S(1)}, bf16[26,16,128]{2,1,0:T(8,128)(2,1)S(1)}, u32[]{:S(2)}, u32[]{:S(2)}) collective-permute-start(bf16[26,16,128]{2,1,0:T(8,128)(2,1)S(1)} %get-tuple-element.26), channel_id=1, source_target_pairs={{0,12},{4,0},{8,4},{12,8},{1,13},{5,1},{9,5},{13,9},{2,14},{6,2},{... | collective-permute-start | bytes 319496 | tf_op jit(solution)/shard_map/ppermute | solution.py:252
  29.4 14.6 %collective-permute-start.1 = (bf16[26,16,128]{2,1,0:T(8,128)(2,1)S(1)}, bf16[26,16,128]{2,1,0:T(8,128)(2,1)S(1)}, u32[]{:S(2)}, u32[]{:S(2)}) collective-permute-start(bf16[26,16,128]{2,1,0:T(8,128)(2,1)S(1)} %get-tuple-element.23.refs_0_), channel_id=1, source_target_pairs={{16,32},{48,64},{80,96},{112,128},{144,160},{176,192},{208,224},{2... | collective-permute-start | bytes 319496 | tf_op jit(solution)/shard_map/ppermute | solution.py:267
  34.0 13.2 %collective-permute-start.5 = (bf16[52,16,128]{2,1,0:T(8,128)(2,1)S(1)}, bf16[52,16,128]{2,1,0:T(8,128)(2,1)S(1)}, u32[]{:S(2)}, u32[]{:S(2)}) collective-permute-start(bf16[52,16,128]{2,1,0:T(8,128)(2,1)S(1)} %constant_dynamic-update-slice_fusion.refs_3_), channel_id=1, source_target_pairs={{16,32},{48,64},{80,96},{112,128},{144,160},{176,192},{208,224},{2... | collective-permute-start | bytes 638984 | tf_op jit(solution)/shard_map/ppermute | solution.py:267
  36.0 11.2 %collective-permute-start.4 = (bf16[52,16,128]{2,1,0:T(8,128)(2,1)S(1)}, bf16[52,16,128]{2,1,0:T(8,128)(2,1)S(1)}, u32[]{:S(2)}, u32[]{:S(2)}) collective-permute-start(bf16[52,16,128]{2,1,0:T(8,128)(2,1)S(1)} %constant_dynamic-update-slice_fusion.refs_3_), channel_id=1, source_target_pairs={{0,16},{16,0},{1,17},{17,1},{2,18},{18,2},{3,19},{19,3},{4,20},{20... | collective-permute-start | bytes 638984 | tf_op jit(solution)/shard_map/ppermute | solution.py:266
  37.9 8.6 %collective-permute-start = (bf16[26,16,128]{2,1,0:T(8,128)(2,1)S(1)}, bf16[26,16,128]{2,1,0:T(8,128)(2,1)S(1)}, u32[]{:S(2)}, u32[]{:S(2)}) collective-permute-start(bf16[26,16,128]{2,1,0:T(8,128)(2,1)S(1)} %get-tuple-element.23.refs_0_), channel_id=1, source_target_pairs={{0,16},{16,0},{1,17},{17,1},{2,18},{18,2},{3,19},{19,3},{4,20},{20... | collective-permute-start | bytes 319496 | tf_op jit(solution)/shard_map/ppermute | solution.py:266
  40.3 6.2 %collective-permute-start.8 = (bf16[26,16,128]{2,1,0:T(8,128)(2,1)S(1)}, bf16[26,16,128]{2,1,0:T(8,128)(2,1)S(1)}, u32[]{:S(2)}, u32[]{:S(2)}) collective-permute-start(bf16[26,16,128]{2,1,0:T(8,128)(2,1)S(1)} %collective-permute-done.6.refs_6_), channel_id=1, source_target_pairs={{16,32},{48,64},{80,96},{112,128},{144,160},{176,192},{208,224},{2... | collective-permute-start | bytes 319496 | tf_op jit(solution)/shard_map/ppermute | solution.py:267
  44.0 3.2 %collective-permute-start.7 = (bf16[26,16,128]{2,1,0:T(8,128)(2,1)S(1)}, bf16[26,16,128]{2,1,0:T(8,128)(2,1)S(1)}, u32[]{:S(2)}, u32[]{:S(2)}) collective-permute-start(bf16[26,16,128]{2,1,0:T(8,128)(2,1)S(1)} %collective-permute-done.6.refs_6_), channel_id=1, source_target_pairs={{0,16},{16,0},{1,17},{17,1},{2,18},{18,2},{3,19},{19,3},{4,20},{20... | collective-permute-start | bytes 319496 | tf_op jit(solution)/shard_map/ppermute | solution.py:266
  51.1 18.7 %all-to-all-start = ((f32[32,1,8,128]{3,2,1,0:T(8,128)}), f32[32,1,8,128]{3,2,1,0:T(8,128)S(1)}, u32[]{:S(2)}, u32[]{:S(2)}) async-start(f32[32,1,8,128]{3,2,1,0:T(8,128)} %bitcast.9), calls=%async_computation | async-start | bytes 262144 | tf_op jit(solution)/shard_map/all_to_all | solution.py:299
  70.4 32.8 %all-to-all-start.1 = ((f32[16,1,8,128]{3,2,1,0:T(8,128)}), f32[16,1,8,128]{3,2,1,0:T(8,128)S(1)}, u32[]{:S(2)}, u32[]{:S(2)}) async-start(f32[16,1,8,128]{3,2,1,0:T(8,128)} %broadcast_in_dim.14), calls=%async_computation.1 | async-start | bytes 131072 | tf_op jit(solution)/shard_map/all_to_all | solution.py:302
  82.1 27.3 %collective-permute-start.9 = (bf16[26,16,128]{2,1,0:T(8,128)(2,1)S(1)}, bf16[26,16,128]{2,1,0:T(8,128)(2,1)S(1)}, u32[]{:S(2)}, u32[]{:S(2)}) collective-permute-start(bf16[26,16,128]{2,1,0:T(8,128)(2,1)S(1)} %get-tuple-element.37), channel_id=1, source_target_pairs={{0,12},{4,0},{8,4},{12,8},{1,13},{5,1},{9,5},{13,9},{2,14},{6,2},{... | collective-permute-start | bytes 319496 | tf_op jit(solution)/shard_map/ppermute | solution.py:252
  89.3 20.2 %collective-permute-start.10 = (bf16[26,16,128]{2,1,0:T(8,128)(2,1)S(1)}, bf16[26,16,128]{2,1,0:T(8,128)(2,1)S(1)}, u32[]{:S(2)}, u32[]{:S(2)}) collective-permute-start(bf16[26,16,128]{2,1,0:T(8,128)(2,1)S(1)} %get-tuple-element.38), channel_id=1, source_target_pairs={{0,8},{4,12},{8,0},{12,4},{1,9},{5,13},{9,1},{13,5},{2,10},{6,14},... | collective-permute-start | bytes 319496 | tf_op jit(solution)/shard_map/ppermute | solution.py:252
  96.3 13.2 %collective-permute-start.11 = (bf16[26,16,128]{2,1,0:T(8,128)(2,1)S(1)}, bf16[26,16,128]{2,1,0:T(8,128)(2,1)S(1)}, u32[]{:S(2)}, u32[]{:S(2)}) collective-permute-start(bf16[26,16,128]{2,1,0:T(8,128)(2,1)S(1)} %get-tuple-element.39), channel_id=1, source_target_pairs={{0,4},{4,8},{8,12},{12,0},{1,5},{5,9},{9,13},{13,1},{2,6},{6,10},{... | collective-permute-start | bytes 319496 | tf_op jit(solution)/shard_map/ppermute | solution.py:252
  104.0 13.1 %all-to-all-start.2 = ((f32[32,1,8,128]{3,2,1,0:T(8,128)}), f32[32,1,8,128]{3,2,1,0:T(8,128)S(1)}, u32[]{:S(2)}, u32[]{:S(2)}) async-start(f32[32,1,8,128]{3,2,1,0:T(8,128)} %broadcast_in_dim.15), calls=%async_computation.2 | async-start | bytes 262144 | tf_op jit(solution)/shard_map/all_to_all | solution.py:305

commit v4 on v3

--- a/solution.py
+++ b/solution.py
@@ -123,14 +123,14 @@
 
 
 def forward_kernel(place, *refs):
-    parts, refs = refs[:9], refs[9:]
+    parts, refs = refs[:6], refs[6:]
     forward, activated, upper, grads, field, cots, sides = refs
     member, core = place[0], place[1]
 
     for s in range(4):
         group = (member + s) & 3
-        mine, near, far = parts[(0, 6, 3, 3)[s] :][:3]
-        base = 26 if s == 3 else 0
+        mine, near, far = parts[(0, 3, 3, 3)[s] :][:3]
+        base = (0, 52, 0, 26)[s]
         near_row = pl.multiple_of((1 - core) * 128 + group * 16, 16)
         far_row = pl.multiple_of(core * 128 + group * 16, 16)
         own_row = pl.multiple_of(64 + group * 16, 16)
@@ -248,7 +248,7 @@
 
 def reshard(parts):
     got = [parts[0], None, None, None]
-    for step in (2, 1, 3):
+    for step in (1, 3, 2):
         got[4 - step] = lax.ppermute(parts[step], "chan", [(i, (i + step) % 4) for i in range(4)])
     return got
 
@@ -262,7 +262,10 @@
     remote = [(2 * i + 1, 2 * i + 2) for i in range(chips - 1)]
     remote += [(j, i) for i, j in remote]
     parts = []
-    for mine in (got[0], jnp.concatenate([got[2], got[3]], axis=0), got[1]):
+    for mine in (got[0], None):
+        if mine is None:
+            *parts, a, b, c = lax.optimization_barrier((*parts, got[2], got[3], got[1]))
+            mine = jnp.concatenate([a, b, c], axis=0)
         near = lax.ppermute(mine, "core", [(0, 1), (1, 0)])
         far = lax.ppermute(mine, ("zlo", "y", "core"), remote)
         parts += [mine, near, far]

time: 119 us -> 114 us (0.958)
  starting transfers between devices: 91.3 us -> 82.1 us
  waiting for transfers between devices: 12.4 us -> 16.5 us
    all_to_all x1, starting transfers between devices: 11.6 us -> 6.17 us  [body(): lax.all_to_all(jnp.broadcast_to(share, (rest,) + share.shape), column, 0, 0)]
    ppermute x6, waiting for transfers between devices: 0.02 us -> 2.6 us  [reshard(): lax.ppermute(parts[step], 'chan', [(i, (i + step) % 4) for i in range(4)])]
    ppermute x3 -> x2, starting transfers between devices: 6.25 us -> 3.84 us  [body(): near = lax.ppermute(mine, 'core', [(0, 1), (1, 0)])]
    ppermute x3 -> x2, waiting for transfers between devices: 0.01 us -> 2.13 us  [body(): far = lax.ppermute(mine, ('zlo', 'y', 'core'), remote)]
    ppermute x3 -> x2, starting transfers between devices: 10.2 us -> 8.93 us  [body(): far = lax.ppermute(mine, ('zlo', 'y', 'core'), remote)]
  transfers between devices with their start and end apart: 15 -> 13, of which waited for: 3 -> 4; matrix products, arithmetic and copies ran while one was open for 1% -> 1% of each run, Pallas kernels for 3% -> 3%
where the time goes in v4:
time: 114 us; the launch traced here: 113 us
  starting transfers between devices  82.1 us (72%)
  waiting for transfers between devices  16.5 us (14%)
  Pallas kernels  8.9 us (8%)
  local copies, waits for them, and re-layouts  3.72 us (3%)
    ppermute x6, starting transfers between devices, reshard(): lax.ppermute(parts[step], 'chan', [(i, (i + step) % 4) for i in range(4)])  46.6 us
    all_to_all x1, starting transfers between devices, body(): lax.all_to_all(grads.reshape((pieces, -1) + grads.shape[1:]), plane, 0, 0)  11.1 us
    ppermute x2, starting transfers between devices, body(): far = lax.ppermute(mine, ('zlo', 'y', 'core'), remote)  8.93 us
    pallas_call x5, Pallas kernels, run(): pl.pallas_call(kernel, out_shape=outs, in_specs=specs, out_specs=jax.tree...  8.9 us
    all_to_all x1, waiting for transfers between devices, body(): lax.all_to_all(grads.reshape((pieces, -1) + grads.shape[1:]), plane, 0, 0)  6.27 us
    all_to_all x1, starting transfers between devices, body(): lax.all_to_all(jnp.broadcast_to(share, (rest,) + share.shape), column, 0, 0)  6.17 us
    all_to_all x1, waiting for transfers between devices, body(): lax.all_to_all(jnp.broadcast_to(share, (pieces,) + share.shape), plane, 0...  5.48 us
    all_to_all x1, starting transfers between devices, body(): lax.all_to_all(jnp.broadcast_to(share, (pieces,) + share.shape), plane, 0...  5.43 us
  transfers between devices with their start and end apart: 13, of which 4 were waited for; matrix products, arithmetic and copies ran while one was open for 1% of the time, Pallas kernels for 3%

profile of v4, /device:TPU:1, one launch (start us, length us, event | category | flops | bytes accessed | tf_op | source)
XLA Modules:
  0.0 113.0 jit_solution(15478476632477550735)
XLA Ops:
  0.6 0.1 pad_add_fusion.place
  0.7 0.9 copy-done.1
  1.6 0.9 copy-done.2
  2.6 1.1 %shard_map.58 = (bf16[26,16,128]{2,1,0:T(8,128)(2,1)S(1)}, bf16[26,16,128]{2,1,0:T(8,128)(2,1)S(1)}, bf16[26,16,128]{2,1,0:T(8,128)(2,1)S(1)}, bf16[26,16,128]{2,1,0:T(8,128)(2,1)S(1)}) custom-call(s32[2]{0:T(128)S(1)} %pad_add_fusion.place, bf16[8,2,48,128]{3,2,1,0:T(8,128)(2,1)S(1)} %bitcast.25, bf16[8,2,48,128]{3,2,1,0:T(8,128)(2,1)S(1)} %bitcast.26), custom_call_target="tpu_custom_call" | custom-call | flops 1000000000 | tf_op jit(solution)/shard_map/pallas_call | solution.py:236
  3.7 16.3 %collective-permute-start.2 = (bf16[26,16,128]{2,1,0:T(8,128)(2,1)S(1)}, bf16[26,16,128]{2,1,0:T(8,128)(2,1)S(1)}, u32[]{:S(2)}, u32[]{:S(2)}) collective-permute-start(bf16[26,16,128]{2,1,0:T(8,128)(2,1)S(1)} %get-tuple-element.30), channel_id=1, source_target_pairs={{0,8},{4,12},{8,0},{12,4},{1,9},{5,13},{9,1},{13,5},{2,10},{6,14},... | collective-permute-start | bytes 319496 | tf_op jit(solution)/shard_map/ppermute | solution.py:252
  20.0 4.0 %collective-permute-start.3 = (bf16[26,16,128]{2,1,0:T(8,128)(2,1)S(1)}, bf16[26,16,128]{2,1,0:T(8,128)(2,1)S(1)}, u32[]{:S(2)}, u32[]{:S(2)}) collective-permute-start(bf16[26,16,128]{2,1,0:T(8,128)(2,1)S(1)} %get-tuple-element.31), channel_id=1, source_target_pairs={{0,4},{4,8},{8,12},{12,0},{1,5},{5,9},{9,13},{13,1},{2,6},{6,10},{... | collective-permute-start | bytes 319496 | tf_op jit(solution)/shard_map/ppermute | solution.py:252
  24.0 5.2 %collective-permute-start.4 = (bf16[26,16,128]{2,1,0:T(8,128)(2,1)S(1)}, bf16[26,16,128]{2,1,0:T(8,128)(2,1)S(1)}, u32[]{:S(2)}, u32[]{:S(2)}) collective-permute-start(bf16[26,16,128]{2,1,0:T(8,128)(2,1)S(1)} %get-tuple-element.32), channel_id=1, source_target_pairs={{0,12},{4,0},{8,4},{12,8},{1,13},{5,1},{9,5},{13,9},{2,14},{6,2},{... | collective-permute-start | bytes 319496 | tf_op jit(solution)/shard_map/ppermute | solution.py:252
  29.2 4.6 %collective-permute-start.1 = (bf16[26,16,128]{2,1,0:T(8,128)(2,1)S(1)}, bf16[26,16,128]{2,1,0:T(8,128)(2,1)S(1)}, u32[]{:S(2)}, u32[]{:S(2)}) collective-permute-start(bf16[26,16,128]{2,1,0:T(8,128)(2,1)S(1)} %get-tuple-element.33.refs_0_), channel_id=1, source_target_pairs={{16,32},{48,64},{80,96},{112,128},{144,160},{176,192},{208,224},{2... | collective-permute-start | bytes 319496 | tf_op jit(solution)/shard_map/ppermute | solution.py:270
  33.8 1.9 %collective-permute-start = (bf16[26,16,128]{2,1,0:T(8,128)(2,1)S(1)}, bf16[26,16,128]{2,1,0:T(8,128)(2,1)S(1)}, u32[]{:S(2)}, u32[]{:S(2)}) collective-permute-start(bf16[26,16,128]{2,1,0:T(8,128)(2,1)S(1)} %get-tuple-element.33.refs_0_), channel_id=1, source_target_pairs={{0,16},{16,0},{1,17},{17,1},{2,18},{18,2},{3,19},{19,3},{4,20},{20... | collective-permute-start | bytes 319496 | tf_op jit(solution)/shard_map/ppermute | solution.py:269
  35.8 2.6 %collective-permute-done.4 = bf16[26,16,128]{2,1,0:T(8,128)(2,1)S(1)} collective-permute-done((bf16[26,16,128]{2,1,0:T(8,128)(2,1)S(1)}, bf16[26,16,128]{2,1,0:T(8,128)(2,1)S(1)}, u32[]{:S(2)}, u32[]{:S(2)}) %collective-permute-start.4) | collective-permute-done | bytes 106528 | tf_op jit(solution)/shard_map/ppermute | solution.py:252
  38.4 0.0 copy-start
  38.4 4.3 %collective-permute-start.6 = (bf16[78,16,128]{2,1,0:T(8,128)(2,1)S(1)}, bf16[78,16,128]{2,1,0:T(8,128)(2,1)S(1)}, u32[]{:S(2)}, u32[]{:S(2)}) collective-permute-start(bf16[78,16,128]{2,1,0:T(8,128)(2,1)S(1)} %constant_dynamic-update-slice_fusion.refs_3_), channel_id=1, source_target_pairs={{16,32},{48,64},{80,96},{112,128},{144,160},{176,192},{208,224},{2... | collective-permute-start | bytes 958472 | tf_op jit(solution)/shard_map/ppermute | solution.py:270
  42.8 1.9 %collective-permute-start.5 = (bf16[78,16,128]{2,1,0:T(8,128)(2,1)S(1)}, bf16[78,16,128]{2,1,0:T(8,128)(2,1)S(1)}, u32[]{:S(2)}, u32[]{:S(2)}) collective-permute-start(bf16[78,16,128]{2,1,0:T(8,128)(2,1)S(1)} %constant_dynamic-update-slice_fusion.refs_3_), channel_id=1, source_target_pairs={{0,16},{16,0},{1,17},{17,1},{2,18},{18,2},{3,19},{19,3},{4,20},{20... | collective-permute-start | bytes 958472 | tf_op jit(solution)/shard_map/ppermute | solution.py:269
  44.7 0.2 copy.16
  44.9 0.4 shard_map.59
  45.3 2.1 %collective-permute-done.6.refs_5_ = bf16[78,16,128]{2,1,0:T(8,128)(2,1)S(1)} collective-permute-done((bf16[78,16,128]{2,1,0:T(8,128)(2,1)S(1)}, bf16[78,16,128]{2,1,0:T(8,128)(2,1)S(1)}, u32[]{:S(2)}, u32[]{:S(2)}) %collective-permute-start.6) | collective-permute-done | bytes 319520 | tf_op jit(solution)/shard_map/ppermute | solution.py:270
  47.4 3.9 %shard_map.60 = (bf16[64,1536]{1,0:T(8,128)(2,1)S(1)}, bf16[128,2048]{1,0:T(8,128)(2,1)S(1)}, f32[32,8,128]{2,1,0:T(8,128)}) custom-call(s32[2]{0:T(128)S(1)} %pad_add_fusion.place, bf16[26,16,128]{2,1,0:T(8,128)(2,1)S(1)} %get-tuple-element.33.refs_0_, bf16[26,16,128]{2,1,0:T(8,128)(2,1)S(1)} %collective-permute-done.refs_1_, ...), custom_call_target="tpu_custom_call" | custom-call | flops 3000000000 | tf_op jit(solution)/shard_map/pallas_call | solution.py:236
  51.3 11.1 %all-to-all-start = ((f32[32,1,8,128]{3,2,1,0:T(8,128)}), f32[32,1,8,128]{3,2,1,0:T(8,128)S(1)}, u32[]{:S(2)}, u32[]{:S(2)}) async-start(f32[32,1,8,128]{3,2,1,0:T(8,128)} %bitcast.9), calls=%async_computation | async-start | bytes 262144 | tf_op jit(solution)/shard_map/all_to_all | solution.py:302
  62.4 1.3 %shard_map.61 = (bf16[26,16,128]{2,1,0:T(8,128)(2,1)S(1)}, bf16[26,16,128]{2,1,0:T(8,128)(2,1)S(1)}, bf16[26,16,128]{2,1,0:T(8,128)(2,1)S(1)}, bf16[26,16,128]{2,1,0:T(8,128)(2,1)S(1)}) custom-call(s32[2]{0:T(128)S(1)} %pad_add_fusion.place, bf16[64,1536]{1,0:T(8,128)(2,1)S(1)} %get-tuple-element.41.activated, ...), custom_call_target="tpu_custom_call" | custom-call | flops 2000000000 | tf_op jit(solution)/shard_map/pallas_call | solution.py:236
  63.7 6.3 %all-to-all-done = f32[32,1,8,128]{3,2,1,0:T(8,128)S(1)} async-done(((f32[32,1,8,128]{3,2,1,0:T(8,128)}), f32[32,1,8,128]{3,2,1,0:T(8,128)S(1)}, u32[]{:S(2)}, u32[]{:S(2)}) %all-to-all-start) | async-done | bytes 131104 | tf_op jit(solution)/shard_map/all_to_all | solution.py:302
  70.0 0.6 broadcast_in_dim.14
  70.7 6.2 %all-to-all-start.1 = ((f32[16,1,8,128]{3,2,1,0:T(8,128)}), f32[16,1,8,128]{3,2,1,0:T(8,128)S(1)}, u32[]{:S(2)}, u32[]{:S(2)}) async-start(f32[16,1,8,128]{3,2,1,0:T(8,128)} %broadcast_in_dim.14), calls=%async_computation.1 | async-start | bytes 131072 | tf_op jit(solution)/shard_map/all_to_all | solution.py:305
  76.8 7.2 %collective-permute-start.7 = (bf16[26,16,128]{2,1,0:T(8,128)(2,1)S(1)}, bf16[26,16,128]{2,1,0:T(8,128)(2,1)S(1)}, u32[]{:S(2)}, u32[]{:S(2)}) collective-permute-start(bf16[26,16,128]{2,1,0:T(8,128)(2,1)S(1)} %get-tuple-element.49), channel_id=1, source_target_pairs={{0,12},{4,0},{8,4},{12,8},{1,13},{5,1},{9,5},{13,9},{2,14},{6,2},{... | collective-permute-start | bytes 319496 | tf_op jit(solution)/shard_map/ppermute | solution.py:252
  84.0 7.0 %collective-permute-start.8 = (bf16[26,16,128]{2,1,0:T(8,128)(2,1)S(1)}, bf16[26,16,128]{2,1,0:T(8,128)(2,1)S(1)}, u32[]{:S(2)}, u32[]{:S(2)}) collective-permute-start(bf16[26,16,128]{2,1,0:T(8,128)(2,1)S(1)} %get-tuple-element.50), channel_id=1, source_target_pairs={{0,8},{4,12},{8,0},{12,4},{1,9},{5,13},{9,1},{13,5},{2,10},{6,14},... | collective-permute-start | bytes 319496 | tf_op jit(solution)/shard_map/ppermute | solution.py:252
  91.0 7.0 %collective-permute-start.9 = (bf16[26,16,128]{2,1,0:T(8,128)(2,1)S(1)}, bf16[26,16,128]{2,1,0:T(8,128)(2,1)S(1)}, u32[]{:S(2)}, u32[]{:S(2)}) collective-permute-start(bf16[26,16,128]{2,1,0:T(8,128)(2,1)S(1)} %get-tuple-element.51), channel_id=1, source_target_pairs={{0,4},{4,8},{8,12},{12,0},{1,5},{5,9},{9,13},{13,1},{2,6},{6,10},{... | collective-permute-start | bytes 319496 | tf_op jit(solution)/shard_map/ppermute | solution.py:252
  98.1 0.7 broadcast_in_dim.15
  98.7 5.4 %all-to-all-start.2 = ((f32[32,1,8,128]{3,2,1,0:T(8,128)}), f32[32,1,8,128]{3,2,1,0:T(8,128)S(1)}, u32[]{:S(2)}, u32[]{:S(2)}) async-start(f32[32,1,8,128]{3,2,1,0:T(8,128)} %broadcast_in_dim.15), calls=%async_computation.2 | async-start | bytes 262144 | tf_op jit(solution)/shard_map/all_to_all | solution.py:308
  104.2 2.1 %shard_map.62 = (bf16[8,2,48,128]{3,2,1,0:T(8,128)(2,1)}, bf16[8,2,48,128]{3,2,1,0:T(8,128)(2,1)}) custom-call(s32[2]{0:T(128)S(1)} %pad_add_fusion.place, bf16[26,16,128]{2,1,0:T(8,128)(2,1)S(1)} %get-tuple-element.48.refs_0_, bf16[26,16,128]{2,1,0:T(8,128)(2,1)S(1)} %collective-permute-done.7.refs_1_, ...), custom_call_target="tpu_custom_call" | custom-call | flops 1000000000 | tf_op jit(solution)/shard_map/pallas_call | solution.py:236
  106.3 5.5 %all-to-all-done.2 = f32[32,1,8,128]{3,2,1,0:T(8,128)S(1)} async-done(((f32[32,1,8,128]{3,2,1,0:T(8,128)}), f32[32,1,8,128]{3,2,1,0:T(8,128)S(1)}, u32[]{:S(2)}, u32[]{:S(2)}) %all-to-all-start.2) | async-done | bytes 131104 | tf_op jit(solution)/shard_map/all_to_all | solution.py:308
  111.8 0.1 reshape.46
  111.9 0.2 reshape.44
  112.2 0.8 pad_maximum_fusion
  (22 shorter events, 0.2 us)
Async XLA Ops:
  0.7 0.9 copy-start.1
  1.6 0.9 copy-start.2
  3.7 32.0 %collective-permute-start.2 = (bf16[26,16,128]{2,1,0:T(8,128)(2,1)S(1)}, bf16[26,16,128]{2,1,0:T(8,128)(2,1)S(1)}, u32[]{:S(2)}, u32[]{:S(2)}) collective-permute-start(bf16[26,16,128]{2,1,0:T(8,128)(2,1)S(1)} %get-tuple-element.30), channel_id=1, source_target_pairs={{0,8},{4,12},{8,0},{12,4},{1,9},{5,13},{9,1},{13,5},{2,10},{6,14},... | collective-permute-start | bytes 319496 | tf_op jit(solution)/shard_map/ppermute | solution.py:252
  20.0 15.8 %collective-permute-start.3 = (bf16[26,16,128]{2,1,0:T(8,128)(2,1)S(1)}, bf16[26,16,128]{2,1,0:T(8,128)(2,1)S(1)}, u32[]{:S(2)}, u32[]{:S(2)}) collective-permute-start(bf16[26,16,128]{2,1,0:T(8,128)(2,1)S(1)} %get-tuple-element.31), channel_id=1, source_target_pairs={{0,4},{4,8},{8,12},{12,0},{1,5},{5,9},{9,13},{13,1},{2,6},{6,10},{... | collective-permute-start | bytes 319496 | tf_op jit(solution)/shard_map/ppermute | solution.py:252
  24.0 14.3 %collective-permute-start.4 = (bf16[26,16,128]{2,1,0:T(8,128)(2,1)S(1)}, bf16[26,16,128]{2,1,0:T(8,128)(2,1)S(1)}, u32[]{:S(2)}, u32[]{:S(2)}) collective-permute-start(bf16[26,16,128]{2,1,0:T(8,128)(2,1)S(1)} %get-tuple-element.32), channel_id=1, source_target_pairs={{0,12},{4,0},{8,4},{12,8},{1,13},{5,1},{9,5},{13,9},{2,14},{6,2},{... | collective-permute-start | bytes 319496 | tf_op jit(solution)/shard_map/ppermute | solution.py:252
  29.2 9.1 %collective-permute-start.1 = (bf16[26,16,128]{2,1,0:T(8,128)(2,1)S(1)}, bf16[26,16,128]{2,1,0:T(8,128)(2,1)S(1)}, u32[]{:S(2)}, u32[]{:S(2)}) collective-permute-start(bf16[26,16,128]{2,1,0:T(8,128)(2,1)S(1)} %get-tuple-element.33.refs_0_), channel_id=1, source_target_pairs={{16,32},{48,64},{80,96},{112,128},{144,160},{176,192},{208,224},{2... | collective-permute-start | bytes 319496 | tf_op jit(solution)/shard_map/ppermute | solution.py:270
  33.8 4.5 %collective-permute-start = (bf16[26,16,128]{2,1,0:T(8,128)(2,1)S(1)}, bf16[26,16,128]{2,1,0:T(8,128)(2,1)S(1)}, u32[]{:S(2)}, u32[]{:S(2)}) collective-permute-start(bf16[26,16,128]{2,1,0:T(8,128)(2,1)S(1)} %get-tuple-element.33.refs_0_), channel_id=1, source_target_pairs={{0,16},{16,0},{1,17},{17,1},{2,18},{18,2},{3,19},{19,3},{4,20},{20... | collective-permute-start | bytes 319496 | tf_op jit(solution)/shard_map/ppermute | solution.py:269
  38.4 6.3 %copy-start = (bf16[32,27,32]{2,0,1:T(8,128)(2,1)S(1)}, bf16[32,27,32]{2,0,1:T(8,128)(2,1)}, u32[]{:S(2)}) copy-start(bf16[32,27,32]{2,0,1:T(8,128)(2,1)} %param.5) | copy-start | bytes 165892
  38.4 9.0 %collective-permute-start.6 = (bf16[78,16,128]{2,1,0:T(8,128)(2,1)S(1)}, bf16[78,16,128]{2,1,0:T(8,128)(2,1)S(1)}, u32[]{:S(2)}, u32[]{:S(2)}) collective-permute-start(bf16[78,16,128]{2,1,0:T(8,128)(2,1)S(1)} %constant_dynamic-update-slice_fusion.refs_3_), channel_id=1, source_target_pairs={{16,32},{48,64},{80,96},{112,128},{144,160},{176,192},{208,224},{2... | collective-permute-start | bytes 958472 | tf_op jit(solution)/shard_map/ppermute | solution.py:270
  42.8 4.7 %collective-permute-start.5 = (bf16[78,16,128]{2,1,0:T(8,128)(2,1)S(1)}, bf16[78,16,128]{2,1,0:T(8,128)(2,1)S(1)}, u32[]{:S(2)}, u32[]{:S(2)}) collective-permute-start(bf16[78,16,128]{2,1,0:T(8,128)(2,1)S(1)} %constant_dynamic-update-slice_fusion.refs_3_), channel_id=1, source_target_pairs={{0,16},{16,0},{1,17},{17,1},{2,18},{18,2},{3,19},{19,3},{4,20},{20... | collective-permute-start | bytes 958472 | tf_op jit(solution)/shard_map/ppermute | solution.py:269
  51.3 18.7 %all-to-all-start = ((f32[32,1,8,128]{3,2,1,0:T(8,128)}), f32[32,1,8,128]{3,2,1,0:T(8,128)S(1)}, u32[]{:S(2)}, u32[]{:S(2)}) async-start(f32[32,1,8,128]{3,2,1,0:T(8,128)} %bitcast.9), calls=%async_computation | async-start | bytes 262144 | tf_op jit(solution)/shard_map/all_to_all | solution.py:302
  70.7 27.4 %all-to-all-start.1 = ((f32[16,1,8,128]{3,2,1,0:T(8,128)}), f32[16,1,8,128]{3,2,1,0:T(8,128)S(1)}, u32[]{:S(2)}, u32[]{:S(2)}) async-start(f32[16,1,8,128]{3,2,1,0:T(8,128)} %broadcast_in_dim.14), calls=%async_computation.1 | async-start | bytes 131072 | tf_op jit(solution)/shard_map/all_to_all | solution.py:305
  76.8 27.3 %collective-permute-start.7 = (bf16[26,16,128]{2,1,0:T(8,128)(2,1)S(1)}, bf16[26,16,128]{2,1,0:T(8,128)(2,1)S(1)}, u32[]{:S(2)}, u32[]{:S(2)}) collective-permute-start(bf16[26,16,128]{2,1,0:T(8,128)(2,1)S(1)} %get-tuple-element.49), channel_id=1, source_target_pairs={{0,12},{4,0},{8,4},{12,8},{1,13},{5,1},{9,5},{13,9},{2,14},{6,2},{... | collective-permute-start | bytes 319496 | tf_op jit(solution)/shard_map/ppermute | solution.py:252
  84.0 20.2 %collective-permute-start.8 = (bf16[26,16,128]{2,1,0:T(8,128)(2,1)S(1)}, bf16[26,16,128]{2,1,0:T(8,128)(2,1)S(1)}, u32[]{:S(2)}, u32[]{:S(2)}) collective-permute-start(bf16[26,16,128]{2,1,0:T(8,128)(2,1)S(1)} %get-tuple-element.50), channel_id=1, source_target_pairs={{0,8},{4,12},{8,0},{12,4},{1,9},{5,13},{9,1},{13,5},{2,10},{6,14},... | collective-permute-start | bytes 319496 | tf_op jit(solution)/shard_map/ppermute | solution.py:252
  91.0 13.2 %collective-permute-start.9 = (bf16[26,16,128]{2,1,0:T(8,128)(2,1)S(1)}, bf16[26,16,128]{2,1,0:T(8,128)(2,1)S(1)}, u32[]{:S(2)}, u32[]{:S(2)}) collective-permute-start(bf16[26,16,128]{2,1,0:T(8,128)(2,1)S(1)} %get-tuple-element.51), channel_id=1, source_target_pairs={{0,4},{4,8},{8,12},{12,0},{1,5},{5,9},{9,13},{13,1},{2,6},{6,10},{... | collective-permute-start | bytes 319496 | tf_op jit(solution)/shard_map/ppermute | solution.py:252
  98.7 13.1 %all-to-all-start.2 = ((f32[32,1,8,128]{3,2,1,0:T(8,128)}), f32[32,1,8,128]{3,2,1,0:T(8,128)S(1)}, u32[]{:S(2)}, u32[]{:S(2)}) async-start(f32[32,1,8,128]{3,2,1,0:T(8,128)} %broadcast_in_dim.15), calls=%async_computation.2 | async-start | bytes 262144 | tf_op jit(solution)/shard_map/all_to_all | solution.py:308

commit v5 on v4

--- a/solution.py
+++ b/solution.py
@@ -57,8 +57,7 @@
         out[14:26] = moved[2:14, :, LANES:]
 
 
-def unpack_kernel(place, *refs):
-    parts, (activated, input_grad) = refs[:4], refs[4:]
+def moves_kernel(place, plain, summed):
     outer = iota((16, 48, LANES), 0)
     y = iota((16, 48, LANES), 1)
     part = (y >= 12).astype(jnp.int32) + (y >= 24).astype(jnp.int32) + (y >= 36).astype(jnp.int32)
@@ -71,16 +70,22 @@
         move = [one_hot(functools.reduce(jnp.logical_or, [at == lane + k * LANES for at in source])) for k in range(tiles)]
         return jnp.concatenate(move, axis=1).astype(BF16)
 
-    rows = jnp.concatenate([part[0:12].reshape(192, LANES) for part in parts], axis=0)
     source = (step * 192 + row * 16 + inner).reshape(768, LANES)
-    activated[...] = dot(gather([source], 6), rows).astype(BF16).reshape(8, 2, 48, LANES)
-
-    rows = jnp.concatenate([part[12:26].reshape(224, LANES) for part in parts], axis=0)
+    plain[...] = gather([source], 6)
     source = (step * 224 + (row + 1) * 16 + inner).reshape(768, LANES)
     other = jnp.where(row == 0, ((step + 3) & 3) * 224 + 13 * 16, ((step + 1) & 3) * 224) + inner
     border = ((row == 0) & (part > 0)) | ((row == 11) & (part < 3))
     other = jnp.where(border, other, -1).reshape(768, LANES)
-    input_grad[...] = dot(gather([source, other], 7), rows).astype(BF16).reshape(8, 2, 48, LANES)
+    summed[...] = gather([source, other], 7)
+
+
+def unpack_kernel(plain, summed, *refs):
+    mine, opposite, *sides = refs[:4]
+    parts, (activated, input_grad) = (mine, sides[0], opposite, sides[1]), refs[4:]
+    rows = jnp.concatenate([part[0:12].reshape(192, LANES) for part in parts], axis=0)
+    activated[...] = dot(plain[...], rows).astype(BF16).reshape(8, 2, 48, LANES)
+    rows = jnp.concatenate([part[12:26].reshape(224, LANES) for part in parts], axis=0)
+    input_grad[...] = dot(summed[...], rows).astype(BF16).reshape(8, 2, 48, LANES)
 
 
 def band_kernel(by_out, by_in, forward, backward):
@@ -307,7 +312,14 @@
     share = jnp.sum(terms, axis=0) / jnp.sqrt(jnp.float32(cells))
     whole = lax.all_to_all(jnp.broadcast_to(share, (pieces,) + share.shape), plane, 0, 0).reshape(32, 8, LANES)
     slab = jax.ShapeDtypeStruct((8, 2, 48, LANES), BF16)
-    activated, input_grad = call(unpack_kernel, (slab, slab), place=True, flops=10**9)(place, *reshard(backs))
+    moves = call(
+        moves_kernel,
+        (jax.ShapeDtypeStruct((768, 768), BF16), jax.ShapeDtypeStruct((768, 896), BF16)),
+        place=True,
+        flops=10**9,
+    )(place)
+    got = reshard(backs)
+    activated, input_grad = call(unpack_kernel, (slab, slab), flops=10**9)(*moves, got[0], got[2], got[1], got[3])
     eight = whole[:24].reshape(3, 2, 4, 8, 4, 32).transpose(2, 3, 1, 4, 0, 5).reshape(32, 8, 3, 32)
     ninth = whole[24:28].reshape(32, 1, 4, 32)[:, :, :3]
     weight_grad = jnp.concatenate([eight, ninth], axis=1).reshape(32, 27, 32)

time: 114 us -> 113 us (level)
    all_to_all x1, waiting for transfers between devices: 5.48 us -> 1.27 us  [body(): lax.all_to_all(jnp.broadcast_to(share, (pieces,) + share.shape), plane, 0...]
    ppermute x6, waiting for transfers between devices: 2.6 us -> 6.32 us  [reshard(): lax.ppermute(parts[step], 'chan', [(i, (i + step) % 4) for i in range(4)])]
    pallas_call x5 -> x6, Pallas kernels: 8.9 us -> 9.4 us  [run(): pl.pallas_call(kernel, out_shape=outs, in_specs=specs, out_specs=jax.tree...]
  transfers between devices with their start and end apart: 13 -> 13, of which waited for: 4 -> 5; matrix products, arithmetic and copies ran while one was open for 1% -> 1% of each run, Pallas kernels for 3% -> 4%
where the time goes in v5:
time: 113 us
  starting transfers between devices  81.9 us (72%)
  waiting for transfers between devices  16 us (14%)
  Pallas kernels  9.4 us (8%)
  local copies, waits for them, and re-layouts  3.71 us (3%)
    ppermute x6, starting transfers between devices, reshard(): lax.ppermute(parts[step], 'chan', [(i, (i + step) % 4) for i in range(4)])  46.6 us
    all_to_all x1, starting transfers between devices, body(): lax.all_to_all(grads.reshape((pieces, -1) + grads.shape[1:]), plane, 0, 0)  11 us
    pallas_call x6, Pallas kernels, run(): pl.pallas_call(kernel, out_shape=outs, in_specs=specs, out_specs=jax.tree...  9.4 us
    ppermute x2, starting transfers between devices, body(): far = lax.ppermute(mine, ('zlo', 'y', 'core'), remote)  8.8 us
    ppermute x6, waiting for transfers between devices, reshard(): lax.ppermute(parts[step], 'chan', [(i, (i + step) % 4) for i in range(4)])  6.32 us
    all_to_all x1, waiting for transfers between devices, body(): lax.all_to_all(grads.reshape((pieces, -1) + grads.shape[1:]), plane, 0, 0)  6.27 us
    all_to_all x1, starting transfers between devices, body(): lax.all_to_all(jnp.broadcast_to(share, (rest,) + share.shape), column, 0, 0)  6.17 us
    all_to_all x1, starting transfers between devices, body(): lax.all_to_all(jnp.broadcast_to(share, (pieces,) + share.shape), plane, 0...  5.43 us
  transfers between devices with their start and end apart: 13, of which 5 were waited for; matrix products, arithmetic and copies ran while one was open for 1% of the time, Pallas kernels for 4%

profile of v5, /device:TPU:1, one launch (start us, length us, event | category | flops | bytes accessed | tf_op | source)
XLA Modules:
  0.0 112.9 jit_solution(14416271245572756530)
XLA Ops:
  0.7 0.9 copy-done.1
  1.6 0.9 copy-done.2
  2.6 1.1 %shard_map.59 = (bf16[26,16,128]{2,1,0:T(8,128)(2,1)S(1)}, bf16[26,16,128]{2,1,0:T(8,128)(2,1)S(1)}, bf16[26,16,128]{2,1,0:T(8,128)(2,1)S(1)}, bf16[26,16,128]{2,1,0:T(8,128)(2,1)S(1)}) custom-call(s32[2]{0:T(128)S(1)} %pad_add_fusion.place, bf16[8,2,48,128]{3,2,1,0:T(8,128)(2,1)S(1)} %bitcast.25, bf16[8,2,48,128]{3,2,1,0:T(8,128)(2,1)S(1)} %bitcast.26), custom_call_target="tpu_custom_call" | custom-call | flops 1000000000 | tf_op jit(solution)/shard_map/pallas_call | solution.py:241
  3.7 16.3 %collective-permute-start.2 = (bf16[26,16,128]{2,1,0:T(8,128)(2,1)S(1)}, bf16[26,16,128]{2,1,0:T(8,128)(2,1)S(1)}, u32[]{:S(2)}, u32[]{:S(2)}) collective-permute-start(bf16[26,16,128]{2,1,0:T(8,128)(2,1)S(1)} %get-tuple-element.34), channel_id=1, source_target_pairs={{0,8},{4,12},{8,0},{12,4},{1,9},{5,13},{9,1},{13,5},{2,10},{6,14},... | collective-permute-start | bytes 319496 | tf_op jit(solution)/shard_map/ppermute | solution.py:257
  20.0 4.0 %collective-permute-start.3 = (bf16[26,16,128]{2,1,0:T(8,128)(2,1)S(1)}, bf16[26,16,128]{2,1,0:T(8,128)(2,1)S(1)}, u32[]{:S(2)}, u32[]{:S(2)}) collective-permute-start(bf16[26,16,128]{2,1,0:T(8,128)(2,1)S(1)} %get-tuple-element.35), channel_id=1, source_target_pairs={{0,4},{4,8},{8,12},{12,0},{1,5},{5,9},{9,13},{13,1},{2,6},{6,10},{... | collective-permute-start | bytes 319496 | tf_op jit(solution)/shard_map/ppermute | solution.py:257
  24.0 5.2 %collective-permute-start.4 = (bf16[26,16,128]{2,1,0:T(8,128)(2,1)S(1)}, bf16[26,16,128]{2,1,0:T(8,128)(2,1)S(1)}, u32[]{:S(2)}, u32[]{:S(2)}) collective-permute-start(bf16[26,16,128]{2,1,0:T(8,128)(2,1)S(1)} %get-tuple-element.36), channel_id=1, source_target_pairs={{0,12},{4,0},{8,4},{12,8},{1,13},{5,1},{9,5},{13,9},{2,14},{6,2},{... | collective-permute-start | bytes 319496 | tf_op jit(solution)/shard_map/ppermute | solution.py:257
  29.2 4.6 %collective-permute-start.1 = (bf16[26,16,128]{2,1,0:T(8,128)(2,1)S(1)}, bf16[26,16,128]{2,1,0:T(8,128)(2,1)S(1)}, u32[]{:S(2)}, u32[]{:S(2)}) collective-permute-start(bf16[26,16,128]{2,1,0:T(8,128)(2,1)S(1)} %get-tuple-element.37.refs_0_), channel_id=1, source_target_pairs={{16,32},{48,64},{80,96},{112,128},{144,160},{176,192},{208,224},{2... | collective-permute-start | bytes 319496 | tf_op jit(solution)/shard_map/ppermute | solution.py:275
  33.8 1.9 %collective-permute-start = (bf16[26,16,128]{2,1,0:T(8,128)(2,1)S(1)}, bf16[26,16,128]{2,1,0:T(8,128)(2,1)S(1)}, u32[]{:S(2)}, u32[]{:S(2)}) collective-permute-start(bf16[26,16,128]{2,1,0:T(8,128)(2,1)S(1)} %get-tuple-element.37.refs_0_), channel_id=1, source_target_pairs={{0,16},{16,0},{1,17},{17,1},{2,18},{18,2},{3,19},{19,3},{4,20},{20... | collective-permute-start | bytes 319496 | tf_op jit(solution)/shard_map/ppermute | solution.py:274
  35.8 2.6 %collective-permute-done.4 = bf16[26,16,128]{2,1,0:T(8,128)(2,1)S(1)} collective-permute-done((bf16[26,16,128]{2,1,0:T(8,128)(2,1)S(1)}, bf16[26,16,128]{2,1,0:T(8,128)(2,1)S(1)}, u32[]{:S(2)}, u32[]{:S(2)}) %collective-permute-start.4) | collective-permute-done | bytes 106528 | tf_op jit(solution)/shard_map/ppermute | solution.py:257
  38.4 4.2 %collective-permute-start.6 = (bf16[78,16,128]{2,1,0:T(8,128)(2,1)S(1)}, bf16[78,16,128]{2,1,0:T(8,128)(2,1)S(1)}, u32[]{:S(2)}, u32[]{:S(2)}) collective-permute-start(bf16[78,16,128]{2,1,0:T(8,128)(2,1)S(1)} %constant_dynamic-update-slice_fusion.refs_3_), channel_id=1, source_target_pairs={{16,32},{48,64},{80,96},{112,128},{144,160},{176,192},{208,224},{2... | collective-permute-start | bytes 958472 | tf_op jit(solution)/shard_map/ppermute | solution.py:275
  42.6 1.9 %collective-permute-start.5 = (bf16[78,16,128]{2,1,0:T(8,128)(2,1)S(1)}, bf16[78,16,128]{2,1,0:T(8,128)(2,1)S(1)}, u32[]{:S(2)}, u32[]{:S(2)}) collective-permute-start(bf16[78,16,128]{2,1,0:T(8,128)(2,1)S(1)} %constant_dynamic-update-slice_fusion.refs_3_), channel_id=1, source_target_pairs={{0,16},{16,0},{1,17},{17,1},{2,18},{18,2},{3,19},{19,3},{4,20},{20... | collective-permute-start | bytes 958472 | tf_op jit(solution)/shard_map/ppermute | solution.py:274
  44.6 0.2 copy.16
  44.7 0.4 shard_map.60
  45.2 2.1 %collective-permute-done.6.refs_5_ = bf16[78,16,128]{2,1,0:T(8,128)(2,1)S(1)} collective-permute-done((bf16[78,16,128]{2,1,0:T(8,128)(2,1)S(1)}, bf16[78,16,128]{2,1,0:T(8,128)(2,1)S(1)}, u32[]{:S(2)}, u32[]{:S(2)}) %collective-permute-start.6) | collective-permute-done | bytes 319520 | tf_op jit(solution)/shard_map/ppermute | solution.py:275
  47.3 3.9 %shard_map.61 = (bf16[64,1536]{1,0:T(8,128)(2,1)S(1)}, bf16[128,2048]{1,0:T(8,128)(2,1)S(1)}, f32[32,8,128]{2,1,0:T(8,128)}) custom-call(s32[2]{0:T(128)S(1)} %pad_add_fusion.place, bf16[26,16,128]{2,1,0:T(8,128)(2,1)S(1)} %get-tuple-element.37.refs_0_, bf16[26,16,128]{2,1,0:T(8,128)(2,1)S(1)} %collective-permute-done.refs_1_, ...), custom_call_target="tpu_custom_call" | custom-call | flops 3000000000 | tf_op jit(solution)/shard_map/pallas_call | solution.py:241
  51.2 11.0 %all-to-all-start = ((f32[32,1,8,128]{3,2,1,0:T(8,128)}), f32[32,1,8,128]{3,2,1,0:T(8,128)S(1)}, u32[]{:S(2)}, u32[]{:S(2)}) async-start(f32[32,1,8,128]{3,2,1,0:T(8,128)} %bitcast.9), calls=%async_computation | async-start | bytes 262144 | tf_op jit(solution)/shard_map/all_to_all | solution.py:307
  62.2 1.3 %shard_map.62 = (bf16[26,16,128]{2,1,0:T(8,128)(2,1)S(1)}, bf16[26,16,128]{2,1,0:T(8,128)(2,1)S(1)}, bf16[26,16,128]{2,1,0:T(8,128)(2,1)S(1)}, bf16[26,16,128]{2,1,0:T(8,128)(2,1)S(1)}) custom-call(s32[2]{0:T(128)S(1)} %pad_add_fusion.place, bf16[64,1536]{1,0:T(8,128)(2,1)S(1)} %get-tuple-element.45.activated, ...), custom_call_target="tpu_custom_call" | custom-call | flops 2000000000 | tf_op jit(solution)/shard_map/pallas_call | solution.py:241
  63.6 6.3 %all-to-all-done = f32[32,1,8,128]{3,2,1,0:T(8,128)S(1)} async-done(((f32[32,1,8,128]{3,2,1,0:T(8,128)}), f32[32,1,8,128]{3,2,1,0:T(8,128)S(1)}, u32[]{:S(2)}, u32[]{:S(2)}) %all-to-all-start) | async-done | bytes 131104 | tf_op jit(solution)/shard_map/all_to_all | solution.py:307
  69.9 0.6 broadcast_in_dim.14
  70.5 6.2 %all-to-all-start.1 = ((f32[16,1,8,128]{3,2,1,0:T(8,128)}), f32[16,1,8,128]{3,2,1,0:T(8,128)S(1)}, u32[]{:S(2)}, u32[]{:S(2)}) async-start(f32[16,1,8,128]{3,2,1,0:T(8,128)} %broadcast_in_dim.14), calls=%async_computation.1 | async-start | bytes 131072 | tf_op jit(solution)/shard_map/all_to_all | solution.py:310
  76.7 12.0 %collective-permute-start.7 = (bf16[26,16,128]{2,1,0:T(8,128)(2,1)S(1)}, bf16[26,16,128]{2,1,0:T(8,128)(2,1)S(1)}, u32[]{:S(2)}, u32[]{:S(2)}) collective-permute-start(bf16[26,16,128]{2,1,0:T(8,128)(2,1)S(1)} %get-tuple-element.53), channel_id=1, source_target_pairs={{0,8},{4,12},{8,0},{12,4},{1,9},{5,13},{9,1},{13,5},{2,10},{6,14},... | collective-permute-start | bytes 319496 | tf_op jit(solution)/shard_map/ppermute | solution.py:257
  88.7 2.2 %collective-permute-start.8 = (bf16[26,16,128]{2,1,0:T(8,128)(2,1)S(1)}, bf16[26,16,128]{2,1,0:T(8,128)(2,1)S(1)}, u32[]{:S(2)}, u32[]{:S(2)}) collective-permute-start(bf16[26,16,128]{2,1,0:T(8,128)(2,1)S(1)} %get-tuple-element.54), channel_id=1, source_target_pairs={{0,12},{4,0},{8,4},{12,8},{1,13},{5,1},{9,5},{13,9},{2,14},{6,2},{... | collective-permute-start | bytes 319496 | tf_op jit(solution)/shard_map/ppermute | solution.py:257
  90.9 7.0 %collective-permute-start.9 = (bf16[26,16,128]{2,1,0:T(8,128)(2,1)S(1)}, bf16[26,16,128]{2,1,0:T(8,128)(2,1)S(1)}, u32[]{:S(2)}, u32[]{:S(2)}) collective-permute-start(bf16[26,16,128]{2,1,0:T(8,128)(2,1)S(1)} %get-tuple-element.55), channel_id=1, source_target_pairs={{0,4},{4,8},{8,12},{12,0},{1,5},{5,9},{9,13},{13,1},{2,6},{6,10},{... | collective-permute-start | bytes 319496 | tf_op jit(solution)/shard_map/ppermute | solution.py:257
  97.9 0.7 broadcast_in_dim.15
  98.6 5.4 %all-to-all-start.2 = ((f32[32,1,8,128]{3,2,1,0:T(8,128)}), f32[32,1,8,128]{3,2,1,0:T(8,128)S(1)}, u32[]{:S(2)}, u32[]{:S(2)}) async-start(f32[32,1,8,128]{3,2,1,0:T(8,128)} %broadcast_in_dim.15), calls=%async_computation.2 | async-start | bytes 262144 | tf_op jit(solution)/shard_map/all_to_all | solution.py:313
  104.0 1.1 shard_map.58
  105.1 3.7 %collective-permute-done.8.refs_2_ = bf16[26,16,128]{2,1,0:T(8,128)(2,1)S(1)} collective-permute-done((bf16[26,16,128]{2,1,0:T(8,128)(2,1)S(1)}, bf16[26,16,128]{2,1,0:T(8,128)(2,1)S(1)}, u32[]{:S(2)}, u32[]{:S(2)}) %collective-permute-start.8) | collective-permute-done | bytes 106528 | tf_op jit(solution)/shard_map/ppermute | solution.py:257
  108.9 1.5 %shard_map.63 = (bf16[8,2,48,128]{3,2,1,0:T(8,128)(2,1)}, bf16[8,2,48,128]{3,2,1,0:T(8,128)(2,1)}) custom-call(bf16[768,768]{1,0:T(8,128)(2,1)S(1)} %get-tuple-element.31.plain, bf16[768,896]{1,0:T(8,128)(2,1)S(1)} %get-tuple-element.32.summed, bf16[26,16,128]{2,1,0:T(8,128)(2,1)S(1)} %get-tuple-element.52.refs_0_, ...), custom_call_target="tpu_custom_call" | custom-call | flops 1000000000 | tf_op jit(solution)/shard_map/pallas_call | solution.py:241
  110.4 1.3 %all-to-all-done.2 = f32[32,1,8,128]{3,2,1,0:T(8,128)S(1)} async-done(((f32[32,1,8,128]{3,2,1,0:T(8,128)}), f32[32,1,8,128]{3,2,1,0:T(8,128)S(1)}, u32[]{:S(2)}, u32[]{:S(2)}) %all-to-all-start.2) | async-done | bytes 131104 | tf_op jit(solution)/shard_map/all_to_all | solution.py:313
  111.7 0.1 reshape.46
  111.8 0.2 reshape.44
  112.1 0.8 pad_maximum_fusion
  (23 shorter events, 0.3 us)
Async XLA Ops:
  0.7 0.9 copy-start.1
  1.6 0.9 copy-start.2
  2.6 42.0 %copy-start = (bf16[32,27,32]{2,0,1:T(8,128)(2,1)S(1)}, bf16[32,27,32]{2,0,1:T(8,128)(2,1)}, u32[]{:S(2)}) copy-start(bf16[32,27,32]{2,0,1:T(8,128)(2,1)} %param.5) | copy-start | bytes 165892
  3.7 32.0 %collective-permute-start.2 = (bf16[26,16,128]{2,1,0:T(8,128)(2,1)S(1)}, bf16[26,16,128]{2,1,0:T(8,128)(2,1)S(1)}, u32[]{:S(2)}, u32[]{:S(2)}) collective-permute-start(bf16[26,16,128]{2,1,0:T(8,128)(2,1)S(1)} %get-tuple-element.34), channel_id=1, source_target_pairs={{0,8},{4,12},{8,0},{12,4},{1,9},{5,13},{9,1},{13,5},{2,10},{6,14},... | collective-permute-start | bytes 319496 | tf_op jit(solution)/shard_map/ppermute | solution.py:257
  20.0 15.8 %collective-permute-start.3 = (bf16[26,16,128]{2,1,0:T(8,128)(2,1)S(1)}, bf16[26,16,128]{2,1,0:T(8,128)(2,1)S(1)}, u32[]{:S(2)}, u32[]{:S(2)}) collective-permute-start(bf16[26,16,128]{2,1,0:T(8,128)(2,1)S(1)} %get-tuple-element.35), channel_id=1, source_target_pairs={{0,4},{4,8},{8,12},{12,0},{1,5},{5,9},{9,13},{13,1},{2,6},{6,10},{... | collective-permute-start | bytes 319496 | tf_op jit(solution)/shard_map/ppermute | solution.py:257
  24.0 14.3 %collective-permute-start.4 = (bf16[26,16,128]{2,1,0:T(8,128)(2,1)S(1)}, bf16[26,16,128]{2,1,0:T(8,128)(2,1)S(1)}, u32[]{:S(2)}, u32[]{:S(2)}) collective-permute-start(bf16[26,16,128]{2,1,0:T(8,128)(2,1)S(1)} %get-tuple-element.36), channel_id=1, source_target_pairs={{0,12},{4,0},{8,4},{12,8},{1,13},{5,1},{9,5},{13,9},{2,14},{6,2},{... | collective-permute-start | bytes 319496 | tf_op jit(solution)/shard_map/ppermute | solution.py:257
  29.2 9.2 %collective-permute-start.1 = (bf16[26,16,128]{2,1,0:T(8,128)(2,1)S(1)}, bf16[26,16,128]{2,1,0:T(8,128)(2,1)S(1)}, u32[]{:S(2)}, u32[]{:S(2)}) collective-permute-start(bf16[26,16,128]{2,1,0:T(8,128)(2,1)S(1)} %get-tuple-element.37.refs_0_), channel_id=1, source_target_pairs={{16,32},{48,64},{80,96},{112,128},{144,160},{176,192},{208,224},{2... | collective-permute-start | bytes 319496 | tf_op jit(solution)/shard_map/ppermute | solution.py:275
  33.8 4.5 %collective-permute-start = (bf16[26,16,128]{2,1,0:T(8,128)(2,1)S(1)}, bf16[26,16,128]{2,1,0:T(8,128)(2,1)S(1)}, u32[]{:S(2)}, u32[]{:S(2)}) collective-permute-start(bf16[26,16,128]{2,1,0:T(8,128)(2,1)S(1)} %get-tuple-element.37.refs_0_), channel_id=1, source_target_pairs={{0,16},{16,0},{1,17},{17,1},{2,18},{18,2},{3,19},{19,3},{4,20},{20... | collective-permute-start | bytes 319496 | tf_op jit(solution)/shard_map/ppermute | solution.py:274
  38.4 8.9 %collective-permute-start.6 = (bf16[78,16,128]{2,1,0:T(8,128)(2,1)S(1)}, bf16[78,16,128]{2,1,0:T(8,128)(2,1)S(1)}, u32[]{:S(2)}, u32[]{:S(2)}) collective-permute-start(bf16[78,16,128]{2,1,0:T(8,128)(2,1)S(1)} %constant_dynamic-update-slice_fusion.refs_3_), channel_id=1, source_target_pairs={{16,32},{48,64},{80,96},{112,128},{144,160},{176,192},{208,224},{2... | collective-permute-start | bytes 958472 | tf_op jit(solution)/shard_map/ppermute | solution.py:275
  42.6 4.7 %collective-permute-start.5 = (bf16[78,16,128]{2,1,0:T(8,128)(2,1)S(1)}, bf16[78,16,128]{2,1,0:T(8,128)(2,1)S(1)}, u32[]{:S(2)}, u32[]{:S(2)}) collective-permute-start(bf16[78,16,128]{2,1,0:T(8,128)(2,1)S(1)} %constant_dynamic-update-slice_fusion.refs_3_), channel_id=1, source_target_pairs={{0,16},{16,0},{1,17},{17,1},{2,18},{18,2},{3,19},{19,3},{4,20},{20... | collective-permute-start | bytes 958472 | tf_op jit(solution)/shard_map/ppermute | solution.py:274
  51.2 18.7 %all-to-all-start = ((f32[32,1,8,128]{3,2,1,0:T(8,128)}), f32[32,1,8,128]{3,2,1,0:T(8,128)S(1)}, u32[]{:S(2)}, u32[]{:S(2)}) async-start(f32[32,1,8,128]{3,2,1,0:T(8,128)} %bitcast.9), calls=%async_computation | async-start | bytes 262144 | tf_op jit(solution)/shard_map/all_to_all | solution.py:307
  70.5 27.4 %all-to-all-start.1 = ((f32[16,1,8,128]{3,2,1,0:T(8,128)}), f32[16,1,8,128]{3,2,1,0:T(8,128)S(1)}, u32[]{:S(2)}, u32[]{:S(2)}) async-start(f32[16,1,8,128]{3,2,1,0:T(8,128)} %broadcast_in_dim.14), calls=%async_computation.1 | async-start | bytes 131072 | tf_op jit(solution)/shard_map/all_to_all | solution.py:310
  76.7 28.4 %collective-permute-start.7 = (bf16[26,16,128]{2,1,0:T(8,128)(2,1)S(1)}, bf16[26,16,128]{2,1,0:T(8,128)(2,1)S(1)}, u32[]{:S(2)}, u32[]{:S(2)}) collective-permute-start(bf16[26,16,128]{2,1,0:T(8,128)(2,1)S(1)} %get-tuple-element.53), channel_id=1, source_target_pairs={{0,8},{4,12},{8,0},{12,4},{1,9},{5,13},{9,1},{13,5},{2,10},{6,14},... | collective-permute-start | bytes 319496 | tf_op jit(solution)/shard_map/ppermute | solution.py:257
  88.7 20.2 %collective-permute-start.8 = (bf16[26,16,128]{2,1,0:T(8,128)(2,1)S(1)}, bf16[26,16,128]{2,1,0:T(8,128)(2,1)S(1)}, u32[]{:S(2)}, u32[]{:S(2)}) collective-permute-start(bf16[26,16,128]{2,1,0:T(8,128)(2,1)S(1)} %get-tuple-element.54), channel_id=1, source_target_pairs={{0,12},{4,0},{8,4},{12,8},{1,13},{5,1},{9,5},{13,9},{2,14},{6,2},{... | collective-permute-start | bytes 319496 | tf_op jit(solution)/shard_map/ppermute | solution.py:257
  90.9 18.0 %collective-permute-start.9 = (bf16[26,16,128]{2,1,0:T(8,128)(2,1)S(1)}, bf16[26,16,128]{2,1,0:T(8,128)(2,1)S(1)}, u32[]{:S(2)}, u32[]{:S(2)}) collective-permute-start(bf16[26,16,128]{2,1,0:T(8,128)(2,1)S(1)} %get-tuple-element.55), channel_id=1, source_target_pairs={{0,4},{4,8},{8,12},{12,0},{1,5},{5,9},{9,13},{13,1},{2,6},{6,10},{... | collective-permute-start | bytes 319496 | tf_op jit(solution)/shard_map/ppermute | solution.py:257
  98.6 13.1 %all-to-all-start.2 = ((f32[32,1,8,128]{3,2,1,0:T(8,128)}), f32[32,1,8,128]{3,2,1,0:T(8,128)S(1)}, u32[]{:S(2)}, u32[]{:S(2)}) async-start(f32[32,1,8,128]{3,2,1,0:T(8,128)} %broadcast_in_dim.15), calls=%async_computation.2 | async-start | bytes 262144 | tf_op jit(solution)/shard_map/all_to_all | solution.py:313

commit v6 on v5

--- a/solution.py
+++ b/solution.py
@@ -40,21 +40,21 @@
 
 
 def pack_kernel(place, crops, cotangent, *outs):
-    row = iota((256, LANES), 0)
-    lane = iota((256, LANES), 1)
+    row = iota((224, LANES), 0)
+    lane = iota((224, LANES), 1)
     base = (row & 7) * 96 + (row >> 3 & 1) * 48
     moves = []
     for step in range(4):
         part = (place[0] + step) & 3
-        y = (row >> 4) + (12 * part - 2)
+        y = (row >> 4) + (12 * part - 1)
         source = jnp.where((y >= 0) & (y < 48), base + y, -1)
         tiles = [one_hot(source == lane + k * LANES).astype(BF16) for k in range(6)]
         moves.append(jnp.concatenate(tiles, axis=1))
     both = jnp.concatenate([crops[...].reshape(768, LANES), cotangent[...].reshape(768, LANES)], axis=1)
     for move, out in zip(moves, outs):
-        moved = dot(move, both).astype(BF16).reshape(16, 16, 2 * LANES)
-        out[0:14] = moved[1:15, :, :LANES]
-        out[14:26] = moved[2:14, :, LANES:]
+        moved = dot(move, both).astype(BF16).reshape(14, 16, 2 * LANES)
+        out[0:14] = moved[:, :, :LANES]
+        out[14:26] = moved[1:13, :, LANES:]
 
 
 def moves_kernel(place, plain, summed):

time: 113 us -> 113 us (level)
  no operation moved by 1% of the time
where the time goes in v6:
time: 113 us
  starting transfers between devices  81.9 us (72%)
  waiting for transfers between devices  16 us (14%)
  Pallas kernels  9.34 us (8%)
  local copies, waits for them, and re-layouts  3.71 us (3%)
    ppermute x6, starting transfers between devices, reshard(): lax.ppermute(parts[step], 'chan', [(i, (i + step) % 4) for i in range(4)])  46.6 us
    all_to_all x1, starting transfers between devices, body(): lax.all_to_all(grads.reshape((pieces, -1) + grads.shape[1:]), plane, 0, 0)  11 us
    pallas_call x6, Pallas kernels, run(): pl.pallas_call(kernel, out_shape=outs, in_specs=specs, out_specs=jax.tree...  9.34 us
    ppermute x2, starting transfers between devices, body(): far = lax.ppermute(mine, ('zlo', 'y', 'core'), remote)  8.83 us
    ppermute x6, waiting for transfers between devices, reshard(): lax.ppermute(parts[step], 'chan', [(i, (i + step) % 4) for i in range(4)])  6.31 us
    all_to_all x1, waiting for transfers between devices, body(): lax.all_to_all(grads.reshape((pieces, -1) + grads.shape[1:]), plane, 0, 0)  6.27 us
    all_to_all x1, starting transfers between devices, body(): lax.all_to_all(jnp.broadcast_to(share, (rest,) + share.shape), column, 0, 0)  6.17 us
    all_to_all x1, starting transfers between devices, body(): lax.all_to_all(jnp.broadcast_to(share, (pieces,) + share.shape), plane, 0...  5.43 us
  transfers between devices with their start and end apart: 13, of which 5 were waited for; matrix products, arithmetic and copies ran while one was open for 1% of the time, Pallas kernels for 4%

profile of v6, /device:TPU:1, one launch (start us, length us, event | category | flops | bytes accessed | tf_op | source)
XLA Modules:
  0.0 112.8 jit_solution(1523015859516444647)
XLA Ops:
  0.7 0.9 copy-done.1
  1.6 0.9 copy-done.2
  2.6 1.1 shard_map.59
  3.7 16.3 %collective-permute-start.2 = (bf16[26,16,128]{2,1,0:T(8,128)(2,1)S(1)}, bf16[26,16,128]{2,1,0:T(8,128)(2,1)S(1)}, u32[]{:S(2)}, u32[]{:S(2)}) collective-permute-start(bf16[26,16,128]{2,1,0:T(8,128)(2,1)S(1)} %get-tuple-element.34), channel_id=1, source_target_pairs={{0,8},{4,12},{8,0},{12,4},{1,9},{5,13},{9,1},{13,5},{2,10},{6,14},... | collective-permute-start | bytes 319496 | tf_op jit(solution)/shard_map/ppermute | solution.py:257
  19.9 4.0 %collective-permute-start.3 = (bf16[26,16,128]{2,1,0:T(8,128)(2,1)S(1)}, bf16[26,16,128]{2,1,0:T(8,128)(2,1)S(1)}, u32[]{:S(2)}, u32[]{:S(2)}) collective-permute-start(bf16[26,16,128]{2,1,0:T(8,128)(2,1)S(1)} %get-tuple-element.35), channel_id=1, source_target_pairs={{0,4},{4,8},{8,12},{12,0},{1,5},{5,9},{9,13},{13,1},{2,6},{6,10},{... | collective-permute-start | bytes 319496 | tf_op jit(solution)/shard_map/ppermute | solution.py:257
  24.0 5.2 %collective-permute-start.4 = (bf16[26,16,128]{2,1,0:T(8,128)(2,1)S(1)}, bf16[26,16,128]{2,1,0:T(8,128)(2,1)S(1)}, u32[]{:S(2)}, u32[]{:S(2)}) collective-permute-start(bf16[26,16,128]{2,1,0:T(8,128)(2,1)S(1)} %get-tuple-element.36), channel_id=1, source_target_pairs={{0,12},{4,0},{8,4},{12,8},{1,13},{5,1},{9,5},{13,9},{2,14},{6,2},{... | collective-permute-start | bytes 319496 | tf_op jit(solution)/shard_map/ppermute | solution.py:257
  29.2 4.6 %collective-permute-start.1 = (bf16[26,16,128]{2,1,0:T(8,128)(2,1)S(1)}, bf16[26,16,128]{2,1,0:T(8,128)(2,1)S(1)}, u32[]{:S(2)}, u32[]{:S(2)}) collective-permute-start(bf16[26,16,128]{2,1,0:T(8,128)(2,1)S(1)} %get-tuple-element.37.refs_0_), channel_id=1, source_target_pairs={{16,32},{48,64},{80,96},{112,128},{144,160},{176,192},{208,224},{2... | collective-permute-start | bytes 319496 | tf_op jit(solution)/shard_map/ppermute | solution.py:275
  33.8 1.9 %collective-permute-start = (bf16[26,16,128]{2,1,0:T(8,128)(2,1)S(1)}, bf16[26,16,128]{2,1,0:T(8,128)(2,1)S(1)}, u32[]{:S(2)}, u32[]{:S(2)}) collective-permute-start(bf16[26,16,128]{2,1,0:T(8,128)(2,1)S(1)} %get-tuple-element.37.refs_0_), channel_id=1, source_target_pairs={{0,16},{16,0},{1,17},{17,1},{2,18},{18,2},{3,19},{19,3},{4,20},{20... | collective-permute-start | bytes 319496 | tf_op jit(solution)/shard_map/ppermute | solution.py:274
  35.7 2.6 %collective-permute-done.4 = bf16[26,16,128]{2,1,0:T(8,128)(2,1)S(1)} collective-permute-done((bf16[26,16,128]{2,1,0:T(8,128)(2,1)S(1)}, bf16[26,16,128]{2,1,0:T(8,128)(2,1)S(1)}, u32[]{:S(2)}, u32[]{:S(2)}) %collective-permute-start.4) | collective-permute-done | bytes 106528 | tf_op jit(solution)/shard_map/ppermute | solution.py:257
  38.4 4.2 %collective-permute-start.6 = (bf16[78,16,128]{2,1,0:T(8,128)(2,1)S(1)}, bf16[78,16,128]{2,1,0:T(8,128)(2,1)S(1)}, u32[]{:S(2)}, u32[]{:S(2)}) collective-permute-start(bf16[78,16,128]{2,1,0:T(8,128)(2,1)S(1)} %constant_dynamic-update-slice_fusion.refs_3_), channel_id=1, source_target_pairs={{16,32},{48,64},{80,96},{112,128},{144,160},{176,192},{208,224},{2... | collective-permute-start | bytes 958472 | tf_op jit(solution)/shard_map/ppermute | solution.py:275
  42.6 1.9 %collective-permute-start.5 = (bf16[78,16,128]{2,1,0:T(8,128)(2,1)S(1)}, bf16[78,16,128]{2,1,0:T(8,128)(2,1)S(1)}, u32[]{:S(2)}, u32[]{:S(2)}) collective-permute-start(bf16[78,16,128]{2,1,0:T(8,128)(2,1)S(1)} %constant_dynamic-update-slice_fusion.refs_3_), channel_id=1, source_target_pairs={{0,16},{16,0},{1,17},{17,1},{2,18},{18,2},{3,19},{19,3},{4,20},{20... | collective-permute-start | bytes 958472 | tf_op jit(solution)/shard_map/ppermute | solution.py:274
  44.5 0.2 copy.16
  44.7 0.4 shard_map.60
  45.1 2.1 %collective-permute-done.6.refs_5_ = bf16[78,16,128]{2,1,0:T(8,128)(2,1)S(1)} collective-permute-done((bf16[78,16,128]{2,1,0:T(8,128)(2,1)S(1)}, bf16[78,16,128]{2,1,0:T(8,128)(2,1)S(1)}, u32[]{:S(2)}, u32[]{:S(2)}) %collective-permute-start.6) | collective-permute-done | bytes 319520 | tf_op jit(solution)/shard_map/ppermute | solution.py:275
  47.2 3.9 %shard_map.61 = (bf16[64,1536]{1,0:T(8,128)(2,1)S(1)}, bf16[128,2048]{1,0:T(8,128)(2,1)S(1)}, f32[32,8,128]{2,1,0:T(8,128)}) custom-call(s32[2]{0:T(128)S(1)} %pad_add_fusion.place, bf16[26,16,128]{2,1,0:T(8,128)(2,1)S(1)} %get-tuple-element.37.refs_0_, bf16[26,16,128]{2,1,0:T(8,128)(2,1)S(1)} %collective-permute-done.refs_1_, ...), custom_call_target="tpu_custom_call" | custom-call | flops 3000000000 | tf_op jit(solution)/shard_map/pallas_call | solution.py:241
  51.1 11.0 %all-to-all-start = ((f32[32,1,8,128]{3,2,1,0:T(8,128)}), f32[32,1,8,128]{3,2,1,0:T(8,128)S(1)}, u32[]{:S(2)}, u32[]{:S(2)}) async-start(f32[32,1,8,128]{3,2,1,0:T(8,128)} %bitcast.9), calls=%async_computation | async-start | bytes 262144 | tf_op jit(solution)/shard_map/all_to_all | solution.py:307
  62.2 1.3 %shard_map.62 = (bf16[26,16,128]{2,1,0:T(8,128)(2,1)S(1)}, bf16[26,16,128]{2,1,0:T(8,128)(2,1)S(1)}, bf16[26,16,128]{2,1,0:T(8,128)(2,1)S(1)}, bf16[26,16,128]{2,1,0:T(8,128)(2,1)S(1)}) custom-call(s32[2]{0:T(128)S(1)} %pad_add_fusion.place, bf16[64,1536]{1,0:T(8,128)(2,1)S(1)} %get-tuple-element.45.activated, ...), custom_call_target="tpu_custom_call" | custom-call | flops 2000000000 | tf_op jit(solution)/shard_map/pallas_call | solution.py:241
  63.5 6.3 %all-to-all-done = f32[32,1,8,128]{3,2,1,0:T(8,128)S(1)} async-done(((f32[32,1,8,128]{3,2,1,0:T(8,128)}), f32[32,1,8,128]{3,2,1,0:T(8,128)S(1)}, u32[]{:S(2)}, u32[]{:S(2)}) %all-to-all-start) | async-done | bytes 131104 | tf_op jit(solution)/shard_map/all_to_all | solution.py:307
  69.8 0.6 broadcast_in_dim.14
  70.5 6.2 %all-to-all-start.1 = ((f32[16,1,8,128]{3,2,1,0:T(8,128)}), f32[16,1,8,128]{3,2,1,0:T(8,128)S(1)}, u32[]{:S(2)}, u32[]{:S(2)}) async-start(f32[16,1,8,128]{3,2,1,0:T(8,128)} %broadcast_in_dim.14), calls=%async_computation.1 | async-start | bytes 131072 | tf_op jit(solution)/shard_map/all_to_all | solution.py:310
  76.6 12.0 %collective-permute-start.7 = (bf16[26,16,128]{2,1,0:T(8,128)(2,1)S(1)}, bf16[26,16,128]{2,1,0:T(8,128)(2,1)S(1)}, u32[]{:S(2)}, u32[]{:S(2)}) collective-permute-start(bf16[26,16,128]{2,1,0:T(8,128)(2,1)S(1)} %get-tuple-element.53), channel_id=1, source_target_pairs={{0,8},{4,12},{8,0},{12,4},{1,9},{5,13},{9,1},{13,5},{2,10},{6,14},... | collective-permute-start | bytes 319496 | tf_op jit(solution)/shard_map/ppermute | solution.py:257
  88.6 2.2 %collective-permute-start.8 = (bf16[26,16,128]{2,1,0:T(8,128)(2,1)S(1)}, bf16[26,16,128]{2,1,0:T(8,128)(2,1)S(1)}, u32[]{:S(2)}, u32[]{:S(2)}) collective-permute-start(bf16[26,16,128]{2,1,0:T(8,128)(2,1)S(1)} %get-tuple-element.54), channel_id=1, source_target_pairs={{0,12},{4,0},{8,4},{12,8},{1,13},{5,1},{9,5},{13,9},{2,14},{6,2},{... | collective-permute-start | bytes 319496 | tf_op jit(solution)/shard_map/ppermute | solution.py:257
  90.8 7.0 %collective-permute-start.9 = (bf16[26,16,128]{2,1,0:T(8,128)(2,1)S(1)}, bf16[26,16,128]{2,1,0:T(8,128)(2,1)S(1)}, u32[]{:S(2)}, u32[]{:S(2)}) collective-permute-start(bf16[26,16,128]{2,1,0:T(8,128)(2,1)S(1)} %get-tuple-element.55), channel_id=1, source_target_pairs={{0,4},{4,8},{8,12},{12,0},{1,5},{5,9},{9,13},{13,1},{2,6},{6,10},{... | collective-permute-start | bytes 319496 | tf_op jit(solution)/shard_map/ppermute | solution.py:257
  97.9 0.7 broadcast_in_dim.15
  98.5 5.4 %all-to-all-start.2 = ((f32[32,1,8,128]{3,2,1,0:T(8,128)}), f32[32,1,8,128]{3,2,1,0:T(8,128)S(1)}, u32[]{:S(2)}, u32[]{:S(2)}) async-start(f32[32,1,8,128]{3,2,1,0:T(8,128)} %broadcast_in_dim.15), calls=%async_computation.2 | async-start | bytes 262144 | tf_op jit(solution)/shard_map/all_to_all | solution.py:313
  104.0 1.1 shard_map.58
  105.1 3.7 %collective-permute-done.8.refs_2_ = bf16[26,16,128]{2,1,0:T(8,128)(2,1)S(1)} collective-permute-done((bf16[26,16,128]{2,1,0:T(8,128)(2,1)S(1)}, bf16[26,16,128]{2,1,0:T(8,128)(2,1)S(1)}, u32[]{:S(2)}, u32[]{:S(2)}) %collective-permute-start.8) | collective-permute-done | bytes 106528 | tf_op jit(solution)/shard_map/ppermute | solution.py:257
  108.8 1.5 %shard_map.63 = (bf16[8,2,48,128]{3,2,1,0:T(8,128)(2,1)}, bf16[8,2,48,128]{3,2,1,0:T(8,128)(2,1)}) custom-call(bf16[768,768]{1,0:T(8,128)(2,1)S(1)} %get-tuple-element.31.plain, bf16[768,896]{1,0:T(8,128)(2,1)S(1)} %get-tuple-element.32.summed, bf16[26,16,128]{2,1,0:T(8,128)(2,1)S(1)} %get-tuple-element.52.refs_0_, ...), custom_call_target="tpu_custom_call" | custom-call | flops 1000000000 | tf_op jit(solution)/shard_map/pallas_call | solution.py:241
  110.3 1.3 %all-to-all-done.2 = f32[32,1,8,128]{3,2,1,0:T(8,128)S(1)} async-done(((f32[32,1,8,128]{3,2,1,0:T(8,128)}), f32[32,1,8,128]{3,2,1,0:T(8,128)S(1)}, u32[]{:S(2)}, u32[]{:S(2)}) %all-to-all-start.2) | async-done | bytes 131104 | tf_op jit(solution)/shard_map/all_to_all | solution.py:313
  111.6 0.1 reshape.46
  111.7 0.2 reshape.44
  112.0 0.8 pad_maximum_fusion
  (23 shorter events, 0.3 us)
Async XLA Ops:
  0.7 0.9 copy-start.1
  1.6 0.9 copy-start.2
  2.6 42.0 %copy-start = (bf16[32,27,32]{2,0,1:T(8,128)(2,1)S(1)}, bf16[32,27,32]{2,0,1:T(8,128)(2,1)}, u32[]{:S(2)}) copy-start(bf16[32,27,32]{2,0,1:T(8,128)(2,1)} %param.5) | copy-start | bytes 165892
  3.7 32.0 %collective-permute-start.2 = (bf16[26,16,128]{2,1,0:T(8,128)(2,1)S(1)}, bf16[26,16,128]{2,1,0:T(8,128)(2,1)S(1)}, u32[]{:S(2)}, u32[]{:S(2)}) collective-permute-start(bf16[26,16,128]{2,1,0:T(8,128)(2,1)S(1)} %get-tuple-element.34), channel_id=1, source_target_pairs={{0,8},{4,12},{8,0},{12,4},{1,9},{5,13},{9,1},{13,5},{2,10},{6,14},... | collective-permute-start | bytes 319496 | tf_op jit(solution)/shard_map/ppermute | solution.py:257
  19.9 15.8 %collective-permute-start.3 = (bf16[26,16,128]{2,1,0:T(8,128)(2,1)S(1)}, bf16[26,16,128]{2,1,0:T(8,128)(2,1)S(1)}, u32[]{:S(2)}, u32[]{:S(2)}) collective-permute-start(bf16[26,16,128]{2,1,0:T(8,128)(2,1)S(1)} %get-tuple-element.35), channel_id=1, source_target_pairs={{0,4},{4,8},{8,12},{12,0},{1,5},{5,9},{9,13},{13,1},{2,6},{6,10},{... | collective-permute-start | bytes 319496 | tf_op jit(solution)/shard_map/ppermute | solution.py:257
  24.0 14.3 %collective-permute-start.4 = (bf16[26,16,128]{2,1,0:T(8,128)(2,1)S(1)}, bf16[26,16,128]{2,1,0:T(8,128)(2,1)S(1)}, u32[]{:S(2)}, u32[]{:S(2)}) collective-permute-start(bf16[26,16,128]{2,1,0:T(8,128)(2,1)S(1)} %get-tuple-element.36), channel_id=1, source_target_pairs={{0,12},{4,0},{8,4},{12,8},{1,13},{5,1},{9,5},{13,9},{2,14},{6,2},{... | collective-permute-start | bytes 319496 | tf_op jit(solution)/shard_map/ppermute | solution.py:257
  29.2 9.1 %collective-permute-start.1 = (bf16[26,16,128]{2,1,0:T(8,128)(2,1)S(1)}, bf16[26,16,128]{2,1,0:T(8,128)(2,1)S(1)}, u32[]{:S(2)}, u32[]{:S(2)}) collective-permute-start(bf16[26,16,128]{2,1,0:T(8,128)(2,1)S(1)} %get-tuple-element.37.refs_0_), channel_id=1, source_target_pairs={{16,32},{48,64},{80,96},{112,128},{144,160},{176,192},{208,224},{2... | collective-permute-start | bytes 319496 | tf_op jit(solution)/shard_map/ppermute | solution.py:275
  33.8 4.5 %collective-permute-start = (bf16[26,16,128]{2,1,0:T(8,128)(2,1)S(1)}, bf16[26,16,128]{2,1,0:T(8,128)(2,1)S(1)}, u32[]{:S(2)}, u32[]{:S(2)}) collective-permute-start(bf16[26,16,128]{2,1,0:T(8,128)(2,1)S(1)} %get-tuple-element.37.refs_0_), channel_id=1, source_target_pairs={{0,16},{16,0},{1,17},{17,1},{2,18},{18,2},{3,19},{19,3},{4,20},{20... | collective-permute-start | bytes 319496 | tf_op jit(solution)/shard_map/ppermute | solution.py:274
  38.4 8.9 %collective-permute-start.6 = (bf16[78,16,128]{2,1,0:T(8,128)(2,1)S(1)}, bf16[78,16,128]{2,1,0:T(8,128)(2,1)S(1)}, u32[]{:S(2)}, u32[]{:S(2)}) collective-permute-start(bf16[78,16,128]{2,1,0:T(8,128)(2,1)S(1)} %constant_dynamic-update-slice_fusion.refs_3_), channel_id=1, source_target_pairs={{16,32},{48,64},{80,96},{112,128},{144,160},{176,192},{208,224},{2... | collective-permute-start | bytes 958472 | tf_op jit(solution)/shard_map/ppermute | solution.py:275
  42.6 4.7 %collective-permute-start.5 = (bf16[78,16,128]{2,1,0:T(8,128)(2,1)S(1)}, bf16[78,16,128]{2,1,0:T(8,128)(2,1)S(1)}, u32[]{:S(2)}, u32[]{:S(2)}) collective-permute-start(bf16[78,16,128]{2,1,0:T(8,128)(2,1)S(1)} %constant_dynamic-update-slice_fusion.refs_3_), channel_id=1, source_target_pairs={{0,16},{16,0},{1,17},{17,1},{2,18},{18,2},{3,19},{19,3},{4,20},{20... | collective-permute-start | bytes 958472 | tf_op jit(solution)/shard_map/ppermute | solution.py:274
  51.1 18.7 %all-to-all-start = ((f32[32,1,8,128]{3,2,1,0:T(8,128)}), f32[32,1,8,128]{3,2,1,0:T(8,128)S(1)}, u32[]{:S(2)}, u32[]{:S(2)}) async-start(f32[32,1,8,128]{3,2,1,0:T(8,128)} %bitcast.9), calls=%async_computation | async-start | bytes 262144 | tf_op jit(solution)/shard_map/all_to_all | solution.py:307
  70.5 27.4 %all-to-all-start.1 = ((f32[16,1,8,128]{3,2,1,0:T(8,128)}), f32[16,1,8,128]{3,2,1,0:T(8,128)S(1)}, u32[]{:S(2)}, u32[]{:S(2)}) async-start(f32[16,1,8,128]{3,2,1,0:T(8,128)} %broadcast_in_dim.14), calls=%async_computation.1 | async-start | bytes 131072 | tf_op jit(solution)/shard_map/all_to_all | solution.py:310
  76.6 28.4 %collective-permute-start.7 = (bf16[26,16,128]{2,1,0:T(8,128)(2,1)S(1)}, bf16[26,16,128]{2,1,0:T(8,128)(2,1)S(1)}, u32[]{:S(2)}, u32[]{:S(2)}) collective-permute-start(bf16[26,16,128]{2,1,0:T(8,128)(2,1)S(1)} %get-tuple-element.53), channel_id=1, source_target_pairs={{0,8},{4,12},{8,0},{12,4},{1,9},{5,13},{9,1},{13,5},{2,10},{6,14},... | collective-permute-start | bytes 319496 | tf_op jit(solution)/shard_map/ppermute | solution.py:257
  88.6 20.2 %collective-permute-start.8 = (bf16[26,16,128]{2,1,0:T(8,128)(2,1)S(1)}, bf16[26,16,128]{2,1,0:T(8,128)(2,1)S(1)}, u32[]{:S(2)}, u32[]{:S(2)}) collective-permute-start(bf16[26,16,128]{2,1,0:T(8,128)(2,1)S(1)} %get-tuple-element.54), channel_id=1, source_target_pairs={{0,12},{4,0},{8,4},{12,8},{1,13},{5,1},{9,5},{13,9},{2,14},{6,2},{... | collective-permute-start | bytes 319496 | tf_op jit(solution)/shard_map/ppermute | solution.py:257
  90.8 18.0 %collective-permute-start.9 = (bf16[26,16,128]{2,1,0:T(8,128)(2,1)S(1)}, bf16[26,16,128]{2,1,0:T(8,128)(2,1)S(1)}, u32[]{:S(2)}, u32[]{:S(2)}) collective-permute-start(bf16[26,16,128]{2,1,0:T(8,128)(2,1)S(1)} %get-tuple-element.55), channel_id=1, source_target_pairs={{0,4},{4,8},{8,12},{12,0},{1,5},{5,9},{9,13},{13,1},{2,6},{6,10},{... | collective-permute-start | bytes 319496 | tf_op jit(solution)/shard_map/ppermute | solution.py:257
  98.5 13.1 %all-to-all-start.2 = ((f32[32,1,8,128]{3,2,1,0:T(8,128)}), f32[32,1,8,128]{3,2,1,0:T(8,128)S(1)}, u32[]{:S(2)}, u32[]{:S(2)}) async-start(f32[32,1,8,128]{3,2,1,0:T(8,128)} %broadcast_in_dim.15), calls=%async_computation.2 | async-start | bytes 262144 | tf_op jit(solution)/shard_map/all_to_all | solution.py:313
